TPU v7x, 256 devices: a whole 4x4x8 slice. The times are simulated.
256 devices in a mesh: ctx: 16 (over y, x_hi, core), head: 16 (over x_lo, z).
Axes of the slice: x: 4 (x_hi: 2, x_lo: 2; x = x_hi * 2 + x_lo), y: 4, z: 8, core: 2. Of those that a mesh axis runs over, the one named last changes fastest.
Arguments:
- tokens: bfloat16 [16384, 2048], P('ctx', 'head'), may hold values from -6 to 6
- w_query: bfloat16 [2048, 2048], P(None, 'head'), may hold values from -0.125 to 0.125
- w_value: bfloat16 [2048, 2048], P(None, 'head'), may hold values from -0.125 to 0.125
- w_out: bfloat16 [2048, 2048], P('head'), may hold values from -1.5 to 1.5
- doc_lengths: int32 [2], replicated, may hold values from 1024 to 8192, as said below
Outputs:
- layer_out: bfloat16 [16384, 2048], P('ctx', 'head')
Inputs may be any that keep to these rules, and one draw needn't show every extreme that they name: `doc_lengths`: one of the two documents, drawn from the seed, has the full length 8192; the other has at least 1024 valid tokens.
All inputs are finite; a program needn't handle non-finite values.
Results may differ from a plain program's by a relative error of at most 0.02.
Values may be sent and summed in bfloat16 or wider, within the bound.
No kernel may reach another device: no remote copies, remote signals or barrier semaphores. Data moves between devices by JAX's collectives and lax.ppermute only.
A program may use at most 64 MiB of HBM per device.

v0:
```python
import math

import jax
import jax.numpy as jnp
from jax import lax
from jax.sharding import Mesh
from jax.sharding import PartitionSpec as P

HD = 128
HEAD = ("head_0", "head_1")


score_bound = 24.0


def in_order(pieces, dim):
    dims = list(pieces.shape[1:])
    dims[dim] *= pieces.shape[0]
    return jnp.moveaxis(pieces, 0, dim).reshape(dims)


def gather_in_order(value, axes, turns):
    pieces = value
    for k in turns:
        pieces = lax.all_gather(pieces, axes[k])
    done = turns[::-1]
    back = [done.index(k) for k in range(len(axes))]
    pieces = pieces.transpose(*back, *range(len(axes), pieces.ndim))
    return pieces.reshape(-1, *value.shape)


def gathered_by_axis(value, axes, turns, dim):
    return in_order(gather_in_order(value, axes, turns), dim)


def from_partner(value, axis, stride):
    mask = 2**stride
    pairs = [(source, source ^ mask) for source in range(lax.axis_size(axis))]
    return lax.ppermute(value, axis, pairs)


def reduced_to_own(pieces, axes, turns):
    inside = pieces.shape[1:]
    pieces = pieces.reshape(*(lax.axis_size(a) for a in axes), *inside)
    pieces = jnp.moveaxis(pieces, turns, range(len(axes))).reshape(-1, *inside)
    for k in turns:
        pieces = lax.psum_scatter(pieces, axes[k], scatter_dimension=0, tiled=True)
    return pieces[0]


def split_up(value, dim, devices):
    dims = value.shape
    pieces = value.reshape(*dims[:dim], devices, dims[dim] // devices, *dims[dim + 1 :])
    return jnp.moveaxis(pieces, dim, 0)


def sum_by_axis(value, axes, turns, dim):
    devices = lax.axis_size(axes)
    return reduced_to_own(split_up(value, dim, devices), axes, turns)


def unit_heads(projected, heads_here, head_size):
    shaped = projected.reshape(projected.shape[0], heads_here, head_size)
    scaled = shaped * lax.rsqrt(jnp.sum(shaped * shaped, axis=-1, keepdims=True) + 1e-06)
    return scaled.astype(jnp.bfloat16)


def per_device(tokens, w_query, w_value, w_out, doc_lengths):
    block_rows = tokens.shape[0]
    width_here = w_query.shape[1]
    heads_here = width_here // HD
    joined = jnp.concatenate([w_query, w_value], axis=1)
    projected = jnp.dot(
        gathered_by_axis(tokens, HEAD, (0, 1), 1), joined, preferred_element_type=jnp.float32
    )
    queries = unit_heads(projected[:, :width_here], heads_here, HD)
    own_values = projected[:, width_here:].astype(jnp.bfloat16).reshape(block_rows, heads_here, HD)
    ctx_count = lax.axis_size("ctx")
    ctx_here = lax.axis_index("ctx")
    doc_span = block_rows * ctx_count // 2
    own_first = ctx_here * block_rows

    def placement(start, length):
        position = start + jnp.arange(length, dtype=jnp.int32)
        doc_index = position // doc_span
        limit = jnp.where(doc_index == 0, doc_lengths[0], doc_lengths[1])
        return (position, doc_index, position - doc_index * doc_span < limit)

    own_position, own_doc, own_valid = placement(own_first, block_rows)

    def tile_weights(key_rows, key_start):
        key_position, key_doc, key_valid = placement(key_start, key_rows.shape[0])
        allowed = own_valid[:, None] & key_valid[None, :] & (own_doc[:, None] == key_doc[None, :])
        allowed = allowed & (own_position[:, None] != key_position[None, :])
        scores = (
            jnp.einsum("qhd,khd->hqk", queries, key_rows, preferred_element_type=jnp.float32)
            * score_bound
        )
        return jnp.exp(scores - score_bound) * allowed.astype(jnp.float32)[None]

    def own_update(key_rows, key_values, key_start, totals):
        weights_tile = tile_weights(key_rows, key_start)
        rounded = weights_tile.astype(jnp.bfloat16)
        numer = totals[0] + jnp.einsum(
            "hqk,khd->qhd", rounded, key_values, preferred_element_type=jnp.float32
        )
        return (numer, totals[1] + jnp.sum(weights_tile, axis=2))

    start_numer = jnp.zeros((block_rows, heads_here, HD), jnp.float32)
    start_denom = jnp.zeros((heads_here, block_rows), jnp.float32)
    group_size = ctx_count // 2
    group_bits = group_size.bit_length() - 1
    held_keys, held_values = (queries, own_values)
    for bit in range(group_bits):
        stride = 1 << bit
        other_keys, other_values = from_partner((held_keys, held_values), "ctx", bit)
        upper = ctx_here // stride % 2 == 1
        held_keys = jnp.where(
            upper,
            jnp.concatenate([other_keys, held_keys], 0),
            jnp.concatenate([held_keys, other_keys], 0),
        )
        held_values = jnp.where(
            upper,
            jnp.concatenate([other_values, held_values], 0),
            jnp.concatenate([held_values, other_values], 0),
        )
    doc_first = ctx_here // group_size * group_size * block_rows
    piece_keys = held_keys
    piece_values = held_values
    piece_rows = piece_keys.shape[0]
    step_rows = math.gcd(piece_rows, block_rows)

    def one_step(step_index, inner):
        offset = step_index * step_rows
        key_start = doc_first + offset
        step_keys = lax.dynamic_slice_in_dim(piece_keys, offset, step_rows, 0)
        step_values = lax.dynamic_slice_in_dim(piece_values, offset, step_rows, 0)
        return own_update(step_keys, step_values, key_start, inner)

    numer, denom = lax.fori_loop(0, piece_rows // step_rows, one_step, (start_numer, start_denom))
    invalid = 1.0 - own_valid.astype(jnp.float32)
    attended = numer / (denom.T[:, :, None] + invalid[:, None, None])
    attended = attended.astype(jnp.bfloat16).reshape(block_rows, width_here)
    partial_out = jnp.dot(attended, w_out, preferred_element_type=jnp.float32)
    return (
        sum_by_axis(partial_out.astype(jnp.bfloat16), HEAD, (1, 0), 1)
        .astype(jnp.float32)
        .astype(jnp.bfloat16)
    )


def solution(mesh):
    finer = Mesh(mesh.devices.reshape(mesh.shape["ctx"], 2, 8), ("ctx", "head_0", "head_1"))
    return jax.shard_map(
        per_device,
        mesh=finer,
        in_specs=(P("ctx", HEAD), P(None, HEAD), P(None, HEAD), P(HEAD, None), P()),
        out_specs=P("ctx", HEAD),
        check_vma=False,
    )
```

profile of v0, /device:TPU:16, one launch (start us, length us, event | category | flops | bytes accessed | tf_op | source)
XLA Modules:
  0.0 308.2 jit_solution(3202143669060859376)
XLA Ops:
  6.5 10.6 %all-gather = bf16[2048,128]{1,0:T(8,128)(2,1)} all-gather(bf16[1024,128]{1,0:T(8,128)(2,1)} %param.7), channel_id=2, replica_groups=mesh['ctx'=16,'head_0'=2,'head_1'=8] {'head_0'}, dimensions={0}, use_global_device_ids=true | all-gather | bytes 786432 | tf_op jit(solution)/shard_map/all_gather | solution.py:25
  18.6 56.0 %all-gather.4.cloned.1.call-done = bf16[16,1024,128]{2,1,0:T(8,128)(2,1)} async-done(((bf16[2,1024,128]{2,1,0:T(8,128)(2,1)}), bf16[16,1024,128]{2,1,0:T(8,128)(2,1)}) %all-gather.4.cloned.1.call-update) | async-done | bytes 4194320 | tf_op jit(solution)/shard_map/all_gather | solution.py:25
  74.6 4.6 %copy.21 = bf16[2,8,1024,128]{3,2,1,0:T(8,128)(2,1)} copy(bf16[2,8,1024,128]{3,2,0,1:T(8,128)(2,1)} %bitcast.91) | data formatting | bytes 8388608 | tf_op jit(solution)/shard_map/transpose | solution.py:28
  79.2 6.5 %copy.22 = bf16[1024,16,128]{0,2,1:T(8,128)(2,1)} copy(bf16[1024,16,128]{2,0,1:T(8,128)(2,1)} %bitcast.87) | data formatting | bytes 8388608 | tf_op jit(solution)/shard_map/transpose | solution.py:19
  85.6 3.5 %convolution_bitcast_fusion = f32[1024,256]{0,1:T(8,128)S(1)} fusion(bf16[1024,2048]{0,1:T(8,128)(2,1)} %bitcast.92, bf16[2048,128]{1,0:T(8,128)(2,1)S(1)} %copy-done.2, bf16[2048,128]{1,0:T(8,128)(2,1)S(1)} %copy-done.3), kind=kOutput, calls=%fused_computation.40 | convolution fusion | flops 1075838976 | bytes 6291456 | tf_op jit(solution)/shard_map/dot_general | solution.py:73
  91.0 3.1 collective-permute-start.4
  95.1 12.2 %collective-permute-done.4 = bf16[2048,1,128]{0,2,1:T(8,128)(2,1)S(1)} collective-permute-done((bf16[2048,1,128]{0,2,1:T(8,128)(2,1)S(1)}, bf16[2048,1,128]{0,2,1:T(8,128)(2,1)S(1)}, u32[]{:S(2)}, u32[]{:S(2)}) %collective-permute-start.4) | collective-permute-done | bytes 524320 | tf_op jit(solution)/shard_map/ppermute | solution.py:39
  108.9 8.9 %collective-permute-done.1 = bf16[2048,1,128]{0,2,1:T(8,128)(2,1)S(1)} collective-permute-done((bf16[2048,1,128]{0,2,1:T(8,128)(2,1)S(1)}, bf16[2048,1,128]{0,2,1:T(8,128)(2,1)S(1)}, u32[]{:S(2)}, u32[]{:S(2)}) %collective-permute-start.1) | collective-permute-done | bytes 524320 | tf_op jit(solution)/shard_map/ppermute | solution.py:39
  120.2 13.6 %collective-permute-done.5 = bf16[4096,1,128]{0,2,1:T(8,128)(2,1)S(1)} collective-permute-done((bf16[4096,1,128]{0,2,1:T(8,128)(2,1)S(1)}, bf16[4096,1,128]{0,2,1:T(8,128)(2,1)S(1)}, u32[]{:S(2)}, u32[]{:S(2)}) %collective-permute-start.5) | collective-permute-done | bytes 1048608 | tf_op jit(solution)/shard_map/ppermute | solution.py:39
  135.7 18.0 %collective-permute-done.2 = bf16[4096,1,128]{0,2,1:T(8,128)(2,1)S(1)} collective-permute-done((bf16[4096,1,128]{0,2,1:T(8,128)(2,1)S(1)}, bf16[4096,1,128]{0,2,1:T(8,128)(2,1)S(1)}, u32[]{:S(2)}, u32[]{:S(2)}) %collective-permute-start.2) | collective-permute-done | bytes 1048608 | tf_op jit(solution)/shard_map/ppermute | solution.py:39
  155.7 64.1 %while.20 = (s32[]{:T(128)}, f32[1024,1,128]{0,2,1:T(8,128)S(1)}, f32[1,1024]{1,0:T(1,128)S(1)}, bf16[8192,1,128]{0,2,1:T(8,128)(2,1)}, s32[]{:T(128)}, /*index=...) while((s32[]{:T(128)}, f32[1024,1,128]{0,2,1:T(8,128)S(1)}, ...), condition=%wide.region_3.4_spmd.clone.clone.clone, body=%wide.region_1.3_spmd.clone.clone.clone.sunk | while | flops 547695616 | bytes 6082826 | solution.py:141
  158.6 3.5 %fusion.54 = (f32[1024]{0:T(1024)S(1)}, bf16[1024,1024]{0,1:T(8,128)(2,1)S(1)}) fusion(bf16[1024,1,128]{2,0,1:T(8,128)(2,1)S(1)} %get-tuple-element.586, bf16[8192,1,128]{0,2,1:T(8,128)(2,1)} %get-tuple-element.585, s32[]{:T(128)S(6)} %select_n.333, s32[1024]{0:T(1024)S(1)} %get-tuple-element.539, s32[1024]{0:T(1024)S(1)} %get-tuple-element.540, ...), kind=kOutput, calls=%fused_computation.73.clone.1 | convolution fusion | flops 278920192 | bytes 2643972 | tf_op jit(solution)/shard_map/while/body/eval_jaxpr/qhd,khd->hqk/dot_general | solution.py:96
  164.3 2.3 select_compare_fusion.4
  166.7 3.5 %fusion.54 = (f32[1024]{0:T(1024)S(1)}, bf16[1024,1024]{0,1:T(8,128)(2,1)S(1)}) fusion(bf16[1024,1,128]{2,0,1:T(8,128)(2,1)S(1)} %get-tuple-element.586, bf16[8192,1,128]{0,2,1:T(8,128)(2,1)} %get-tuple-element.585, s32[]{:T(128)S(6)} %select_n.333, s32[1024]{0:T(1024)S(1)} %get-tuple-element.539, s32[1024]{0:T(1024)S(1)} %get-tuple-element.540, ...), kind=kOutput, calls=%fused_computation.73.clone.1 | convolution fusion | flops 278920192 | bytes 2643972 | tf_op jit(solution)/shard_map/while/body/eval_jaxpr/qhd,khd->hqk/dot_general | solution.py:96
  174.7 3.5 %fusion.54 = (f32[1024]{0:T(1024)S(1)}, bf16[1024,1024]{0,1:T(8,128)(2,1)S(1)}) fusion(bf16[1024,1,128]{2,0,1:T(8,128)(2,1)S(1)} %get-tuple-element.586, bf16[8192,1,128]{0,2,1:T(8,128)(2,1)} %get-tuple-element.585, s32[]{:T(128)S(6)} %select_n.333, s32[1024]{0:T(1024)S(1)} %get-tuple-element.539, s32[1024]{0:T(1024)S(1)} %get-tuple-element.540, ...), kind=kOutput, calls=%fused_computation.73.clone.1 | convolution fusion | flops 278920192 | bytes 2643972 | tf_op jit(solution)/shard_map/while/body/eval_jaxpr/qhd,khd->hqk/dot_general | solution.py:96
  182.7 3.5 %fusion.54 = (f32[1024]{0:T(1024)S(1)}, bf16[1024,1024]{0,1:T(8,128)(2,1)S(1)}) fusion(bf16[1024,1,128]{2,0,1:T(8,128)(2,1)S(1)} %get-tuple-element.586, bf16[8192,1,128]{0,2,1:T(8,128)(2,1)} %get-tuple-element.585, s32[]{:T(128)S(6)} %select_n.333, s32[1024]{0:T(1024)S(1)} %get-tuple-element.539, s32[1024]{0:T(1024)S(1)} %get-tuple-element.540, ...), kind=kOutput, calls=%fused_computation.73.clone.1 | convolution fusion | flops 278920192 | bytes 2643972 | tf_op jit(solution)/shard_map/while/body/eval_jaxpr/qhd,khd->hqk/dot_general | solution.py:96
  190.7 3.5 %fusion.54 = (f32[1024]{0:T(1024)S(1)}, bf16[1024,1024]{0,1:T(8,128)(2,1)S(1)}) fusion(bf16[1024,1,128]{2,0,1:T(8,128)(2,1)S(1)} %get-tuple-element.586, bf16[8192,1,128]{0,2,1:T(8,128)(2,1)} %get-tuple-element.585, s32[]{:T(128)S(6)} %select_n.333, s32[1024]{0:T(1024)S(1)} %get-tuple-element.539, s32[1024]{0:T(1024)S(1)} %get-tuple-element.540, ...), kind=kOutput, calls=%fused_computation.73.clone.1 | convolution fusion | flops 278920192 | bytes 2643972 | tf_op jit(solution)/shard_map/while/body/eval_jaxpr/qhd,khd->hqk/dot_general | solution.py:96
  198.7 3.5 %fusion.54 = (f32[1024]{0:T(1024)S(1)}, bf16[1024,1024]{0,1:T(8,128)(2,1)S(1)}) fusion(bf16[1024,1,128]{2,0,1:T(8,128)(2,1)S(1)} %get-tuple-element.586, bf16[8192,1,128]{0,2,1:T(8,128)(2,1)} %get-tuple-element.585, s32[]{:T(128)S(6)} %select_n.333, s32[1024]{0:T(1024)S(1)} %get-tuple-element.539, s32[1024]{0:T(1024)S(1)} %get-tuple-element.540, ...), kind=kOutput, calls=%fused_computation.73.clone.1 | convolution fusion | flops 278920192 | bytes 2643972 | tf_op jit(solution)/shard_map/while/body/eval_jaxpr/qhd,khd->hqk/dot_general | solution.py:96
  206.7 3.5 %fusion.54 = (f32[1024]{0:T(1024)S(1)}, bf16[1024,1024]{0,1:T(8,128)(2,1)S(1)}) fusion(bf16[1024,1,128]{2,0,1:T(8,128)(2,1)S(1)} %get-tuple-element.586, bf16[8192,1,128]{0,2,1:T(8,128)(2,1)} %get-tuple-element.585, s32[]{:T(128)S(6)} %select_n.333, s32[1024]{0:T(1024)S(1)} %get-tuple-element.539, s32[1024]{0:T(1024)S(1)} %get-tuple-element.540, ...), kind=kOutput, calls=%fused_computation.73.clone.1 | convolution fusion | flops 278920192 | bytes 2643972 | tf_op jit(solution)/shard_map/while/body/eval_jaxpr/qhd,khd->hqk/dot_general | solution.py:96
  212.4 2.3 select_compare_fusion.4
  214.8 3.5 %fusion.54 = (f32[1024]{0:T(1024)S(1)}, bf16[1024,1024]{0,1:T(8,128)(2,1)S(1)}) fusion(bf16[1024,1,128]{2,0,1:T(8,128)(2,1)S(1)} %get-tuple-element.586, bf16[8192,1,128]{0,2,1:T(8,128)(2,1)} %get-tuple-element.585, s32[]{:T(128)S(6)} %select_n.333, s32[1024]{0:T(1024)S(1)} %get-tuple-element.539, s32[1024]{0:T(1024)S(1)} %get-tuple-element.540, ...), kind=kOutput, calls=%fused_computation.73.clone.1 | convolution fusion | flops 278920192 | bytes 2643972 | tf_op jit(solution)/shard_map/while/body/eval_jaxpr/qhd,khd->hqk/dot_general | solution.py:96
  223.7 3.0 copy.26
  226.8 54.0 %reduce-scatter.3.cloned.1.call-done = bf16[2,1024,128]{2,1,0:T(8,128)(2,1)} async-done(((bf16[16,1024,128]{2,1,0:T(8,128)(2,1)}), bf16[2,1024,128]{2,1,0:T(8,128)(2,1)}) %reduce-scatter.3.cloned.1.call-update) | async-done | bytes 524304 | tf_op jit(solution)/shard_map/reduce_scatter | solution.py:47
  280.9 20.8 %reduce-scatter.5.cloned.1.call-done = bf16[1,1024,128]{2,1,0:T(8,128)(2,1)} async-done(((bf16[2,1024,128]{2,1,0:T(8,128)(2,1)}), bf16[1,1024,128]{2,1,0:T(8,128)(2,1)}) %reduce-scatter.5.cloned.1.call-update) | async-done | bytes 262160 | tf_op jit(solution)/shard_map/reduce_scatter | solution.py:47
  (90 shorter events, 46.7 us)
Async XLA Ops:
  6.5 214.5 %copy-start = (bf16[128,2048]{1,0:T(8,128)(2,1)S(1)}, bf16[128,2048]{1,0:T(8,128)(2,1)}, u32[]{:S(2)}) copy-start(bf16[128,2048]{1,0:T(8,128)(2,1)} %param.10) | copy-start | bytes 1572868
  6.5 68.1 %all-gather.4.cloned.1.call-start = ((), (), s32[]{:S(2)}) async-start(), calls=%async_computation.4 | async-start | bytes 4718592 | tf_op jit(solution)/shard_map/all_gather | solution.py:25
  17.1 263.7 %reduce-scatter.3.cloned.1.call-start = ((), (), s32[]{:S(2)}) async-start(), calls=%async_computation.2 | async-start | bytes 4718592 | tf_op jit(solution)/shard_map/reduce_scatter | solution.py:47
  79.2 6.5 %copy-start.2 = (bf16[2048,128]{1,0:T(8,128)(2,1)S(1)}, bf16[2048,128]{1,0:T(8,128)(2,1)}, u32[]{:S(2)}) copy-start(bf16[2048,128]{1,0:T(8,128)(2,1)} %param.9) | copy-start | bytes 1572868
  79.2 6.5 %copy-start.3 = (bf16[2048,128]{1,0:T(8,128)(2,1)S(1)}, bf16[2048,128]{1,0:T(8,128)(2,1)}, u32[]{:S(2)}) copy-start(bf16[2048,128]{1,0:T(8,128)(2,1)} %param.8) | copy-start | bytes 1572868
  89.2 1.6 collective-permute-start.3
  89.4 4.7 %collective-permute-start = (bf16[1024,1,128]{0,2,1:T(8,128)(2,1)S(1)}, bf16[1024,1,128]{0,2,1:T(8,128)(2,1)S(1)}, u32[]{:S(2)}, u32[]{:S(2)}) collective-permute-start(bf16[1024,1,128]{0,2,1:T(8,128)(2,1)S(1)} %slice_bitcast_fusion), channel_id=1, source_target_pairs={{0,16},{16,0},{32,48},{48,32},{64,80},{80,64},{96,112},{112,96},{1... | collective-permute-start | bytes 786440 | tf_op jit(solution)/shard_map/ppermute | solution.py:39
  91.0 16.4 %collective-permute-start.4 = (bf16[2048,1,128]{0,2,1:T(8,128)(2,1)S(1)}, bf16[2048,1,128]{0,2,1:T(8,128)(2,1)S(1)}, u32[]{:S(2)}, u32[]{:S(2)}) collective-permute-start(bf16[2048,1,128]{0,2,1:T(8,128)(2,1)S(1)} %maximum_select_fusion.8), channel_id=1, source_target_pairs={{0,32},{16,48},{32,0},{48,16},{64,96},{80,112},{96,64},{112,80},{1... | collective-permute-start | bytes 1572872 | tf_op jit(solution)/shard_map/ppermute | solution.py:39
  94.2 23.6 %collective-permute-start.1 = (bf16[2048,1,128]{0,2,1:T(8,128)(2,1)S(1)}, bf16[2048,1,128]{0,2,1:T(8,128)(2,1)S(1)}, u32[]{:S(2)}, u32[]{:S(2)}) collective-permute-start(bf16[2048,1,128]{0,2,1:T(8,128)(2,1)S(1)} %maximum_select_fusion.6), channel_id=1, source_target_pairs={{0,32},{16,48},{32,0},{48,16},{64,96},{80,112},{96,64},{112,80},{1... | collective-permute-start | bytes 1572872 | tf_op jit(solution)/shard_map/ppermute | solution.py:39
  107.6 26.2 %collective-permute-start.5 = (bf16[4096,1,128]{0,2,1:T(8,128)(2,1)S(1)}, bf16[4096,1,128]{0,2,1:T(8,128)(2,1)S(1)}, u32[]{:S(2)}, u32[]{:S(2)}) collective-permute-start(bf16[4096,1,128]{0,2,1:T(8,128)(2,1)S(1)} %maximum_select_fusion.4), channel_id=1, source_target_pairs={{0,64},{16,80},{32,96},{48,112},{64,0},{80,16},{96,32},{112,48},{1... | collective-permute-start | bytes 3145736 | tf_op jit(solution)/shard_map/ppermute | solution.py:39
  118.1 35.6 %collective-permute-start.2 = (bf16[4096,1,128]{0,2,1:T(8,128)(2,1)S(1)}, bf16[4096,1,128]{0,2,1:T(8,128)(2,1)S(1)}, u32[]{:S(2)}, u32[]{:S(2)}) collective-permute-start(bf16[4096,1,128]{0,2,1:T(8,128)(2,1)S(1)} %maximum_select_fusion.2), channel_id=1, source_target_pairs={{0,64},{16,80},{32,96},{48,112},{64,0},{80,16},{96,32},{112,48},{1... | collective-permute-start | bytes 3145736 | tf_op jit(solution)/shard_map/ppermute | solution.py:39
  135.7 20.0 %copy-start.1 = (s32[2]{0:T(128)S(1)}, s32[2]{0:T(128)}, u32[]{:S(2)}) copy-start(s32[2]{0:T(128)} %param.11) | copy-start | bytes 28
  226.8 74.8 %reduce-scatter.5.cloned.1.call-start = ((), (), s32[]{:S(2)}) async-start(), calls=%async_computation.3 | async-start | bytes 786432 | tf_op jit(solution)/shard_map/reduce_scatter | solution.py:47
Sparse Core Ops, SparseCore 0:
  17.2 57.3 all-gather.3
  226.9 53.8 reduce-scatter.2
  283.4 18.2 reduce-scatter.4
where the time goes:
time: 310 us; the launch traced here: 308 us
  waiting for transfers between devices  184 us (59%)
  matrix products  44.8 us (14%)
  other arithmetic  25.8 us (8%)
  local copies, waits for them, and re-layouts  21.7 us (7%)
  between operations  13.4 us (4%)
  blocking collectives  10.6 us (3%)
  starting transfers between devices  7.21 us (2%)
    reduce_scatter x2, waiting for transfers between devices, reduced_to_own(): pieces = lax.psum_scatter(pieces, axes[k], scatter_dimension=0, tiled=True)  74.8 us
    all_gather x1, waiting for transfers between devices, gather_in_order(): pieces = lax.all_gather(pieces, axes[k])  56 us
    ppermute x6, waiting for transfers between devices, from_partner(): return lax.ppermute(value, axis, pairs)  53.4 us
    dot_general x8, matrix products, tile_weights(): jnp.einsum('qhd,khd->hqk', queries, key_rows, preferred_element_type=jnp....  28.3 us
    lt x8, other arithmetic, placement(): return (position, doc_index, position - doc_index * doc_span < limit)  18.5 us
    dot_general x8, matrix products, own_update(): jnp.einsum('hqk,khd->qhd', rounded, key_values, preferred_element_type=jn...  11.8 us
    all_gather x1, blocking collectives, gather_in_order(): pieces = lax.all_gather(pieces, axes[k])  10.6 us
    ppermute x6, starting transfers between devices, from_partner(): return lax.ppermute(value, axis, pairs)  7.12 us
  transfers between devices with their start and end apart: 9, of which 8 were waited for; matrix products, arithmetic and copies ran while one was open for 2% of the time, Pallas kernels for 0%

commit v1 on v0

v1 whole, which is shorter than its diff:
```python
import itertools
import math

import jax
import jax.numpy as jnp
from jax import lax
from jax.experimental import pallas as pl
from jax.experimental.pallas import tpu as pltpu
from jax.sharding import Mesh
from jax.sharding import PartitionSpec as P

HD = 128
HEAD = ("xl", "z")
CTX = ("yh", "yl", "xh", "core")
AXES = CTX + HEAD
SCORE_BOUND = 24.0
SCALE = SCORE_BOUND * math.log2(math.e)
VMEM = pl.BlockSpec(memory_space=pltpu.VMEM)
SMEM = pl.BlockSpec(memory_space=pltpu.SMEM)
F32 = jnp.float32
BF16 = jnp.bfloat16


def hop(value, axes, target):
    places = list(itertools.product(*(range(lax.axis_size(a)) for a in axes)))
    number = {place: i for i, place in enumerate(places)}
    return lax.ppermute(value, axes, [(number[c], number[tuple(target(*c))]) for c in places])


def swap(value, *axes):
    return hop(value, axes, lambda *c: tuple(1 - i for i in c))


def z_step(value):
    depth = lax.axis_size("z")
    return hop(value, ("core", "z"), lambda c, z: (c, (z + 1 - 2 * c) % depth))


def params(mib):
    return pltpu.CompilerParams(vmem_limit_bytes=mib * 2**20)


def call(kernel, outs, smem_count, args, name, flops, limit=24):
    moved = sum(math.prod(a.shape) * a.dtype.itemsize for a in [*args, *outs])
    return pl.pallas_call(
        kernel,
        out_shape=outs,
        in_specs=[SMEM] * smem_count + [VMEM] * (len(args) - smem_count),
        out_specs=[VMEM] * len(outs),
        compiler_params=params(limit),
        cost_estimate=pl.CostEstimate(flops=flops, bytes_accessed=moved, transcendentals=0),
        name=name,
    )(*args)


def contract(rows_at, weights, jobs, name, finish=None, extras=(), outs=None, smem=()):
    width = sum(w.shape[1] for w in weights)
    flat, plan = [], []
    for total, *terms in jobs:
        plan.append((total is not None, [t[0] for t in terms]))
        flat += ([total] if total is not None else []) + [b for t in terms for b in t[1:]]
    rows = jobs[0][1][1].shape[0]
    tile = 256
    if outs is None:
        outs = [jax.ShapeDtypeStruct((rows, width), F32)] * len(jobs)
    n_s, n_w, n_e, n_f = 1 + len(smem), len(weights), len(extras), len(flat)

    def kernel(*refs):
        at = refs[0]
        w_refs = refs[n_s : n_s + n_w]
        e_refs = refs[n_s + n_w : n_s + n_w + n_e]
        b_refs = list(refs[n_s + n_w + n_e : n_s + n_w + n_e + n_f])
        o_refs = refs[n_s + n_w + n_e + n_f :]
        taken = {}

        def weight(step):
            if step not in taken:
                halves = []
                for i in (0, 1):
                    first = pl.multiple_of(at[2 * step + i], HD)
                    halves.append(
                        jnp.concatenate([w[pl.ds(first, HD), :] for w in w_refs], axis=1)
                    )
                taken[step] = jnp.concatenate(halves, axis=0)
            return taken[step]

        for index, (has_total, steps) in enumerate(plan):
            total_ref = b_refs.pop(0) if has_total else None
            pairs = [(s, b_refs.pop(0), b_refs.pop(0)) for s in steps]
            for first in range(0, rows, tile):
                here = slice(first, first + tile)
                total = None if total_ref is None else total_ref[here, :]
                for s, one, two in pairs:
                    both = jnp.concatenate([one[here, :], two[here, :]], axis=1)
                    term = jnp.dot(both, weight(s), preferred_element_type=F32)
                    total = term if total is None else total + term
                if finish is None:
                    o_refs[index][here, :] = total.astype(o_refs[index].dtype)
                else:
                    finish(refs[1:n_s], e_refs, o_refs, total, first, tile)

    terms = sum(len(steps) for _, steps in plan)
    return call(
        kernel,
        outs,
        n_s,
        [rows_at, *smem, *weights, *extras, *flat],
        name,
        2 * rows * 256 * width * terms,
    )


def finish_units(smem, extras, outs, total, first, tile):
    here = slice(first, first + tile)
    total = total + extras[0][here, :]
    proj = total[:, :HD]
    unit = proj * lax.rsqrt(jnp.sum(proj * proj, axis=-1, keepdims=True) + 1e-06)
    row = lax.broadcasted_iota(jnp.int32, (tile, HD), 0) + first
    value = jnp.where(row < smem[0][0], total[:, HD:], 0.0).astype(BF16)
    unit = unit.astype(BF16)
    outs[0][here, :HD] = unit
    outs[0][here, HD:] = value
    outs[1][here, :] = unit


def finish_out(smem, extras, outs, total, first, tile):
    here = slice(first, first + tile)
    outs[0][here, :] = (total + extras[0][here, :]).astype(BF16)


def attend(limits, groups, blocks, name, out_type=F32, tile_q=512, tile_k=512):
    n_b = len(blocks)
    flat, plan = [], []
    for queries, total, own in groups:
        plan.append((total is not None, own))
        flat += [queries] + ([total] if total is not None else [])
    rows = groups[0][0].shape[0]
    outs = [jax.ShapeDtypeStruct((rows, 2 * HD), out_type)] * len(groups)

    def kernel(*refs):
        limit = refs[0]
        kv_refs = refs[1 : 1 + n_b]
        g_refs = list(refs[1 + n_b : 1 + n_b + len(flat)])
        o_refs = refs[1 + n_b + len(flat) :]
        for index, (has_total, own) in enumerate(plan):
            q_ref = g_refs.pop(0)
            t_ref = g_refs.pop(0) if has_total else None

            @pl.loop(0, rows // tile_q)
            def _(step):
                first = pl.multiple_of(step * tile_q, tile_q)
                here = pl.ds(first, tile_q)
                queries = q_ref[here, :]
                total = None if t_ref is None else t_ref[here, :]
                for b, kv in enumerate(kv_refs):
                    for start in range(0, kv.shape[0], tile_k):
                        keys = kv[start : start + tile_k, :HD]
                        values = kv[start : start + tile_k, HD:]
                        row = lax.broadcasted_iota(jnp.int32, (tile_k, HD), 0) + start
                        counted = jnp.where(row < limit[b], 1.0, 0.0).astype(BF16)
                        scores = lax.dot_general(
                            queries, keys, (((1,), (1,)), ((), ())), preferred_element_type=F32
                        )
                        weights = jnp.exp2(scores * SCALE - SCALE)
                        if own and b == 0:
                            q_at = lax.broadcasted_iota(jnp.int32, weights.shape, 0) + first
                            k_at = lax.broadcasted_iota(jnp.int32, weights.shape, 1) + start
                            weights = jnp.where(q_at == k_at, 0.0, weights)
                        term = jnp.dot(
                            weights.astype(BF16),
                            jnp.concatenate([values, counted], axis=1),
                            preferred_element_type=F32,
                        )
                        total = term if total is None else total + term
                o_refs[index][here, :] = total.astype(out_type)

    flops = len(groups) * n_b * 4 * rows * blocks[0].shape[0] * HD * 2
    return call(kernel, outs, 1, [limits, *blocks, *flat], name, flops)


def combine(limits, mine, theirs, name):
    rows = mine.shape[0]

    def kernel(limit, a_ref, b_ref, o_ref):
        total = a_ref[...] + b_ref[...].astype(F32)
        row = lax.broadcasted_iota(jnp.int32, (rows, HD), 0)
        valid = row < limit[0]
        denom = jnp.where(valid, total[:, HD:], 1.0)
        o_ref[...] = jnp.where(valid, total[:, :HD] / denom, 0.0).astype(BF16)

    out = jax.ShapeDtypeStruct((rows, HD), BF16)
    return call(kernel, [out], 1, [limits, mine, theirs], name, rows * HD * 8)[0]


def gathered_product(block, rows_at, weights, finish, outs, smem, name):
    depth = lax.axis_size("z")
    half = depth // 2
    own, cross = block, swap(block, "xl")
    other = swap(block, "core")
    mine = [(0, own, cross)]
    both = None
    total_own = total_other = None
    for s in range(1, half):
        own, other, cross = z_step(own), z_step(other), z_step(cross)
        mine.append((s, own, cross))
        far = (s, other, swap(other, "xl"))
        if s < half - 1:
            total_own, total_other = contract(
                rows_at, weights, [[total_own, *mine], [total_other, far]], f"{name}_{s}"
            )
            mine = []
        else:
            (total_other,) = contract(
                rows_at, weights, [[total_other, far]], f"{name}_{s}"
            )
            both = swap(total_other, "core")
    own, cross = z_step(own), z_step(cross)
    mine.append((half, own, cross))
    return contract(
        rows_at,
        weights,
        [[total_own, *mine]],
        f"{name}_last",
        finish=finish,
        extras=[both],
        outs=outs,
        smem=smem,
    )


def per_device(tokens, w_query, w_value, w_out, doc_lengths):
    rows = tokens.shape[0]
    depth = lax.axis_size("z")
    xl, z, core = lax.axis_index("xl"), lax.axis_index("z"), lax.axis_index("core")
    heads = lax.axis_size(HEAD)

    steps = jnp.arange(depth // 2 + 1, dtype=jnp.int32)
    z_at = (z + jnp.where(core == 0, -steps, steps)) % depth
    rows_at = (jnp.stack([xl * depth + z_at, (1 - xl) * depth + z_at], 1).reshape(-1) * HD).astype(
        jnp.int32
    )

    in_doc = (lax.axis_index("yl") * 2 + lax.axis_index("xh")) * 2 + core
    limit = doc_lengths[lax.axis_index("yh")]

    def limits(*masks):
        return jnp.stack([limit - (in_doc ^ m) * rows for m in masks]).astype(jnp.int32)

    w_cols = lax.all_to_all(
        jnp.moveaxis(w_out.reshape(HD, heads, HD), 1, 0), HEAD, 0, 0
    ).reshape(heads * HD, HD)

    joined, unit = gathered_product(
        tokens,
        rows_at,
        [w_query, w_value],
        finish_units,
        [jax.ShapeDtypeStruct((rows, 2 * HD), BF16), jax.ShapeDtypeStruct((rows, HD), BF16)],
        [limits(0)],
        "project",
    )
    unit_other = swap(unit, "core")
    from_y, from_x = swap(joined, "yl"), swap(joined, "xh")
    from_yx = swap(joined, "yl", "xh")

    own, other = attend(
        limits(0), [(unit, None, True), (unit_other, None, False)], [joined], "attend_own"
    )
    own, other = attend(
        limits(4, 2), [(unit, own, False), (unit_other, other, False)], [from_y, from_x], "attend_near"
    )
    (other,) = attend(
        limits(6), [(unit_other, other, False)], [from_yx], "attend_far_other", out_type=BF16
    )
    theirs = swap(other, "core")
    (own,) = attend(limits(6), [(unit, own, False)], [from_yx], "attend_far_own")
    attended = combine(limits(0), own, theirs, "combine")

    return gathered_product(
        attended,
        rows_at,
        [w_cols],
        finish_out,
        [jax.ShapeDtypeStruct((rows, HD), BF16)],
        [],
        "output",
    )[0]


def solution(mesh):
    finer = Mesh(mesh.devices.reshape(2, 2, 2, 2, 2, 8), AXES)
    return jax.shard_map(
        per_device,
        mesh=finer,
        in_specs=(P(CTX, HEAD), P(None, HEAD), P(None, HEAD), P(HEAD, None), P()),
        out_specs=P(CTX, HEAD),
        check_vma=False,
    )
```

time: 310 us -> 160 us (0.52)
  waiting for transfers between devices: 184 us -> 82.4 us
  matrix products: 44.8 us -> 0 us
  Pallas kernels: 0 us -> 29.7 us
  starting transfers between devices: 7.21 us -> 35.7 us
  other arithmetic: 25.8 us -> 0.1 us
  local copies, waits for them, and re-layouts: 21.7 us -> 8.73 us
  between operations: 13.4 us -> 2.75 us
  blocking collectives: 10.6 us -> 0 us
    reduce_scatter x2 -> x0, waiting for transfers between devices: 74.8 us -> none  [reduced_to_own(): pieces = lax.psum_scatter(pieces, axes[k], scatter_dimension=0, tiled=True)]
    all_gather x1 -> x0, waiting for transfers between devices: 56 us -> none  [gather_in_order(): pieces = lax.all_gather(pieces, axes[k])]
    dot_general x18 -> x0, matrix products: 44.8 us -> none  [the longest x8 28.3 us: tile_weights(): jnp.einsum('qhd,khd->hqk', queries, key_rows, preferred_element_type=jnp....]
    pallas_call x0 -> x13, Pallas kernels: none -> 29.7 us  [call(): pl.pallas_call(kernel, out_shape=outs, in_specs=[SMEM] * smem_count + [VM...]
    ppermute x6 -> x39, waiting for transfers between devices: 53.4 us -> 82.4 us  [hop(): lax.ppermute(value, axes, [(number[c], number[tuple(target(*c))]) for c i...]
    ppermute x6 -> x39, starting transfers between devices: 7.12 us -> 28.5 us  [hop(): lax.ppermute(value, axes, [(number[c], number[tuple(target(*c))]) for c i...]
    lt x8 -> x0, other arithmetic: 18.5 us -> none  [placement(): return (position, doc_index, position - doc_index * doc_span < limit)]
    all_gather x1 -> x0, blocking collectives: 10.6 us -> none  [gather_in_order(): pieces = lax.all_gather(pieces, axes[k])]
  transfers between devices with their start and end apart: 9 -> 40, of which waited for: 8 -> 26; matrix products, arithmetic and copies ran while one was open for 2% -> 1% of each run, Pallas kernels for 0% -> 13%
where the time goes in v1:
time: 160 us; the launch traced here: 159 us
  waiting for transfers between devices  82.4 us (52%)
  starting transfers between devices  35.7 us (22%)
  Pallas kernels  29.7 us (19%)
  local copies, waits for them, and re-layouts  8.73 us (5%)
  between operations  2.75 us (2%)
    ppermute x39, waiting for transfers between devices, hop(): lax.ppermute(value, axes, [(number[c], number[tuple(target(*c))]) for c i...  82.4 us
    pallas_call x13, Pallas kernels, call(): pl.pallas_call(kernel, out_shape=outs, in_specs=[SMEM] * smem_count + [VM...  29.7 us
    ppermute x39, starting transfers between devices, hop(): lax.ppermute(value, axes, [(number[c], number[tuple(target(*c))]) for c i...  28.5 us
    all_to_all x1, starting transfers between devices, per_device(): lax.all_to_all(jnp.moveaxis(w_out.reshape(HD, heads, HD), 1, 0), HEAD, 0, 0)  7.27 us
    unnamed x22, local copies, waits for them, and re-layouts  7 us
  transfers between devices with their start and end apart: 40, of which 26 were waited for; matrix products, arithmetic and copies ran while one was open for 1% of the time, Pallas kernels for 13%

profile of v1, /device:TPU:16, one launch (start us, length us, event | category | flops | bytes accessed | tf_op | source)
XLA Modules:
  0.0 159.4 jit_solution(16330611349813199078)
XLA Ops:
  5.2 6.8 %collective-permute-done.4.refs_7_ = bf16[1024,128]{1,0:T(8,128)(2,1)S(1)} collective-permute-done((bf16[1024,128]{1,0:T(8,128)(2,1)S(1)}, bf16[1024,128]{1,0:T(8,128)(2,1)S(1)}, u32[]{:S(2)}, u32[]{:S(2)}) %collective-permute-start.4) | collective-permute-done | bytes 262176 | tf_op jit(solution)/shard_map/ppermute | solution.py:27
  12.0 2.6 %collective-permute-start.2 = (bf16[1024,128]{1,0:T(8,128)(2,1)S(1)}, bf16[1024,128]{1,0:T(8,128)(2,1)}, u32[]{:S(2)}, u32[]{:S(2)}) collective-permute-start(bf16[1024,128]{1,0:T(8,128)(2,1)S(1)} %collective-permute-done.refs_4_), channel_id=1, source_target_pairs={{0,1},{1,2},{2,3},{3,4},{4,5},{5,6},{6,7},{7,0},{16,23},{17,16},{1... | collective-permute-start | bytes 786440 | tf_op jit(solution)/shard_map/ppermute | solution.py:27
  14.5 5.0 %collective-permute-done.8.refs_7_ = bf16[1024,128]{1,0:T(8,128)(2,1)S(1)} collective-permute-done((bf16[1024,128]{1,0:T(8,128)(2,1)S(1)}, bf16[1024,128]{1,0:T(8,128)(2,1)S(1)}, u32[]{:S(2)}, u32[]{:S(2)}) %collective-permute-start.8) | collective-permute-done | bytes 262176 | tf_op jit(solution)/shard_map/ppermute | solution.py:27
  22.4 2.9 %collective-permute-done.2.refs_6_ = bf16[1024,128]{1,0:T(8,128)(2,1)} collective-permute-done((bf16[1024,128]{1,0:T(8,128)(2,1)S(1)}, bf16[1024,128]{1,0:T(8,128)(2,1)}, u32[]{:S(2)}, u32[]{:S(2)}) %collective-permute-start.2) | collective-permute-done | bytes 262176 | tf_op jit(solution)/shard_map/ppermute | solution.py:27
  42.5 7.5 %collective-permute-done.13.refs_6_ = bf16[1024,128]{1,0:T(8,128)(2,1)S(1)} collective-permute-done((bf16[1024,128]{1,0:T(8,128)(2,1)S(1)}, bf16[1024,128]{1,0:T(8,128)(2,1)S(1)}, u32[]{:S(2)}, u32[]{:S(2)}) %collective-permute-start.13) | collective-permute-done | bytes 262176 | tf_op jit(solution)/shard_map/ppermute | solution.py:27
  50.0 2.9 %collective-permute-done.14.refs_7_ = bf16[1024,128]{1,0:T(8,128)(2,1)} collective-permute-done((bf16[1024,128]{1,0:T(8,128)(2,1)S(1)}, bf16[1024,128]{1,0:T(8,128)(2,1)}, u32[]{:S(2)}, u32[]{:S(2)}) %collective-permute-start.14) | collective-permute-done | bytes 262176 | tf_op jit(solution)/shard_map/ppermute | solution.py:27
  54.9 2.8 %collective-permute-done.15.refs_8_ = bf16[1024,128]{1,0:T(8,128)(2,1)S(1)} collective-permute-done((bf16[1024,128]{1,0:T(8,128)(2,1)S(1)}, bf16[1024,128]{1,0:T(8,128)(2,1)S(1)}, u32[]{:S(2)}, u32[]{:S(2)}) %collective-permute-start.15) | collective-permute-done | bytes 262176 | tf_op jit(solution)/shard_map/ppermute | solution.py:27
  57.6 3.1 %collective-permute-done.16.refs_9_ = bf16[1024,128]{1,0:T(8,128)(2,1)S(1)} collective-permute-done((bf16[1024,128]{1,0:T(8,128)(2,1)}, bf16[1024,128]{1,0:T(8,128)(2,1)S(1)}, u32[]{:S(2)}, u32[]{:S(2)}) %collective-permute-start.16) | collective-permute-done | bytes 262176 | tf_op jit(solution)/shard_map/ppermute | solution.py:27
  60.8 2.7 %project_last.1 = (bf16[1024,256]{1,0:T(8,128)(2,1)}, bf16[1024,128]{1,0:T(8,128)(2,1)}) custom-call(s32[10]{0:T(128)S(1)} %mul.35.refs_0_, s32[1]{0:T(128)} %bitcast.3.refs_1_.refs_0_.limit, bf16[2048,128]{1,0:T(8,128)(2,1)S(1)} %copy-done.2, bf16[2048,128]{1,0:T(8,128)(2,1)S(1)} %copy-done.4, f32[1024,256]{1,0:T(8,128)} %collective-permute-done.12.refs_4_, ...), custom_call_target="tpu_custom_call" | custom-call | flops 268435456 | bytes 4980780 | tf_op jit(solution)/shard_map/project_last/pallas_call | solution.py:45
  64.7 3.0 %collective-permute-start.19 = (bf16[1024,256]{1,0:T(8,128)(2,1)}, bf16[1024,256]{1,0:T(8,128)(2,1)S(1)}, u32[]{:S(2)}, u32[]{:S(2)}) collective-permute-start(bf16[1024,256]{1,0:T(8,128)(2,1)} %get-tuple-element.23.refs_1_), channel_id=1, source_target_pairs={{0,32},{32,0},{1,33},{33,1},{2,34},{34,2},{3,35},{35,3},{4,36},{36... | collective-permute-start | bytes 1572872 | tf_op jit(solution)/shard_map/ppermute | solution.py:27
  70.5 5.5 %attend_own.1 = (f32[1024,256]{1,0:T(8,128)S(1)}, f32[1024,256]{1,0:T(8,128)S(1)}) custom-call(s32[1]{0:T(128)} %bitcast.3.refs_1_.refs_0_.limit, bf16[1024,256]{1,0:T(8,128)(2,1)} %get-tuple-element.23.refs_1_, bf16[1024,128]{1,0:T(8,128)(2,1)} %get-tuple-element.24.refs_2_.refs_3_, bf16[1024,128]{1,0:T(8,128)(2,1)S(1)} %collective-permute-done.20.refs_3_.refs_5_.refs_2_), custom_call_target="tpu_custom_call" | custom-call | flops 2147483648 | bytes 3145732 | tf_op jit(solution)/shard_map/attend_own/pallas_call | solution.py:45
  76.0 3.6 %collective-permute-done.19.refs_2_ = bf16[1024,256]{1,0:T(8,128)(2,1)S(1)} collective-permute-done((bf16[1024,256]{1,0:T(8,128)(2,1)}, bf16[1024,256]{1,0:T(8,128)(2,1)S(1)}, u32[]{:S(2)}, u32[]{:S(2)}) %collective-permute-start.19) | collective-permute-done | bytes 524320 | tf_op jit(solution)/shard_map/ppermute | solution.py:27
  79.6 6.4 %attend_near.1 = (f32[1024,256]{1,0:T(8,128)S(1)}, f32[1024,256]{1,0:T(8,128)S(1)}) custom-call(s32[2]{0:T(128)S(1)} %pad_add_fusion.refs_0_, bf16[1024,256]{1,0:T(8,128)(2,1)S(1)} %collective-permute-done.18.refs_1_, bf16[1024,256]{1,0:T(8,128)(2,1)S(1)} %collective-permute-done.19.refs_2_, bf16[1024,128]{1,0:T(8,128)(2,1)} %get-tuple-element.24.refs_2_.refs_3_, ...), custom_call_target="tpu_custom_call" | custom-call | flops 4294967296 | bytes 5767176 | tf_op jit(solution)/shard_map/attend_near/pallas_call | solution.py:45
  89.6 2.6 %attend_far_own.1.a_ref = f32[1024,256]{1,0:T(8,128)S(1)} custom-call(s32[1]{0:T(128)} %bitcast.4.refs_0_, bf16[1024,256]{1,0:T(8,128)(2,1)S(1)} %collective-permute-done.17.refs_1_, bf16[1024,128]{1,0:T(8,128)(2,1)} %get-tuple-element.24.refs_2_.refs_3_, f32[1024,256]{1,0:T(8,128)S(1)} %get-tuple-element.27.refs_3_), custom_call_target="tpu_custom_call" | custom-call | flops 1073741824 | bytes 2883588 | tf_op jit(solution)/shard_map/attend_far_own/pallas_call | solution.py:45
  95.2 7.3 %all-to-all-start = ((bf16[16,128,128]{2,1,0:T(8,128)(2,1)}), bf16[16,128,128]{2,1,0:T(8,128)(2,1)S(1)}, u32[]{:S(2)}, u32[]{:S(2)}) async-start(bf16[16,128,128]{2,1,0:T(8,128)(2,1)} %bitcast_bitcast_fusion), calls=%async_computation | async-start | bytes 1048576 | tf_op jit(solution)/shard_map/all_to_all | solution.py:249
  107.4 7.3 %collective-permute-done.22.refs_3_ = bf16[1024,128]{1,0:T(8,128)(2,1)S(1)} collective-permute-done((bf16[1024,128]{1,0:T(8,128)(2,1)S(1)}, bf16[1024,128]{1,0:T(8,128)(2,1)S(1)}, u32[]{:S(2)}, u32[]{:S(2)}) %collective-permute-start.22) | collective-permute-done | bytes 262176 | tf_op jit(solution)/shard_map/ppermute | solution.py:27
  115.9 5.6 %collective-permute-done.30.refs_6_ = bf16[1024,128]{1,0:T(8,128)(2,1)} collective-permute-done((bf16[1024,128]{1,0:T(8,128)(2,1)S(1)}, bf16[1024,128]{1,0:T(8,128)(2,1)}, u32[]{:S(2)}, u32[]{:S(2)}) %collective-permute-start.30) | collective-permute-done | bytes 262176 | tf_op jit(solution)/shard_map/ppermute | solution.py:27
  121.5 2.7 %collective-permute-done.23.refs_4_ = bf16[1024,128]{1,0:T(8,128)(2,1)S(1)} collective-permute-done((bf16[1024,128]{1,0:T(8,128)(2,1)S(1)}, bf16[1024,128]{1,0:T(8,128)(2,1)S(1)}, u32[]{:S(2)}, u32[]{:S(2)}) %collective-permute-start.23) | collective-permute-done | bytes 262176 | tf_op jit(solution)/shard_map/ppermute | solution.py:27
  124.2 2.8 %collective-permute-done.24.refs_5_ = bf16[1024,128]{1,0:T(8,128)(2,1)S(1)} collective-permute-done((bf16[1024,128]{1,0:T(8,128)(2,1)S(1)}, bf16[1024,128]{1,0:T(8,128)(2,1)S(1)}, u32[]{:S(2)}, u32[]{:S(2)}) %collective-permute-start.24) | collective-permute-done | bytes 262176 | tf_op jit(solution)/shard_map/ppermute | solution.py:27
  132.8 2.8 %collective-permute-done.29.refs_4_ = bf16[1024,128]{1,0:T(8,128)(2,1)} collective-permute-done((bf16[1024,128]{1,0:T(8,128)(2,1)S(1)}, bf16[1024,128]{1,0:T(8,128)(2,1)}, u32[]{:S(2)}, u32[]{:S(2)}) %collective-permute-start.29) | collective-permute-done | bytes 262176 | tf_op jit(solution)/shard_map/ppermute | solution.py:27
  137.9 4.1 %collective-permute-done.31.refs_7_ = bf16[1024,128]{1,0:T(8,128)(2,1)} collective-permute-done((bf16[1024,128]{1,0:T(8,128)(2,1)}, bf16[1024,128]{1,0:T(8,128)(2,1)}, u32[]{:S(2)}, u32[]{:S(2)}) %collective-permute-start.31) | collective-permute-done | bytes 262176 | tf_op jit(solution)/shard_map/ppermute | solution.py:27
  143.6 2.7 %collective-permute-done.33.refs_4_ = bf16[1024,128]{1,0:T(8,128)(2,1)S(1)} collective-permute-done((bf16[1024,128]{1,0:T(8,128)(2,1)S(1)}, bf16[1024,128]{1,0:T(8,128)(2,1)S(1)}, u32[]{:S(2)}, u32[]{:S(2)}) %collective-permute-start.33) | collective-permute-done | bytes 262176 | tf_op jit(solution)/shard_map/ppermute | solution.py:27
  149.7 5.2 %collective-permute-done.37.refs_6_ = bf16[1024,128]{1,0:T(8,128)(2,1)S(1)} collective-permute-done((bf16[1024,128]{1,0:T(8,128)(2,1)S(1)}, bf16[1024,128]{1,0:T(8,128)(2,1)S(1)}, u32[]{:S(2)}, u32[]{:S(2)}) %collective-permute-start.37) | collective-permute-done | bytes 262176 | tf_op jit(solution)/shard_map/ppermute | solution.py:27
  154.9 2.8 %collective-permute-done.38.refs_7_ = bf16[1024,128]{1,0:T(8,128)(2,1)S(1)} collective-permute-done((bf16[1024,128]{1,0:T(8,128)(2,1)S(1)}, bf16[1024,128]{1,0:T(8,128)(2,1)S(1)}, u32[]{:S(2)}, u32[]{:S(2)}) %collective-permute-start.38) | collective-permute-done | bytes 262176 | tf_op jit(solution)/shard_map/ppermute | solution.py:27
  (98 shorter events, 55.8 us)
Async XLA Ops:
  1.8 10.2 %collective-permute-start.4 = (bf16[1024,128]{1,0:T(8,128)(2,1)S(1)}, bf16[1024,128]{1,0:T(8,128)(2,1)S(1)}, u32[]{:S(2)}, u32[]{:S(2)}) collective-permute-start(bf16[1024,128]{1,0:T(8,128)(2,1)S(1)} %collective-permute-done.3), channel_id=1, source_target_pairs={{0,1},{1,2},{2,3},{3,4},{4,5},{5,6},{6,7},{7,0},{16,23},{17,16},{1... | collective-permute-start | bytes 786440 | tf_op jit(solution)/shard_map/ppermute | solution.py:27
  12.0 10.4 %collective-permute-start.1 = (bf16[1024,128]{1,0:T(8,128)(2,1)}, bf16[1024,128]{1,0:T(8,128)(2,1)S(1)}, u32[]{:S(2)}, u32[]{:S(2)}) collective-permute-start(bf16[1024,128]{1,0:T(8,128)(2,1)} %refs_3_.2), channel_id=1, source_target_pairs={{0,1},{1,2},{2,3},{3,4},{4,5},{5,6},{6,7},{7,0},{16,23},{17,16},{1... | collective-permute-start | bytes 786440 | tf_op jit(solution)/shard_map/ppermute | solution.py:27
  12.0 13.3 %collective-permute-start.2 = (bf16[1024,128]{1,0:T(8,128)(2,1)S(1)}, bf16[1024,128]{1,0:T(8,128)(2,1)}, u32[]{:S(2)}, u32[]{:S(2)}) collective-permute-start(bf16[1024,128]{1,0:T(8,128)(2,1)S(1)} %collective-permute-done.refs_4_), channel_id=1, source_target_pairs={{0,1},{1,2},{2,3},{3,4},{4,5},{5,6},{6,7},{7,0},{16,23},{17,16},{1... | collective-permute-start | bytes 786440 | tf_op jit(solution)/shard_map/ppermute | solution.py:27
  19.5 10.2 %collective-permute-start.5 = (bf16[1024,128]{1,0:T(8,128)(2,1)S(1)}, bf16[1024,128]{1,0:T(8,128)(2,1)S(1)}, u32[]{:S(2)}, u32[]{:S(2)}) collective-permute-start(bf16[1024,128]{1,0:T(8,128)(2,1)S(1)} %collective-permute-done.4.refs_7_), channel_id=1, source_target_pairs={{0,8},{8,0},{1,9},{9,1},{2,10},{10,2},{3,11},{11,3},{4,12},{12,4},... | collective-permute-start | bytes 786440 | tf_op jit(solution)/shard_map/ppermute | solution.py:27
  22.3 13.7 %collective-permute-start.6 = (bf16[1024,128]{1,0:T(8,128)(2,1)S(1)}, bf16[1024,128]{1,0:T(8,128)(2,1)S(1)}, u32[]{:S(2)}, u32[]{:S(2)}) collective-permute-start(bf16[1024,128]{1,0:T(8,128)(2,1)S(1)} %collective-permute-done.1.refs_5_), channel_id=1, source_target_pairs={{0,1},{1,2},{2,3},{3,4},{4,5},{5,6},{6,7},{7,0},{16,23},{17,16},{1... | collective-permute-start | bytes 786440 | tf_op jit(solution)/shard_map/ppermute | solution.py:27
  25.3 10.8 %collective-permute-start.7 = (bf16[1024,128]{1,0:T(8,128)(2,1)}, bf16[1024,128]{1,0:T(8,128)(2,1)S(1)}, u32[]{:S(2)}, u32[]{:S(2)}) collective-permute-start(bf16[1024,128]{1,0:T(8,128)(2,1)} %collective-permute-done.2.refs_6_), channel_id=1, source_target_pairs={{0,1},{1,2},{2,3},{3,4},{4,5},{5,6},{6,7},{7,0},{16,23},{17,16},{1... | collective-permute-start | bytes 786440 | tf_op jit(solution)/shard_map/ppermute | solution.py:27
  25.3 10.8 %collective-permute-start.9 = (bf16[1024,128]{1,0:T(8,128)(2,1)S(1)}, bf16[1024,128]{1,0:T(8,128)(2,1)S(1)}, u32[]{:S(2)}, u32[]{:S(2)}) collective-permute-start(bf16[1024,128]{1,0:T(8,128)(2,1)S(1)} %collective-permute-done.8.refs_7_), channel_id=1, source_target_pairs={{0,8},{8,0},{1,9},{9,1},{2,10},{10,2},{3,11},{11,3},{4,12},{12,4},... | collective-permute-start | bytes 786440 | tf_op jit(solution)/shard_map/ppermute | solution.py:27
  28.1 11.9 %collective-permute-start.11 = (bf16[1024,128]{1,0:T(8,128)(2,1)}, bf16[1024,128]{1,0:T(8,128)(2,1)}, u32[]{:S(2)}, u32[]{:S(2)}) collective-permute-start(bf16[1024,128]{1,0:T(8,128)(2,1)} %collective-permute-done.10.refs_4_), channel_id=1, source_target_pairs={{0,8},{8,0},{1,9},{9,1},{2,10},{10,2},{3,11},{11,3},{4,12},{12,4},... | collective-permute-start | bytes 786440 | tf_op jit(solution)/shard_map/ppermute | solution.py:27
  42.4 18.3 %collective-permute-start.12 = (f32[1024,256]{1,0:T(8,128)}, f32[1024,256]{1,0:T(8,128)}, u32[]{:S(2)}, u32[]{:S(2)}) collective-permute-start(f32[1024,256]{1,0:T(8,128)} %project_3.1), channel_id=1, source_target_pairs={{0,16},{16,0},{1,17},{17,1},{2,18},{18,2},{3,19},{19,3},{4,20},{20... | collective-permute-start | bytes 3145736 | tf_op jit(solution)/shard_map/ppermute | solution.py:27
  42.5 10.5 %collective-permute-start.14 = (bf16[1024,128]{1,0:T(8,128)(2,1)S(1)}, bf16[1024,128]{1,0:T(8,128)(2,1)}, u32[]{:S(2)}, u32[]{:S(2)}) collective-permute-start(bf16[1024,128]{1,0:T(8,128)(2,1)S(1)} %collective-permute-done.7.refs_5_), channel_id=1, source_target_pairs={{0,1},{1,2},{2,3},{3,4},{4,5},{5,6},{6,7},{7,0},{16,23},{17,16},{1... | collective-permute-start | bytes 786440 | tf_op jit(solution)/shard_map/ppermute | solution.py:27
  63.5 12.5 %collective-permute-start.18 = (bf16[1024,256]{1,0:T(8,128)(2,1)}, bf16[1024,256]{1,0:T(8,128)(2,1)S(1)}, u32[]{:S(2)}, u32[]{:S(2)}) collective-permute-start(bf16[1024,256]{1,0:T(8,128)(2,1)} %get-tuple-element.23.refs_1_), channel_id=1, source_target_pairs={{0,64},{64,0},{1,65},{65,1},{2,66},{66,2},{3,67},{67,3},{4,68},{68... | collective-permute-start | bytes 1572872 | tf_op jit(solution)/shard_map/ppermute | solution.py:27
  64.7 14.8 %collective-permute-start.19 = (bf16[1024,256]{1,0:T(8,128)(2,1)}, bf16[1024,256]{1,0:T(8,128)(2,1)S(1)}, u32[]{:S(2)}, u32[]{:S(2)}) collective-permute-start(bf16[1024,256]{1,0:T(8,128)(2,1)} %get-tuple-element.23.refs_1_), channel_id=1, source_target_pairs={{0,32},{32,0},{1,33},{33,1},{2,34},{34,2},{3,35},{35,3},{4,36},{36... | collective-permute-start | bytes 1572872 | tf_op jit(solution)/shard_map/ppermute | solution.py:27
  69.8 18.0 %collective-permute-start.17 = (bf16[1024,256]{1,0:T(8,128)(2,1)}, bf16[1024,256]{1,0:T(8,128)(2,1)S(1)}, u32[]{:S(2)}, u32[]{:S(2)}) collective-permute-start(bf16[1024,256]{1,0:T(8,128)(2,1)} %get-tuple-element.23.refs_1_), channel_id=1, source_target_pairs={{0,96},{32,64},{64,32},{96,0},{1,97},{33,65},{65,33},{97,1},{2,98}... | collective-permute-start | bytes 1572872 | tf_op jit(solution)/shard_map/ppermute | solution.py:27
  94.1 10.3 %collective-permute-start.26 = (bf16[1024,128]{1,0:T(8,128)(2,1)S(1)}, bf16[1024,128]{1,0:T(8,128)(2,1)S(1)}, u32[]{:S(2)}, u32[]{:S(2)}) collective-permute-start(bf16[1024,128]{1,0:T(8,128)(2,1)S(1)} %collective-permute-done.25), channel_id=1, source_target_pairs={{0,1},{1,2},{2,3},{3,4},{4,5},{5,6},{6,7},{7,0},{16,23},{17,16},{1... | collective-permute-start | bytes 786440 | tf_op jit(solution)/shard_map/ppermute | solution.py:27
  95.2 40.4 %all-to-all-start = ((bf16[16,128,128]{2,1,0:T(8,128)(2,1)}), bf16[16,128,128]{2,1,0:T(8,128)(2,1)S(1)}, u32[]{:S(2)}, u32[]{:S(2)}) async-start(bf16[16,128,128]{2,1,0:T(8,128)(2,1)} %bitcast_bitcast_fusion), calls=%async_computation | async-start | bytes 1048576 | tf_op jit(solution)/shard_map/all_to_all | solution.py:249
  102.5 12.2 %collective-permute-start.22 = (bf16[1024,128]{1,0:T(8,128)(2,1)S(1)}, bf16[1024,128]{1,0:T(8,128)(2,1)S(1)}, u32[]{:S(2)}, u32[]{:S(2)}) collective-permute-start(bf16[1024,128]{1,0:T(8,128)(2,1)S(1)} %combine.1.refs_2_), channel_id=1, source_target_pairs={{0,8},{8,0},{1,9},{9,1},{2,10},{10,2},{3,11},{11,3},{4,12},{12,4},... | collective-permute-start | bytes 786440 | tf_op jit(solution)/shard_map/ppermute | solution.py:27
  104.4 17.1 %collective-permute-start.30 = (bf16[1024,128]{1,0:T(8,128)(2,1)S(1)}, bf16[1024,128]{1,0:T(8,128)(2,1)}, u32[]{:S(2)}, u32[]{:S(2)}) collective-permute-start(bf16[1024,128]{1,0:T(8,128)(2,1)S(1)} %collective-permute-done.26.refs_6_), channel_id=1, source_target_pairs={{0,1},{1,2},{2,3},{3,4},{4,5},{5,6},{6,7},{7,0},{16,23},{17,16},{1... | collective-permute-start | bytes 786440 | tf_op jit(solution)/shard_map/ppermute | solution.py:27
  105.9 18.3 %collective-permute-start.23 = (bf16[1024,128]{1,0:T(8,128)(2,1)S(1)}, bf16[1024,128]{1,0:T(8,128)(2,1)S(1)}, u32[]{:S(2)}, u32[]{:S(2)}) collective-permute-start(bf16[1024,128]{1,0:T(8,128)(2,1)S(1)} %combine.1.refs_2_), channel_id=1, source_target_pairs={{0,1},{1,2},{2,3},{3,4},{4,5},{5,6},{6,7},{7,0},{16,23},{17,16},{1... | collective-permute-start | bytes 786440 | tf_op jit(solution)/shard_map/ppermute | solution.py:27
  114.7 12.3 %collective-permute-start.24 = (bf16[1024,128]{1,0:T(8,128)(2,1)S(1)}, bf16[1024,128]{1,0:T(8,128)(2,1)S(1)}, u32[]{:S(2)}, u32[]{:S(2)}) collective-permute-start(bf16[1024,128]{1,0:T(8,128)(2,1)S(1)} %collective-permute-done.22.refs_3_), channel_id=1, source_target_pairs={{0,1},{1,2},{2,3},{3,4},{4,5},{5,6},{6,7},{7,0},{16,23},{17,16},{1... | collective-permute-start | bytes 786440 | tf_op jit(solution)/shard_map/ppermute | solution.py:27
  128.5 13.4 %collective-permute-start.31 = (bf16[1024,128]{1,0:T(8,128)(2,1)}, bf16[1024,128]{1,0:T(8,128)(2,1)}, u32[]{:S(2)}, u32[]{:S(2)}) collective-permute-start(bf16[1024,128]{1,0:T(8,128)(2,1)} %collective-permute-done.30.refs_6_), channel_id=1, source_target_pairs={{0,8},{8,0},{1,9},{9,1},{2,10},{10,2},{3,11},{11,3},{4,12},{12,4},... | collective-permute-start | bytes 786440 | tf_op jit(solution)/shard_map/ppermute | solution.py:27
  129.8 16.5 %collective-permute-start.33 = (bf16[1024,128]{1,0:T(8,128)(2,1)S(1)}, bf16[1024,128]{1,0:T(8,128)(2,1)S(1)}, u32[]{:S(2)}, u32[]{:S(2)}) collective-permute-start(bf16[1024,128]{1,0:T(8,128)(2,1)S(1)} %collective-permute-done.32.refs_3_), channel_id=1, source_target_pairs={{0,8},{8,0},{1,9},{9,1},{2,10},{10,2},{3,11},{11,3},{4,12},{12,4},... | collective-permute-start | bytes 786440 | tf_op jit(solution)/shard_map/ppermute | solution.py:27
  132.8 14.5 %collective-permute-start.35 = (bf16[1024,128]{1,0:T(8,128)(2,1)}, bf16[1024,128]{1,0:T(8,128)(2,1)S(1)}, u32[]{:S(2)}, u32[]{:S(2)}) collective-permute-start(bf16[1024,128]{1,0:T(8,128)(2,1)} %collective-permute-done.28.refs_3_), channel_id=1, source_target_pairs={{0,1},{1,2},{2,3},{3,4},{4,5},{5,6},{6,7},{7,0},{16,23},{17,16},{1... | collective-permute-start | bytes 786440 | tf_op jit(solution)/shard_map/ppermute | solution.py:27
  135.6 12.6 %collective-permute-start.36 = (bf16[1024,128]{1,0:T(8,128)(2,1)}, bf16[1024,128]{1,0:T(8,128)(2,1)S(1)}, u32[]{:S(2)}, u32[]{:S(2)}) collective-permute-start(bf16[1024,128]{1,0:T(8,128)(2,1)} %collective-permute-done.29.refs_4_), channel_id=1, source_target_pairs={{0,1},{1,2},{2,3},{3,4},{4,5},{5,6},{6,7},{7,0},{16,23},{17,16},{1... | collective-permute-start | bytes 786440 | tf_op jit(solution)/shard_map/ppermute | solution.py:27
  147.1 10.6 %collective-permute-start.34 = (f32[1024,128]{1,0:T(8,128)S(1)}, f32[1024,128]{1,0:T(8,128)S(1)}, u32[]{:S(2)}, u32[]{:S(2)}) collective-permute-start(f32[1024,128]{1,0:T(8,128)S(1)} %output_3.1), channel_id=1, source_target_pairs={{0,16},{16,0},{1,17},{17,1},{2,18},{18,2},{3,19},{19,3},{4,20},{20... | collective-permute-start | bytes 1572872 | tf_op jit(solution)/shard_map/ppermute | solution.py:27
  (27 other events, 251.0 us)

commit v2 on v1

--- a/solution.py
+++ b/solution.py
@@ -10,6 +10,7 @@
 from jax.sharding import PartitionSpec as P
 
 HD = 128
+ROWS = 1024
 HEAD = ("xl", "z")
 CTX = ("yh", "yl", "xh", "core")
 AXES = CTX + HEAD
@@ -53,7 +54,16 @@
     )(*args)
 
 
-def contract(rows_at, weights, jobs, name, finish=None, extras=(), outs=None, smem=()):
+def after(value, *others):
+    return lax.optimization_barrier((value, *others))[0]
+
+
+def valid_rows(doc_ref, mask):
+    in_doc = (lax.axis_index("yl") * 2 + lax.axis_index("xh")) * 2 + lax.axis_index("core")
+    return doc_ref[lax.axis_index("yh")] - (in_doc ^ mask) * ROWS
+
+
+def contract(weights, jobs, name, finish=None, extras=(), outs=None, smem=()):
     width = sum(w.shape[1] for w in weights)
     flat, plan = [], []
     for total, *terms in jobs:
@@ -63,21 +73,23 @@
     tile = 256
     if outs is None:
         outs = [jax.ShapeDtypeStruct((rows, width), F32)] * len(jobs)
-    n_s, n_w, n_e, n_f = 1 + len(smem), len(weights), len(extras), len(flat)
+    n_s, n_w, n_e, n_f = len(smem), len(weights), len(extras), len(flat)
+    depth = lax.axis_size("z")
 
     def kernel(*refs):
-        at = refs[0]
         w_refs = refs[n_s : n_s + n_w]
         e_refs = refs[n_s + n_w : n_s + n_w + n_e]
         b_refs = list(refs[n_s + n_w + n_e : n_s + n_w + n_e + n_f])
         o_refs = refs[n_s + n_w + n_e + n_f :]
+        xl, z, core = lax.axis_index("xl"), lax.axis_index("z"), lax.axis_index("core")
         taken = {}
 
         def weight(step):
             if step not in taken:
+                z_at = (z + depth + (2 * core - 1) * step) % depth
                 halves = []
-                for i in (0, 1):
-                    first = pl.multiple_of(at[2 * step + i], HD)
+                for side in (xl, 1 - xl):
+                    first = pl.multiple_of((side * depth + z_at) * HD, HD)
                     halves.append(
                         jnp.concatenate([w[pl.ds(first, HD), :] for w in w_refs], axis=1)
                     )
@@ -97,14 +109,14 @@
                 if finish is None:
                     o_refs[index][here, :] = total.astype(o_refs[index].dtype)
                 else:
-                    finish(refs[1:n_s], e_refs, o_refs, total, first, tile)
+                    finish(refs[:n_s], e_refs, o_refs, total, first, tile)
 
     terms = sum(len(steps) for _, steps in plan)
     return call(
         kernel,
         outs,
         n_s,
-        [rows_at, *smem, *weights, *extras, *flat],
+        [*smem, *weights, *extras, *flat],
         name,
         2 * rows * 256 * width * terms,
     )
@@ -116,7 +128,7 @@
     proj = total[:, :HD]
     unit = proj * lax.rsqrt(jnp.sum(proj * proj, axis=-1, keepdims=True) + 1e-06)
     row = lax.broadcasted_iota(jnp.int32, (tile, HD), 0) + first
-    value = jnp.where(row < smem[0][0], total[:, HD:], 0.0).astype(BF16)
+    value = jnp.where(row < valid_rows(smem[0], 0), total[:, HD:], 0.0).astype(BF16)
     unit = unit.astype(BF16)
     outs[0][here, :HD] = unit
     outs[0][here, HD:] = value
@@ -128,7 +140,8 @@
     outs[0][here, :] = (total + extras[0][here, :]).astype(BF16)
 
 
-def attend(limits, groups, blocks, name, out_type=F32, tile_q=512, tile_k=512):
+def attend(doc_lengths, groups, blocks, name, out_type=F32, tile_q=512, tile_k=512):
+    masks, blocks = zip(*blocks)
     n_b = len(blocks)
     flat, plan = [], []
     for queries, total, own in groups:
@@ -138,7 +151,7 @@
     outs = [jax.ShapeDtypeStruct((rows, 2 * HD), out_type)] * len(groups)
 
     def kernel(*refs):
-        limit = refs[0]
+        limit = [valid_rows(refs[0], mask) for mask in masks]
         kv_refs = refs[1 : 1 + n_b]
         g_refs = list(refs[1 + n_b : 1 + n_b + len(flat)])
         o_refs = refs[1 + n_b + len(flat) :]
@@ -175,49 +188,67 @@
                 o_refs[index][here, :] = total.astype(out_type)
 
     flops = len(groups) * n_b * 4 * rows * blocks[0].shape[0] * HD * 2
-    return call(kernel, outs, 1, [limits, *blocks, *flat], name, flops)
-
-
-def combine(limits, mine, theirs, name):
+    return call(kernel, outs, 1, [doc_lengths, *blocks, *flat], name, flops)
+
+
+def combine(doc_lengths, mine, theirs, name):
     rows = mine.shape[0]
 
-    def kernel(limit, a_ref, b_ref, o_ref):
+    def kernel(doc_ref, a_ref, b_ref, o_ref):
         total = a_ref[...] + b_ref[...].astype(F32)
         row = lax.broadcasted_iota(jnp.int32, (rows, HD), 0)
-        valid = row < limit[0]
+        valid = row < valid_rows(doc_ref, 0)
         denom = jnp.where(valid, total[:, HD:], 1.0)
         o_ref[...] = jnp.where(valid, total[:, :HD] / denom, 0.0).astype(BF16)
 
     out = jax.ShapeDtypeStruct((rows, HD), BF16)
-    return call(kernel, [out], 1, [limits, mine, theirs], name, rows * HD * 8)[0]
-
-
-def gathered_product(block, rows_at, weights, finish, outs, smem, name):
-    depth = lax.axis_size("z")
-    half = depth // 2
-    own, cross = block, swap(block, "xl")
-    other = swap(block, "core")
-    mine = [(0, own, cross)]
-    both = None
+    return call(kernel, [out], 1, [doc_lengths, mine, theirs], name, rows * HD * 8)[0]
+
+
+def column_parts(matrix, count):
+    rows, width = matrix.shape[0], matrix.shape[1] // count
+
+    def kernel(m_ref, o_ref):
+        for i in range(count):
+            o_ref[i] = m_ref[:, i * width : (i + 1) * width]
+
+    out = jax.ShapeDtypeStruct((count, rows, width), matrix.dtype)
+    return call(kernel, [out], 0, [matrix], "column_parts", 0)[0]
+
+
+def gathered_product(block, weights, finish, outs, smem, name):
+    half = lax.axis_size("z") // 2
+    own, other, cross = [block], [swap(block, "core")], [swap(block, "xl")]
+    far = [None]
     total_own = total_other = None
+    mine = [(0, own[0], cross[0])]
     for s in range(1, half):
-        own, other, cross = z_step(own), z_step(other), z_step(cross)
-        mine.append((s, own, cross))
-        far = (s, other, swap(other, "xl"))
-        if s < half - 1:
-            total_own, total_other = contract(
-                rows_at, weights, [[total_own, *mine], [total_other, far]], f"{name}_{s}"
-            )
-            mine = []
-        else:
-            (total_other,) = contract(
-                rows_at, weights, [[total_other, far]], f"{name}_{s}"
-            )
-            both = swap(total_other, "core")
-    own, cross = z_step(own), z_step(cross)
-    mine.append((half, own, cross))
+        own_from, other_from, cross_from = own[-1], other[-1], cross[-1]
+        if s > 1:
+            own_from = after(own_from, cross[s - 2])
+            other_from = after(other_from, own[s - 1])
+            cross_from = after(cross_from, other[s - 1], *far[s - 2 : s - 1][: s - 2])
+        own.append(z_step(own_from))
+        other.append(z_step(other_from))
+        cross.append(z_step(cross_from))
+        far.append(swap(other[s], "xl"))
+    own.append(z_step(after(own[-1], cross[half - 2])))
+    cross.append(z_step(after(cross[-1], own[half - 1], far[half - 2])))
+
+    for s in range(1, half - 1):
+        mine.append((s, own[s], cross[s]))
+        mine[0] = (mine[0][0], after(mine[0][1], own[s + 1], other[s + 1], cross[s + 1]), mine[0][2])
+        total_own, total_other = contract(
+            weights, [[total_own, *mine], [total_other, (s, other[s], far[s])]], f"{name}_{s}"
+        )
+        mine = []
+    last_other = after(other[half - 1], own[half])
+    (total_other,) = contract(
+        weights, [[total_other, (half - 1, last_other, far[half - 1])]], f"{name}_{half - 1}"
+    )
+    both = swap(total_other, "core")
+    mine += [(s, own[s], cross[s]) for s in (half - 1, half)]
     return contract(
-        rows_at,
         weights,
         [[total_own, *mine]],
         f"{name}_last",
@@ -230,55 +261,41 @@
 
 def per_device(tokens, w_query, w_value, w_out, doc_lengths):
     rows = tokens.shape[0]
-    depth = lax.axis_size("z")
-    xl, z, core = lax.axis_index("xl"), lax.axis_index("z"), lax.axis_index("core")
     heads = lax.axis_size(HEAD)
-
-    steps = jnp.arange(depth // 2 + 1, dtype=jnp.int32)
-    z_at = (z + jnp.where(core == 0, -steps, steps)) % depth
-    rows_at = (jnp.stack([xl * depth + z_at, (1 - xl) * depth + z_at], 1).reshape(-1) * HD).astype(
-        jnp.int32
-    )
-
-    in_doc = (lax.axis_index("yl") * 2 + lax.axis_index("xh")) * 2 + core
-    limit = doc_lengths[lax.axis_index("yh")]
-
-    def limits(*masks):
-        return jnp.stack([limit - (in_doc ^ m) * rows for m in masks]).astype(jnp.int32)
-
-    w_cols = lax.all_to_all(
-        jnp.moveaxis(w_out.reshape(HD, heads, HD), 1, 0), HEAD, 0, 0
-    ).reshape(heads * HD, HD)
 
     joined, unit = gathered_product(
         tokens,
-        rows_at,
         [w_query, w_value],
         finish_units,
         [jax.ShapeDtypeStruct((rows, 2 * HD), BF16), jax.ShapeDtypeStruct((rows, HD), BF16)],
-        [limits(0)],
+        [doc_lengths],
         "project",
     )
     unit_other = swap(unit, "core")
     from_y, from_x = swap(joined, "yl"), swap(joined, "xh")
     from_yx = swap(joined, "yl", "xh")
+    w_parts = column_parts(w_out, heads)
 
     own, other = attend(
-        limits(0), [(unit, None, True), (unit_other, None, False)], [joined], "attend_own"
-    )
+        doc_lengths, [(unit, None, True), (unit_other, None, False)], [(0, joined)], "attend_own"
+    )
+    w_cols = lax.all_to_all(after(w_parts, own, from_y, from_x), HEAD, 0, 0)
+    w_cols = w_cols.reshape(heads * HD, HD)
     own, other = attend(
-        limits(4, 2), [(unit, own, False), (unit_other, other, False)], [from_y, from_x], "attend_near"
+        doc_lengths,
+        [(unit, own, False), (unit_other, other, False)],
+        [(4, from_y), (2, from_x)],
+        "attend_near",
     )
     (other,) = attend(
-        limits(6), [(unit_other, other, False)], [from_yx], "attend_far_other", out_type=BF16
+        doc_lengths, [(unit_other, other, False)], [(6, from_yx)], "attend_far_other", out_type=BF16
     )
     theirs = swap(other, "core")
-    (own,) = attend(limits(6), [(unit, own, False)], [from_yx], "attend_far_own")
-    attended = combine(limits(0), own, theirs, "combine")
+    (own,) = attend(doc_lengths, [(unit, own, False)], [(6, from_yx)], "attend_far_own")
+    attended = combine(doc_lengths, after(own, w_cols), theirs, "combine")
 
     return gathered_product(
         attended,
-        rows_at,
         [w_cols],
         finish_out,
         [jax.ShapeDtypeStruct((rows, HD), BF16)],

time: 160 us -> 144 us (0.900)
  waiting for transfers between devices: 82.4 us -> 71.2 us
  Pallas kernels: 29.7 us -> 21.9 us
  starting transfers between devices: 35.7 us -> 41.9 us
  between operations: 2.75 us -> 0.22 us
    ppermute x39, waiting for transfers between devices: 82.4 us -> 71.2 us  [hop(): lax.ppermute(value, axes, [(number[c], number[tuple(target(*c))]) for c i...]
    ppermute x39, starting transfers between devices: 28.5 us -> 36.9 us  [hop(): lax.ppermute(value, axes, [(number[c], number[tuple(target(*c))]) for c i...]
    pallas_call x13 -> x14, Pallas kernels: 29.7 us -> 21.9 us  [call(): pl.pallas_call(kernel, out_shape=outs, in_specs=[SMEM] * smem_count + [VM...]
    all_to_all x1, starting transfers between devices: 7.27 us -> 4.93 us  [per_device(): w_cols = lax.all_to_all(after(w_parts, own, from_y, from_x), HEAD, 0, 0)]
  transfers between devices with their start and end apart: 40 -> 40, of which waited for: 26 -> 27; matrix products, arithmetic and copies ran while one was open for 1% -> 0% of each run, Pallas kernels for 13% -> 13%
where the time goes in v2:
time: 144 us
  waiting for transfers between devices  71.2 us (49%)
  starting transfers between devices  41.9 us (29%)
  Pallas kernels  21.9 us (15%)
  local copies, waits for them, and re-layouts  8.43 us (6%)
    ppermute x39, waiting for transfers between devices, hop(): lax.ppermute(value, axes, [(number[c], number[tuple(target(*c))]) for c i...  71.2 us
    ppermute x39, starting transfers between devices, hop(): lax.ppermute(value, axes, [(number[c], number[tuple(target(*c))]) for c i...  36.9 us
    pallas_call x14, Pallas kernels, call(): pl.pallas_call(kernel, out_shape=outs, in_specs=[SMEM] * smem_count + [VM...  21.9 us
    unnamed x22, local copies, waits for them, and re-layouts  8.43 us
    all_to_all x1, starting transfers between devices, per_device(): w_cols = lax.all_to_all(after(w_parts, own, from_y, from_x), HEAD, 0, 0)  4.93 us
  transfers between devices with their start and end apart: 40, of which 27 were waited for; matrix products, arithmetic and copies ran while one was open for 0% of the time, Pallas kernels for 13%

profile of v2, /device:TPU:16, one launch (start us, length us, event | category | flops | bytes accessed | tf_op | source)
XLA Modules:
  0.0 143.6 jit_solution(4416508415133295344)
XLA Ops:
  5.3 3.6 %collective-permute-done.1.refs_3_ = bf16[1024,128]{1,0:T(8,128)(2,1)S(1)} collective-permute-done((bf16[1024,128]{1,0:T(8,128)(2,1)}, bf16[1024,128]{1,0:T(8,128)(2,1)S(1)}, u32[]{:S(2)}, u32[]{:S(2)}) %collective-permute-start.1) | collective-permute-done | bytes 262176 | tf_op jit(solution)/shard_map/ppermute | solution.py:28
  12.8 2.0 %collective-permute-done.4.refs_6_ = bf16[1024,128]{1,0:T(8,128)(2,1)S(1)} collective-permute-done((bf16[1024,128]{1,0:T(8,128)(2,1)S(1)}, bf16[1024,128]{1,0:T(8,128)(2,1)S(1)}, u32[]{:S(2)}, u32[]{:S(2)}) %collective-permute-start.4) | collective-permute-done | bytes 262176 | tf_op jit(solution)/shard_map/ppermute | solution.py:28
  14.8 4.4 %collective-permute-done.6.refs_5_ = bf16[1024,128]{1,0:T(8,128)(2,1)S(1)} collective-permute-done((bf16[1024,128]{1,0:T(8,128)(2,1)S(1)}, bf16[1024,128]{1,0:T(8,128)(2,1)S(1)}, u32[]{:S(2)}, u32[]{:S(2)}) %collective-permute-start.6) | collective-permute-done | bytes 262176 | tf_op jit(solution)/shard_map/ppermute | solution.py:28
  22.0 2.8 %collective-permute-done.5.refs_6_ = bf16[1024,128]{1,0:T(8,128)(2,1)S(1)} collective-permute-done((bf16[1024,128]{1,0:T(8,128)(2,1)S(1)}, bf16[1024,128]{1,0:T(8,128)(2,1)S(1)}, u32[]{:S(2)}, u32[]{:S(2)}) %collective-permute-start.5) | collective-permute-done | bytes 262176 | tf_op jit(solution)/shard_map/ppermute | solution.py:28
  24.8 2.8 %collective-permute-done.7.refs_4_ = bf16[1024,128]{1,0:T(8,128)(2,1)S(1)} collective-permute-done((bf16[1024,128]{1,0:T(8,128)(2,1)S(1)}, bf16[1024,128]{1,0:T(8,128)(2,1)S(1)}, u32[]{:S(2)}, u32[]{:S(2)}) %collective-permute-start.7) | collective-permute-done | bytes 262176 | tf_op jit(solution)/shard_map/ppermute | solution.py:28
  27.8 2.5 %collective-permute-done.9.refs_5_ = bf16[1024,128]{1,0:T(8,128)(2,1)S(1)} collective-permute-done((bf16[1024,128]{1,0:T(8,128)(2,1)S(1)}, bf16[1024,128]{1,0:T(8,128)(2,1)S(1)}, u32[]{:S(2)}, u32[]{:S(2)}) %collective-permute-start.9) | collective-permute-done | bytes 262176 | tf_op jit(solution)/shard_map/ppermute | solution.py:28
  39.5 5.2 %collective-permute-done.14.refs_4_ = bf16[1024,128]{1,0:T(8,128)(2,1)S(1)} collective-permute-done((bf16[1024,128]{1,0:T(8,128)(2,1)S(1)}, bf16[1024,128]{1,0:T(8,128)(2,1)S(1)}, u32[]{:S(2)}, u32[]{:S(2)}) %collective-permute-start.14) | collective-permute-done | bytes 262176 | tf_op jit(solution)/shard_map/ppermute | solution.py:28
  45.4 7.6 %collective-permute-done.16.refs_8_ = bf16[1024,128]{1,0:T(8,128)(2,1)S(1)} collective-permute-done((bf16[1024,128]{1,0:T(8,128)(2,1)S(1)}, bf16[1024,128]{1,0:T(8,128)(2,1)S(1)}, u32[]{:S(2)}, u32[]{:S(2)}) %collective-permute-start.16) | collective-permute-done | bytes 262176 | tf_op jit(solution)/shard_map/ppermute | solution.py:28
  55.5 3.0 %collective-permute-start.19 = (bf16[1024,256]{1,0:T(8,128)(2,1)S(1)}, bf16[1024,256]{1,0:T(8,128)(2,1)S(1)}, u32[]{:S(2)}, u32[]{:S(2)}) collective-permute-start(bf16[1024,256]{1,0:T(8,128)(2,1)S(1)} %get-tuple-element.58.refs_1_), channel_id=1, source_target_pairs={{0,32},{32,0},{1,33},{33,1},{2,34},{34,2},{3,35},{35,3},{4,36},{36... | collective-permute-start | bytes 1572872 | tf_op jit(solution)/shard_map/ppermute | solution.py:28
  60.1 4.9 %attend_own.1 = (f32[1024,256]{1,0:T(8,128)S(1)}, f32[1024,256]{1,0:T(8,128)S(1)}) custom-call(s32[2]{0:T(128)S(1)} %copy-done.4, bf16[1024,256]{1,0:T(8,128)(2,1)S(1)} %get-tuple-element.58.refs_1_, bf16[1024,128]{1,0:T(8,128)(2,1)S(1)} %get-tuple-element.59.refs_2_.refs_3_, bf16[1024,128]{1,0:T(8,128)(2,1)S(1)} %collective-permute-done.17.refs_3_.refs_5_.refs_2_), custom_call_target="tpu_custom_call" | custom-call | flops 2147483648 | bytes 3145736 | tf_op jit(solution)/shard_map/attend_own/pallas_call | solution.py:46
  67.0 4.8 %collective-permute-done.19.refs_2_ = bf16[1024,256]{1,0:T(8,128)(2,1)S(1)} collective-permute-done((bf16[1024,256]{1,0:T(8,128)(2,1)S(1)}, bf16[1024,256]{1,0:T(8,128)(2,1)S(1)}, u32[]{:S(2)}, u32[]{:S(2)}) %collective-permute-start.19) | collective-permute-done | bytes 524320 | tf_op jit(solution)/shard_map/ppermute | solution.py:28
  71.9 4.9 %all-to-all-start = ((bf16[16,128,128]{2,1,0:T(8,128)(2,1)}), bf16[16,128,128]{2,1,0:T(8,128)(2,1)S(1)}, u32[]{:S(2)}, u32[]{:S(2)}) async-start(bf16[16,128,128]{2,1,0:T(8,128)(2,1)} %column_parts.1), calls=%async_computation | async-start | bytes 1048576 | tf_op jit(solution)/shard_map/all_to_all | solution.py:282
  79.3 6.0 %attend_near.1 = (f32[1024,256]{1,0:T(8,128)S(1)}, f32[1024,256]{1,0:T(8,128)S(1)}) custom-call(s32[2]{0:T(128)S(1)} %copy-done.4, bf16[1024,256]{1,0:T(8,128)(2,1)S(1)} %collective-permute-done.18.refs_1_, bf16[1024,256]{1,0:T(8,128)(2,1)S(1)} %collective-permute-done.19.refs_2_, bf16[1024,128]{1,0:T(8,128)(2,1)S(1)} %get-tuple-element.59.refs_2_.refs_3_, ...), custom_call_target="tpu_custom_call" | custom-call | flops 4294967296 | bytes 5767176 | tf_op jit(solution)/shard_map/attend_near/pallas_call | solution.py:46
  86.3 2.2 %attend_far_other.1 = bf16[1024,256]{1,0:T(8,128)(2,1)S(1)} custom-call(s32[2]{0:T(128)S(1)} %copy-done.4, bf16[1024,256]{1,0:T(8,128)(2,1)S(1)} %collective-permute-done.20.refs_1_, bf16[1024,128]{1,0:T(8,128)(2,1)S(1)} %copy-done.6, f32[1024,256]{1,0:T(8,128)S(1)} %get-tuple-element.65.refs_3_), custom_call_target="tpu_custom_call" | custom-call | flops 1073741824 | bytes 2359304 | tf_op jit(solution)/shard_map/attend_far_other/pallas_call | solution.py:46
  88.6 2.2 %attend_far_own.1.a_ref = f32[1024,256]{1,0:T(8,128)S(1)} custom-call(s32[2]{0:T(128)S(1)} %copy-done.4, bf16[1024,256]{1,0:T(8,128)(2,1)S(1)} %collective-permute-done.20.refs_1_, bf16[1024,128]{1,0:T(8,128)(2,1)S(1)} %get-tuple-element.59.refs_2_.refs_3_, f32[1024,256]{1,0:T(8,128)S(1)} %get-tuple-element.63.refs_3_), custom_call_target="tpu_custom_call" | custom-call | flops 1073741824 | bytes 2883592 | tf_op jit(solution)/shard_map/attend_far_own/pallas_call | solution.py:46
  97.0 3.6 %collective-permute-done.23.refs_2_ = bf16[1024,128]{1,0:T(8,128)(2,1)S(1)} collective-permute-done((bf16[1024,128]{1,0:T(8,128)(2,1)S(1)}, bf16[1024,128]{1,0:T(8,128)(2,1)S(1)}, u32[]{:S(2)}, u32[]{:S(2)}) %collective-permute-start.23) | collective-permute-done | bytes 262176 | tf_op jit(solution)/shard_map/ppermute | solution.py:28
  105.3 2.9 %collective-permute-done.28.refs_4_ = bf16[1024,128]{1,0:T(8,128)(2,1)S(1)} collective-permute-done((bf16[1024,128]{1,0:T(8,128)(2,1)S(1)}, bf16[1024,128]{1,0:T(8,128)(2,1)S(1)}, u32[]{:S(2)}, u32[]{:S(2)}) %collective-permute-start.28) | collective-permute-done | bytes 262176 | tf_op jit(solution)/shard_map/ppermute | solution.py:28
  108.7 2.3 %collective-permute-done.24.refs_2_ = bf16[1024,128]{1,0:T(8,128)(2,1)S(1)} collective-permute-done((bf16[1024,128]{1,0:T(8,128)(2,1)S(1)}, bf16[1024,128]{1,0:T(8,128)(2,1)S(1)}, u32[]{:S(2)}, u32[]{:S(2)}) %collective-permute-start.24) | collective-permute-done | bytes 262176 | tf_op jit(solution)/shard_map/ppermute | solution.py:28
  114.5 2.2 %collective-permute-done.29.refs_3_ = bf16[1024,128]{1,0:T(8,128)(2,1)S(1)} collective-permute-done((bf16[1024,128]{1,0:T(8,128)(2,1)S(1)}, bf16[1024,128]{1,0:T(8,128)(2,1)S(1)}, u32[]{:S(2)}, u32[]{:S(2)}) %collective-permute-start.29) | collective-permute-done | bytes 262176 | tf_op jit(solution)/shard_map/ppermute | solution.py:28
  116.6 2.8 %collective-permute-done.31.refs_3_ = bf16[1024,128]{1,0:T(8,128)(2,1)S(1)} collective-permute-done((bf16[1024,128]{1,0:T(8,128)(2,1)S(1)}, bf16[1024,128]{1,0:T(8,128)(2,1)S(1)}, u32[]{:S(2)}, u32[]{:S(2)}) %collective-permute-start.31) | collective-permute-done | bytes 262176 | tf_op jit(solution)/shard_map/ppermute | solution.py:28
  124.6 2.5 %collective-permute-done.35.refs_5_ = bf16[1024,128]{1,0:T(8,128)(2,1)S(1)} collective-permute-done((bf16[1024,128]{1,0:T(8,128)(2,1)S(1)}, bf16[1024,128]{1,0:T(8,128)(2,1)S(1)}, u32[]{:S(2)}, u32[]{:S(2)}) %collective-permute-start.35) | collective-permute-done | bytes 262176 | tf_op jit(solution)/shard_map/ppermute | solution.py:28
  127.0 2.8 %collective-permute-done.33.refs_4_ = bf16[1024,128]{1,0:T(8,128)(2,1)S(1)} collective-permute-done((bf16[1024,128]{1,0:T(8,128)(2,1)S(1)}, bf16[1024,128]{1,0:T(8,128)(2,1)S(1)}, u32[]{:S(2)}, u32[]{:S(2)}) %collective-permute-start.33) | collective-permute-done | bytes 262176 | tf_op jit(solution)/shard_map/ppermute | solution.py:28
  131.1 3.2 %collective-permute-done.36.refs_3_ = bf16[1024,128]{1,0:T(8,128)(2,1)S(1)} collective-permute-done((bf16[1024,128]{1,0:T(8,128)(2,1)S(1)}, bf16[1024,128]{1,0:T(8,128)(2,1)S(1)}, u32[]{:S(2)}, u32[]{:S(2)}) %collective-permute-start.36) | collective-permute-done | bytes 262176 | tf_op jit(solution)/shard_map/ppermute | solution.py:28
  136.3 6.1 %collective-permute-done.38.refs_6_ = bf16[1024,128]{1,0:T(8,128)(2,1)S(1)} collective-permute-done((bf16[1024,128]{1,0:T(8,128)(2,1)S(1)}, bf16[1024,128]{1,0:T(8,128)(2,1)S(1)}, u32[]{:S(2)}, u32[]{:S(2)}) %collective-permute-start.38) | collective-permute-done | bytes 262176 | tf_op jit(solution)/shard_map/ppermute | solution.py:28
  (92 shorter events, 55.9 us)
Async XLA Ops:
  0.0 8.9 %collective-permute-start.1 = (bf16[1024,128]{1,0:T(8,128)(2,1)}, bf16[1024,128]{1,0:T(8,128)(2,1)S(1)}, u32[]{:S(2)}, u32[]{:S(2)}) collective-permute-start(bf16[1024,128]{1,0:T(8,128)(2,1)} %refs_2_.1), channel_id=1, source_target_pairs={{0,8},{8,0},{1,9},{9,1},{2,10},{10,2},{3,11},{11,3},{4,12},{12,4},... | collective-permute-start | bytes 786440 | tf_op jit(solution)/shard_map/ppermute | solution.py:28
  1.5 10.4 %collective-permute-start = (bf16[1024,128]{1,0:T(8,128)(2,1)}, bf16[1024,128]{1,0:T(8,128)(2,1)S(1)}, u32[]{:S(2)}, u32[]{:S(2)}) collective-permute-start(bf16[1024,128]{1,0:T(8,128)(2,1)} %refs_2_.1), channel_id=1, source_target_pairs={{0,1},{1,2},{2,3},{3,4},{4,5},{5,6},{6,7},{7,0},{16,23},{17,16},{1... | collective-permute-start | bytes 786440 | tf_op jit(solution)/shard_map/ppermute | solution.py:28
  3.4 11.3 %collective-permute-start.4 = (bf16[1024,128]{1,0:T(8,128)(2,1)S(1)}, bf16[1024,128]{1,0:T(8,128)(2,1)S(1)}, u32[]{:S(2)}, u32[]{:S(2)}) collective-permute-start(bf16[1024,128]{1,0:T(8,128)(2,1)S(1)} %collective-permute-done.3), channel_id=1, source_target_pairs={{0,1},{1,2},{2,3},{3,4},{4,5},{5,6},{6,7},{7,0},{16,23},{17,16},{1... | collective-permute-start | bytes 786440 | tf_op jit(solution)/shard_map/ppermute | solution.py:28
  8.9 10.2 %collective-permute-start.6 = (bf16[1024,128]{1,0:T(8,128)(2,1)S(1)}, bf16[1024,128]{1,0:T(8,128)(2,1)S(1)}, u32[]{:S(2)}, u32[]{:S(2)}) collective-permute-start(bf16[1024,128]{1,0:T(8,128)(2,1)S(1)} %collective-permute-done.1.refs_3_), channel_id=1, source_target_pairs={{0,1},{1,2},{2,3},{3,4},{4,5},{5,6},{6,7},{7,0},{16,23},{17,16},{1... | collective-permute-start | bytes 786440 | tf_op jit(solution)/shard_map/ppermute | solution.py:28
  11.9 10.0 %collective-permute-start.2 = (bf16[1024,128]{1,0:T(8,128)(2,1)S(1)}, bf16[1024,128]{1,0:T(8,128)(2,1)S(1)}, u32[]{:S(2)}, u32[]{:S(2)}) collective-permute-start(bf16[1024,128]{1,0:T(8,128)(2,1)S(1)} %collective-permute-done.refs_4_), channel_id=1, source_target_pairs={{0,1},{1,2},{2,3},{3,4},{4,5},{5,6},{6,7},{7,0},{16,23},{17,16},{1... | collective-permute-start | bytes 786440 | tf_op jit(solution)/shard_map/ppermute | solution.py:28
  14.8 10.0 %collective-permute-start.5 = (bf16[1024,128]{1,0:T(8,128)(2,1)S(1)}, bf16[1024,128]{1,0:T(8,128)(2,1)S(1)}, u32[]{:S(2)}, u32[]{:S(2)}) collective-permute-start(bf16[1024,128]{1,0:T(8,128)(2,1)S(1)} %collective-permute-done.4.refs_6_), channel_id=1, source_target_pairs={{0,1},{1,2},{2,3},{3,4},{4,5},{5,6},{6,7},{7,0},{16,23},{17,16},{1... | collective-permute-start | bytes 786440 | tf_op jit(solution)/shard_map/ppermute | solution.py:28
  19.1 8.7 %collective-permute-start.8 = (bf16[1024,128]{1,0:T(8,128)(2,1)S(1)}, bf16[1024,128]{1,0:T(8,128)(2,1)S(1)}, u32[]{:S(2)}, u32[]{:S(2)}) collective-permute-start(bf16[1024,128]{1,0:T(8,128)(2,1)S(1)} %collective-permute-done.4.refs_6_), channel_id=1, source_target_pairs={{0,8},{8,0},{1,9},{9,1},{2,10},{10,2},{3,11},{11,3},{4,12},{12,4},... | collective-permute-start | bytes 786440 | tf_op jit(solution)/shard_map/ppermute | solution.py:28
  21.9 8.4 %collective-permute-start.9 = (bf16[1024,128]{1,0:T(8,128)(2,1)S(1)}, bf16[1024,128]{1,0:T(8,128)(2,1)S(1)}, u32[]{:S(2)}, u32[]{:S(2)}) collective-permute-start(bf16[1024,128]{1,0:T(8,128)(2,1)S(1)} %collective-permute-done.2.refs_3_), channel_id=1, source_target_pairs={{0,1},{1,2},{2,3},{3,4},{4,5},{5,6},{6,7},{7,0},{16,23},{17,16},{1... | collective-permute-start | bytes 786440 | tf_op jit(solution)/shard_map/ppermute | solution.py:28
  27.8 10.5 %collective-permute-start.11 = (bf16[1024,128]{1,0:T(8,128)(2,1)S(1)}, bf16[1024,128]{1,0:T(8,128)(2,1)S(1)}, u32[]{:S(2)}, u32[]{:S(2)}) collective-permute-start(bf16[1024,128]{1,0:T(8,128)(2,1)S(1)} %collective-permute-done.7.refs_4_), channel_id=1, source_target_pairs={{0,1},{1,2},{2,3},{3,4},{4,5},{5,6},{6,7},{7,0},{16,23},{17,16},{1... | collective-permute-start | bytes 786440 | tf_op jit(solution)/shard_map/ppermute | solution.py:28
  30.4 8.7 %collective-permute-start.12 = (bf16[1024,128]{1,0:T(8,128)(2,1)S(1)}, bf16[1024,128]{1,0:T(8,128)(2,1)S(1)}, u32[]{:S(2)}, u32[]{:S(2)}) collective-permute-start(bf16[1024,128]{1,0:T(8,128)(2,1)S(1)} %collective-permute-done.5.refs_6_), channel_id=1, source_target_pairs={{0,8},{8,0},{1,9},{9,1},{2,10},{10,2},{3,11},{11,3},{4,12},{12,4},... | collective-permute-start | bytes 786440 | tf_op jit(solution)/shard_map/ppermute | solution.py:28
  33.2 11.5 %collective-permute-start.14 = (bf16[1024,128]{1,0:T(8,128)(2,1)S(1)}, bf16[1024,128]{1,0:T(8,128)(2,1)S(1)}, u32[]{:S(2)}, u32[]{:S(2)}) collective-permute-start(bf16[1024,128]{1,0:T(8,128)(2,1)S(1)} %collective-permute-done.10.refs_3_), channel_id=1, source_target_pairs={{0,8},{8,0},{1,9},{9,1},{2,10},{10,2},{3,11},{11,3},{4,12},{12,4},... | collective-permute-start | bytes 786440 | tf_op jit(solution)/shard_map/ppermute | solution.py:28
  54.1 12.9 %collective-permute-start.18 = (bf16[1024,256]{1,0:T(8,128)(2,1)S(1)}, bf16[1024,256]{1,0:T(8,128)(2,1)S(1)}, u32[]{:S(2)}, u32[]{:S(2)}) collective-permute-start(bf16[1024,256]{1,0:T(8,128)(2,1)S(1)} %get-tuple-element.58.refs_1_), channel_id=1, source_target_pairs={{0,64},{64,0},{1,65},{65,1},{2,66},{66,2},{3,67},{67,3},{4,68},{68... | collective-permute-start | bytes 1572872 | tf_op jit(solution)/shard_map/ppermute | solution.py:28
  55.5 16.4 %collective-permute-start.19 = (bf16[1024,256]{1,0:T(8,128)(2,1)S(1)}, bf16[1024,256]{1,0:T(8,128)(2,1)S(1)}, u32[]{:S(2)}, u32[]{:S(2)}) collective-permute-start(bf16[1024,256]{1,0:T(8,128)(2,1)S(1)} %get-tuple-element.58.refs_1_), channel_id=1, source_target_pairs={{0,32},{32,0},{1,33},{33,1},{2,34},{34,2},{3,35},{35,3},{4,36},{36... | collective-permute-start | bytes 1572872 | tf_op jit(solution)/shard_map/ppermute | solution.py:28
  59.4 25.9 %collective-permute-start.20 = (bf16[1024,256]{1,0:T(8,128)(2,1)S(1)}, bf16[1024,256]{1,0:T(8,128)(2,1)S(1)}, u32[]{:S(2)}, u32[]{:S(2)}) collective-permute-start(bf16[1024,256]{1,0:T(8,128)(2,1)S(1)} %get-tuple-element.58.refs_1_), channel_id=1, source_target_pairs={{0,96},{32,64},{64,32},{96,0},{1,97},{33,65},{65,33},{97,1},{2,98}... | collective-permute-start | bytes 1572872 | tf_op jit(solution)/shard_map/ppermute | solution.py:28
  71.9 18.9 %all-to-all-start = ((bf16[16,128,128]{2,1,0:T(8,128)(2,1)}), bf16[16,128,128]{2,1,0:T(8,128)(2,1)S(1)}, u32[]{:S(2)}, u32[]{:S(2)}) async-start(bf16[16,128,128]{2,1,0:T(8,128)(2,1)} %column_parts.1), calls=%async_computation | async-start | bytes 1048576 | tf_op jit(solution)/shard_map/all_to_all | solution.py:282
  92.1 8.5 %collective-permute-start.23 = (bf16[1024,128]{1,0:T(8,128)(2,1)S(1)}, bf16[1024,128]{1,0:T(8,128)(2,1)S(1)}, u32[]{:S(2)}, u32[]{:S(2)}) collective-permute-start(bf16[1024,128]{1,0:T(8,128)(2,1)S(1)} %combine.1.refs_1_), channel_id=1, source_target_pairs={{0,8},{8,0},{1,9},{9,1},{2,10},{10,2},{3,11},{11,3},{4,12},{12,4},... | collective-permute-start | bytes 786440 | tf_op jit(solution)/shard_map/ppermute | solution.py:28
  95.5 8.9 %collective-permute-start.26 = (bf16[1024,128]{1,0:T(8,128)(2,1)S(1)}, bf16[1024,128]{1,0:T(8,128)(2,1)S(1)}, u32[]{:S(2)}, u32[]{:S(2)}) collective-permute-start(bf16[1024,128]{1,0:T(8,128)(2,1)S(1)} %collective-permute-done.25), channel_id=1, source_target_pairs={{0,1},{1,2},{2,3},{3,4},{4,5},{5,6},{6,7},{7,0},{16,23},{17,16},{1... | collective-permute-start | bytes 786440 | tf_op jit(solution)/shard_map/ppermute | solution.py:28
  102.4 8.7 %collective-permute-start.24 = (bf16[1024,128]{1,0:T(8,128)(2,1)S(1)}, bf16[1024,128]{1,0:T(8,128)(2,1)S(1)}, u32[]{:S(2)}, u32[]{:S(2)}) collective-permute-start(bf16[1024,128]{1,0:T(8,128)(2,1)S(1)} %collective-permute-done.22.refs_3_), channel_id=1, source_target_pairs={{0,1},{1,2},{2,3},{3,4},{4,5},{5,6},{6,7},{7,0},{16,23},{17,16},{1... | collective-permute-start | bytes 786440 | tf_op jit(solution)/shard_map/ppermute | solution.py:28
  104.5 9.4 %collective-permute-start.27 = (bf16[1024,128]{1,0:T(8,128)(2,1)S(1)}, bf16[1024,128]{1,0:T(8,128)(2,1)S(1)}, u32[]{:S(2)}, u32[]{:S(2)}) collective-permute-start(bf16[1024,128]{1,0:T(8,128)(2,1)S(1)} %collective-permute-done.26.refs_5_), channel_id=1, source_target_pairs={{0,1},{1,2},{2,3},{3,4},{4,5},{5,6},{6,7},{7,0},{16,23},{17,16},{1... | collective-permute-start | bytes 786440 | tf_op jit(solution)/shard_map/ppermute | solution.py:28
  111.6 8.5 %collective-permute-start.30 = (bf16[1024,128]{1,0:T(8,128)(2,1)S(1)}, bf16[1024,128]{1,0:T(8,128)(2,1)S(1)}, u32[]{:S(2)}, u32[]{:S(2)}) collective-permute-start(bf16[1024,128]{1,0:T(8,128)(2,1)S(1)} %collective-permute-done.26.refs_5_), channel_id=1, source_target_pairs={{0,8},{8,0},{1,9},{9,1},{2,10},{10,2},{3,11},{11,3},{4,12},{12,4},... | collective-permute-start | bytes 786440 | tf_op jit(solution)/shard_map/ppermute | solution.py:28
  113.8 9.1 %collective-permute-start.32 = (bf16[1024,128]{1,0:T(8,128)(2,1)S(1)}, bf16[1024,128]{1,0:T(8,128)(2,1)S(1)}, u32[]{:S(2)}, u32[]{:S(2)}) collective-permute-start(bf16[1024,128]{1,0:T(8,128)(2,1)S(1)} %collective-permute-done.27.refs_5_), channel_id=1, source_target_pairs={{0,1},{1,2},{2,3},{3,4},{4,5},{5,6},{6,7},{7,0},{16,23},{17,16},{1... | collective-permute-start | bytes 786440 | tf_op jit(solution)/shard_map/ppermute | solution.py:28
  120.0 9.8 %collective-permute-start.33 = (bf16[1024,128]{1,0:T(8,128)(2,1)S(1)}, bf16[1024,128]{1,0:T(8,128)(2,1)S(1)}, u32[]{:S(2)}, u32[]{:S(2)}) collective-permute-start(bf16[1024,128]{1,0:T(8,128)(2,1)S(1)} %collective-permute-done.29.refs_3_), channel_id=1, source_target_pairs={{0,1},{1,2},{2,3},{3,4},{4,5},{5,6},{6,7},{7,0},{16,23},{17,16},{1... | collective-permute-start | bytes 786440 | tf_op jit(solution)/shard_map/ppermute | solution.py:28
  121.5 9.2 %collective-permute-start.34 = (bf16[1024,128]{1,0:T(8,128)(2,1)S(1)}, bf16[1024,128]{1,0:T(8,128)(2,1)S(1)}, u32[]{:S(2)}, u32[]{:S(2)}) collective-permute-start(bf16[1024,128]{1,0:T(8,128)(2,1)S(1)} %collective-permute-done.27.refs_5_), channel_id=1, source_target_pairs={{0,8},{8,0},{1,9},{9,1},{2,10},{10,2},{3,11},{11,3},{4,12},{12,4},... | collective-permute-start | bytes 786440 | tf_op jit(solution)/shard_map/ppermute | solution.py:28
  122.9 11.4 %collective-permute-start.36 = (bf16[1024,128]{1,0:T(8,128)(2,1)S(1)}, bf16[1024,128]{1,0:T(8,128)(2,1)S(1)}, u32[]{:S(2)}, u32[]{:S(2)}) collective-permute-start(bf16[1024,128]{1,0:T(8,128)(2,1)S(1)} %collective-permute-done.32.refs_2_), channel_id=1, source_target_pairs={{0,8},{8,0},{1,9},{9,1},{2,10},{10,2},{3,11},{11,3},{4,12},{12,4},... | collective-permute-start | bytes 786440 | tf_op jit(solution)/shard_map/ppermute | solution.py:28
  (27 other events, 146.6 us)

commit v3 on v2

--- a/solution.py
+++ b/solution.py
@@ -227,25 +227,32 @@
         if s > 1:
             own_from = after(own_from, cross[s - 2])
             other_from = after(other_from, own[s - 1])
-            cross_from = after(cross_from, other[s - 1], *far[s - 2 : s - 1][: s - 2])
+            cross_from = after(cross_from, other[s - 1])
         own.append(z_step(own_from))
         other.append(z_step(other_from))
         cross.append(z_step(cross_from))
         far.append(swap(other[s], "xl"))
-    own.append(z_step(after(own[-1], cross[half - 2])))
-    cross.append(z_step(after(cross[-1], own[half - 1], far[half - 2])))
-
-    for s in range(1, half - 1):
-        mine.append((s, own[s], cross[s]))
-        mine[0] = (mine[0][0], after(mine[0][1], own[s + 1], other[s + 1], cross[s + 1]), mine[0][2])
-        total_own, total_other = contract(
-            weights, [[total_own, *mine], [total_other, (s, other[s], far[s])]], f"{name}_{s}"
-        )
-        mine = []
-    last_other = after(other[half - 1], own[half])
-    (total_other,) = contract(
-        weights, [[total_other, (half - 1, last_other, far[half - 1])]], f"{name}_{half - 1}"
-    )
+    own.append(z_step(after(own[-1], cross[half - 2], far[1])))
+    cross.append(z_step(after(cross[-1], own[half - 1], far[2])))
+
+    total_own, total_other = contract(
+        weights,
+        [
+            [None, *mine, (1, own[1], after(cross[1], own[3], other[3], cross[3]))],
+            [None, (1, other[1], far[1])],
+        ],
+        f"{name}_1",
+    )
+    last_other = after(other[3], own[4], cross[4], total_own)
+    total_own, total_other = contract(
+        weights,
+        [
+            [total_own, (2, own[2], cross[2])],
+            [total_other, (2, other[2], far[2]), (3, last_other, far[3])],
+        ],
+        f"{name}_2",
+    )
+    mine = []
     both = swap(total_other, "core")
     mine += [(s, own[s], cross[s]) for s in (half - 1, half)]
     return contract(

time: 144 us -> 144 us (level)
  waiting for transfers between devices: 71.2 us -> 65.2 us
  starting transfers between devices: 41.9 us -> 47.3 us
    ppermute x39, waiting for transfers between devices: 71.2 us -> 65.2 us  [hop(): lax.ppermute(value, axes, [(number[c], number[tuple(target(*c))]) for c i...]
    ppermute x39, starting transfers between devices: 36.9 us -> 40.4 us  [hop(): lax.ppermute(value, axes, [(number[c], number[tuple(target(*c))]) for c i...]
    all_to_all x1, starting transfers between devices: 4.93 us -> 6.88 us  [per_device(): w_cols = lax.all_to_all(after(w_parts, own, from_y, from_x), HEAD, 0, 0)]
    pallas_call x14 -> x12, Pallas kernels: 21.9 us -> 21.5 us  [call(): pl.pallas_call(kernel, out_shape=outs, in_specs=[SMEM] * smem_count + [VM...]
  transfers between devices with their start and end apart: 40 -> 40, of which waited for: 27 -> 29; matrix products, arithmetic and copies ran while one was open for 0% -> 0% of each run, Pallas kernels for 13% -> 12%
where the time goes in v3:
time: 144 us; the launch traced here: 143 us
  waiting for transfers between devices  65.2 us (45%)
  starting transfers between devices  47.3 us (33%)
  Pallas kernels  21.5 us (15%)
  local copies, waits for them, and re-layouts  8.43 us (6%)
    ppermute x39, waiting for transfers between devices, hop(): lax.ppermute(value, axes, [(number[c], number[tuple(target(*c))]) for c i...  65.2 us
    ppermute x39, starting transfers between devices, hop(): lax.ppermute(value, axes, [(number[c], number[tuple(target(*c))]) for c i...  40.4 us
    pallas_call x12, Pallas kernels, call(): pl.pallas_call(kernel, out_shape=outs, in_specs=[SMEM] * smem_count + [VM...  21.5 us
    unnamed x22, local copies, waits for them, and re-layouts  8.43 us
    all_to_all x1, starting transfers between devices, per_device(): w_cols = lax.all_to_all(after(w_parts, own, from_y, from_x), HEAD, 0, 0)  6.88 us
  transfers between devices with their start and end apart: 40, of which 29 were waited for; matrix products, arithmetic and copies ran while one was open for 0% of the time, Pallas kernels for 12%

profile of v3, /device:TPU:16, one launch (start us, length us, event | category | flops | bytes accessed | tf_op | source)
XLA Modules:
  0.0 142.6 jit_solution(17987582409680583491)
XLA Ops:
  3.4 4.8 %collective-permute-done.refs_3_ = bf16[1024,128]{1,0:T(8,128)(2,1)S(1)} collective-permute-done((bf16[1024,128]{1,0:T(8,128)(2,1)}, bf16[1024,128]{1,0:T(8,128)(2,1)S(1)}, u32[]{:S(2)}, u32[]{:S(2)}) %collective-permute-start) | collective-permute-done | bytes 262176 | tf_op jit(solution)/shard_map/ppermute | solution.py:28
  14.0 4.4 %collective-permute-done.2.refs_5_ = bf16[1024,128]{1,0:T(8,128)(2,1)S(1)} collective-permute-done((bf16[1024,128]{1,0:T(8,128)(2,1)S(1)}, bf16[1024,128]{1,0:T(8,128)(2,1)S(1)}, u32[]{:S(2)}, u32[]{:S(2)}) %collective-permute-start.2) | collective-permute-done | bytes 262176 | tf_op jit(solution)/shard_map/ppermute | solution.py:28
  18.5 2.8 %collective-permute-done.6.refs_6_ = bf16[1024,128]{1,0:T(8,128)(2,1)S(1)} collective-permute-done((bf16[1024,128]{1,0:T(8,128)(2,1)S(1)}, bf16[1024,128]{1,0:T(8,128)(2,1)S(1)}, u32[]{:S(2)}, u32[]{:S(2)}) %collective-permute-start.6) | collective-permute-done | bytes 262176 | tf_op jit(solution)/shard_map/ppermute | solution.py:28
  21.3 2.8 %collective-permute-done.3.refs_3_ = bf16[1024,128]{1,0:T(8,128)(2,1)S(1)} collective-permute-done((bf16[1024,128]{1,0:T(8,128)(2,1)S(1)}, bf16[1024,128]{1,0:T(8,128)(2,1)S(1)}, u32[]{:S(2)}, u32[]{:S(2)}) %collective-permute-start.3) | collective-permute-done | bytes 262176 | tf_op jit(solution)/shard_map/ppermute | solution.py:28
  25.6 3.3 %collective-permute-done.9.refs_4_ = bf16[1024,128]{1,0:T(8,128)(2,1)S(1)} collective-permute-done((bf16[1024,128]{1,0:T(8,128)(2,1)S(1)}, bf16[1024,128]{1,0:T(8,128)(2,1)S(1)}, u32[]{:S(2)}, u32[]{:S(2)}) %collective-permute-start.9) | collective-permute-done | bytes 262176 | tf_op jit(solution)/shard_map/ppermute | solution.py:28
  28.9 2.8 %collective-permute-done.7.refs_6_ = bf16[1024,128]{1,0:T(8,128)(2,1)S(1)} collective-permute-done((bf16[1024,128]{1,0:T(8,128)(2,1)S(1)}, bf16[1024,128]{1,0:T(8,128)(2,1)S(1)}, u32[]{:S(2)}, u32[]{:S(2)}) %collective-permute-start.7) | collective-permute-done | bytes 262176 | tf_op jit(solution)/shard_map/ppermute | solution.py:28
  35.7 3.5 %collective-permute-done.10.refs_6_ = bf16[1024,128]{1,0:T(8,128)(2,1)S(1)} collective-permute-done((bf16[1024,128]{1,0:T(8,128)(2,1)S(1)}, bf16[1024,128]{1,0:T(8,128)(2,1)S(1)}, u32[]{:S(2)}, u32[]{:S(2)}) %collective-permute-start.10) | collective-permute-done | bytes 262176 | tf_op jit(solution)/shard_map/ppermute | solution.py:28
  39.5 2.5 %collective-permute-done.8.refs_8_ = bf16[1024,128]{1,0:T(8,128)(2,1)S(1)} collective-permute-done((bf16[1024,128]{1,0:T(8,128)(2,1)S(1)}, bf16[1024,128]{1,0:T(8,128)(2,1)S(1)}, u32[]{:S(2)}, u32[]{:S(2)}) %collective-permute-start.8) | collective-permute-done | bytes 262176 | tf_op jit(solution)/shard_map/ppermute | solution.py:28
  49.3 2.6 %collective-permute-done.16.refs_3_ = f32[1024,256]{1,0:T(8,128)S(1)} collective-permute-done((f32[1024,256]{1,0:T(8,128)S(1)}, f32[1024,256]{1,0:T(8,128)S(1)}, u32[]{:S(2)}, u32[]{:S(2)}) %collective-permute-start.16) | collective-permute-done | bytes 1048608 | tf_op jit(solution)/shard_map/ppermute | solution.py:28
  54.4 3.0 %collective-permute-start.19 = (bf16[1024,256]{1,0:T(8,128)(2,1)S(1)}, bf16[1024,256]{1,0:T(8,128)(2,1)S(1)}, u32[]{:S(2)}, u32[]{:S(2)}) collective-permute-start(bf16[1024,256]{1,0:T(8,128)(2,1)S(1)} %get-tuple-element.55.refs_1_), channel_id=1, source_target_pairs={{0,32},{32,0},{1,33},{33,1},{2,34},{34,2},{3,35},{35,3},{4,36},{36... | collective-permute-start | bytes 1572872 | tf_op jit(solution)/shard_map/ppermute | solution.py:28
  59.1 4.9 %attend_own.1 = (f32[1024,256]{1,0:T(8,128)S(1)}, f32[1024,256]{1,0:T(8,128)S(1)}) custom-call(s32[2]{0:T(128)S(1)} %copy-done.4, bf16[1024,256]{1,0:T(8,128)(2,1)S(1)} %get-tuple-element.55.refs_1_, bf16[1024,128]{1,0:T(8,128)(2,1)S(1)} %get-tuple-element.56.refs_2_.refs_3_, bf16[1024,128]{1,0:T(8,128)(2,1)S(1)} %collective-permute-done.17.refs_3_.refs_5_.refs_2_), custom_call_target="tpu_custom_call" | custom-call | flops 2147483648 | bytes 3145736 | tf_op jit(solution)/shard_map/attend_own/pallas_call | solution.py:46
  67.1 3.6 %collective-permute-done.19.refs_2_ = bf16[1024,256]{1,0:T(8,128)(2,1)S(1)} collective-permute-done((bf16[1024,256]{1,0:T(8,128)(2,1)S(1)}, bf16[1024,256]{1,0:T(8,128)(2,1)S(1)}, u32[]{:S(2)}, u32[]{:S(2)}) %collective-permute-start.19) | collective-permute-done | bytes 524320 | tf_op jit(solution)/shard_map/ppermute | solution.py:28
  70.8 6.9 %all-to-all-start = ((bf16[16,128,128]{2,1,0:T(8,128)(2,1)}), bf16[16,128,128]{2,1,0:T(8,128)(2,1)S(1)}, u32[]{:S(2)}, u32[]{:S(2)}) async-start(bf16[16,128,128]{2,1,0:T(8,128)(2,1)} %column_parts.1), calls=%async_computation | async-start | bytes 1048576 | tf_op jit(solution)/shard_map/all_to_all | solution.py:289
  80.1 6.0 %attend_near.1 = (f32[1024,256]{1,0:T(8,128)S(1)}, f32[1024,256]{1,0:T(8,128)S(1)}) custom-call(s32[2]{0:T(128)S(1)} %copy-done.4, bf16[1024,256]{1,0:T(8,128)(2,1)S(1)} %collective-permute-done.18.refs_1_, bf16[1024,256]{1,0:T(8,128)(2,1)S(1)} %collective-permute-done.19.refs_2_, bf16[1024,128]{1,0:T(8,128)(2,1)S(1)} %get-tuple-element.56.refs_2_.refs_3_, ...), custom_call_target="tpu_custom_call" | custom-call | flops 4294967296 | bytes 5767176 | tf_op jit(solution)/shard_map/attend_near/pallas_call | solution.py:46
  87.1 2.2 %attend_far_other.1 = bf16[1024,256]{1,0:T(8,128)(2,1)S(1)} custom-call(s32[2]{0:T(128)S(1)} %copy-done.4, bf16[1024,256]{1,0:T(8,128)(2,1)S(1)} %collective-permute-done.20.refs_1_, bf16[1024,128]{1,0:T(8,128)(2,1)S(1)} %copy-done.6, f32[1024,256]{1,0:T(8,128)S(1)} %get-tuple-element.62.refs_3_), custom_call_target="tpu_custom_call" | custom-call | flops 1073741824 | bytes 2359304 | tf_op jit(solution)/shard_map/attend_far_other/pallas_call | solution.py:46
  89.4 2.2 %attend_far_own.1.a_ref = f32[1024,256]{1,0:T(8,128)S(1)} custom-call(s32[2]{0:T(128)S(1)} %copy-done.4, bf16[1024,256]{1,0:T(8,128)(2,1)S(1)} %collective-permute-done.20.refs_1_, bf16[1024,128]{1,0:T(8,128)(2,1)S(1)} %get-tuple-element.56.refs_2_.refs_3_, f32[1024,256]{1,0:T(8,128)S(1)} %get-tuple-element.60.refs_3_), custom_call_target="tpu_custom_call" | custom-call | flops 1073741824 | bytes 2883592 | tf_op jit(solution)/shard_map/attend_far_own/pallas_call | solution.py:46
  96.1 5.3 %collective-permute-done.22.refs_2_ = bf16[1024,128]{1,0:T(8,128)(2,1)S(1)} collective-permute-done((bf16[1024,128]{1,0:T(8,128)(2,1)S(1)}, bf16[1024,128]{1,0:T(8,128)(2,1)S(1)}, u32[]{:S(2)}, u32[]{:S(2)}) %collective-permute-start.22) | collective-permute-done | bytes 262176 | tf_op jit(solution)/shard_map/ppermute | solution.py:28
  106.1 2.9 %collective-permute-done.24.refs_4_ = bf16[1024,128]{1,0:T(8,128)(2,1)S(1)} collective-permute-done((bf16[1024,128]{1,0:T(8,128)(2,1)S(1)}, bf16[1024,128]{1,0:T(8,128)(2,1)S(1)}, u32[]{:S(2)}, u32[]{:S(2)}) %collective-permute-start.24) | collective-permute-done | bytes 262176 | tf_op jit(solution)/shard_map/ppermute | solution.py:28
  109.0 2.8 %collective-permute-done.28.refs_5_ = bf16[1024,128]{1,0:T(8,128)(2,1)S(1)} collective-permute-done((bf16[1024,128]{1,0:T(8,128)(2,1)S(1)}, bf16[1024,128]{1,0:T(8,128)(2,1)S(1)}, u32[]{:S(2)}, u32[]{:S(2)}) %collective-permute-start.28) | collective-permute-done | bytes 262176 | tf_op jit(solution)/shard_map/ppermute | solution.py:28
  116.9 2.4 %collective-permute-done.31.refs_3_ = bf16[1024,128]{1,0:T(8,128)(2,1)S(1)} collective-permute-done((bf16[1024,128]{1,0:T(8,128)(2,1)S(1)}, bf16[1024,128]{1,0:T(8,128)(2,1)S(1)}, u32[]{:S(2)}, u32[]{:S(2)}) %collective-permute-start.31) | collective-permute-done | bytes 262176 | tf_op jit(solution)/shard_map/ppermute | solution.py:28
  119.4 2.8 %collective-permute-done.29.refs_5_ = bf16[1024,128]{1,0:T(8,128)(2,1)S(1)} collective-permute-done((bf16[1024,128]{1,0:T(8,128)(2,1)S(1)}, bf16[1024,128]{1,0:T(8,128)(2,1)S(1)}, u32[]{:S(2)}, u32[]{:S(2)}) %collective-permute-start.29) | collective-permute-done | bytes 262176 | tf_op jit(solution)/shard_map/ppermute | solution.py:28
  125.0 2.6 %collective-permute-start.35 = (bf16[1024,128]{1,0:T(8,128)(2,1)S(1)}, bf16[1024,128]{1,0:T(8,128)(2,1)S(1)}, u32[]{:S(2)}, u32[]{:S(2)}) collective-permute-start(bf16[1024,128]{1,0:T(8,128)(2,1)S(1)} %collective-permute-done.26.refs_3_), channel_id=1, source_target_pairs={{0,1},{1,2},{2,3},{3,4},{4,5},{5,6},{6,7},{7,0},{16,23},{17,16},{1... | collective-permute-start | bytes 786440 | tf_op jit(solution)/shard_map/ppermute | solution.py:28
  127.5 2.2 %collective-permute-done.32.refs_4_ = bf16[1024,128]{1,0:T(8,128)(2,1)S(1)} collective-permute-done((bf16[1024,128]{1,0:T(8,128)(2,1)S(1)}, bf16[1024,128]{1,0:T(8,128)(2,1)S(1)}, u32[]{:S(2)}, u32[]{:S(2)}) %collective-permute-start.32) | collective-permute-done | bytes 262176 | tf_op jit(solution)/shard_map/ppermute | solution.py:28
  135.4 2.8 %collective-permute-done.36.refs_6_ = bf16[1024,128]{1,0:T(8,128)(2,1)S(1)} collective-permute-done((bf16[1024,128]{1,0:T(8,128)(2,1)S(1)}, bf16[1024,128]{1,0:T(8,128)(2,1)S(1)}, u32[]{:S(2)}, u32[]{:S(2)}) %collective-permute-start.36) | collective-permute-done | bytes 262176 | tf_op jit(solution)/shard_map/ppermute | solution.py:28
  (90 shorter events, 60.0 us)
Async XLA Ops:
  1.5 8.7 %collective-permute-start.5 = (bf16[1024,128]{1,0:T(8,128)(2,1)}, bf16[1024,128]{1,0:T(8,128)(2,1)S(1)}, u32[]{:S(2)}, u32[]{:S(2)}) collective-permute-start(bf16[1024,128]{1,0:T(8,128)(2,1)} %refs_2_.2), channel_id=1, source_target_pairs={{0,16},{16,0},{1,17},{17,1},{2,18},{18,2},{3,19},{19,3},{4,20},{20... | collective-permute-start | bytes 786440 | tf_op jit(solution)/shard_map/ppermute | solution.py:28
  1.5 10.6 %collective-permute-start.1 = (bf16[1024,128]{1,0:T(8,128)(2,1)}, bf16[1024,128]{1,0:T(8,128)(2,1)S(1)}, u32[]{:S(2)}, u32[]{:S(2)}) collective-permute-start(bf16[1024,128]{1,0:T(8,128)(2,1)} %refs_2_.2), channel_id=1, source_target_pairs={{0,1},{1,2},{2,3},{3,4},{4,5},{5,6},{6,7},{7,0},{16,23},{17,16},{1... | collective-permute-start | bytes 786440 | tf_op jit(solution)/shard_map/ppermute | solution.py:28
  8.3 10.2 %collective-permute-start.2 = (bf16[1024,128]{1,0:T(8,128)(2,1)S(1)}, bf16[1024,128]{1,0:T(8,128)(2,1)S(1)}, u32[]{:S(2)}, u32[]{:S(2)}) collective-permute-start(bf16[1024,128]{1,0:T(8,128)(2,1)S(1)} %collective-permute-done.refs_3_), channel_id=1, source_target_pairs={{0,1},{1,2},{2,3},{3,4},{4,5},{5,6},{6,7},{7,0},{16,23},{17,16},{1... | collective-permute-start | bytes 786440 | tf_op jit(solution)/shard_map/ppermute | solution.py:28
  10.2 11.1 %collective-permute-start.6 = (bf16[1024,128]{1,0:T(8,128)(2,1)S(1)}, bf16[1024,128]{1,0:T(8,128)(2,1)S(1)}, u32[]{:S(2)}, u32[]{:S(2)}) collective-permute-start(bf16[1024,128]{1,0:T(8,128)(2,1)S(1)} %collective-permute-done.5), channel_id=1, source_target_pairs={{0,1},{1,2},{2,3},{3,4},{4,5},{5,6},{6,7},{7,0},{16,23},{17,16},{1... | collective-permute-start | bytes 786440 | tf_op jit(solution)/shard_map/ppermute | solution.py:28
  12.1 12.0 %collective-permute-start.3 = (bf16[1024,128]{1,0:T(8,128)(2,1)S(1)}, bf16[1024,128]{1,0:T(8,128)(2,1)S(1)}, u32[]{:S(2)}, u32[]{:S(2)}) collective-permute-start(bf16[1024,128]{1,0:T(8,128)(2,1)S(1)} %collective-permute-done.1.refs_4_), channel_id=1, source_target_pairs={{0,1},{1,2},{2,3},{3,4},{4,5},{5,6},{6,7},{7,0},{16,23},{17,16},{1... | collective-permute-start | bytes 786440 | tf_op jit(solution)/shard_map/ppermute | solution.py:28
  21.3 10.4 %collective-permute-start.7 = (bf16[1024,128]{1,0:T(8,128)(2,1)S(1)}, bf16[1024,128]{1,0:T(8,128)(2,1)S(1)}, u32[]{:S(2)}, u32[]{:S(2)}) collective-permute-start(bf16[1024,128]{1,0:T(8,128)(2,1)S(1)} %collective-permute-done.6.refs_6_), channel_id=1, source_target_pairs={{0,1},{1,2},{2,3},{3,4},{4,5},{5,6},{6,7},{7,0},{16,23},{17,16},{1... | collective-permute-start | bytes 786440 | tf_op jit(solution)/shard_map/ppermute | solution.py:28
  24.1 10.4 %collective-permute-start.4 = (bf16[1024,128]{1,0:T(8,128)(2,1)S(1)}, bf16[1024,128]{1,0:T(8,128)(2,1)S(1)}, u32[]{:S(2)}, u32[]{:S(2)}) collective-permute-start(bf16[1024,128]{1,0:T(8,128)(2,1)S(1)} %collective-permute-done.3.refs_3_), channel_id=1, source_target_pairs={{0,1},{1,2},{2,3},{3,4},{4,5},{5,6},{6,7},{7,0},{16,23},{17,16},{1... | collective-permute-start | bytes 786440 | tf_op jit(solution)/shard_map/ppermute | solution.py:28
  24.1 10.4 %collective-permute-start.11 = (bf16[1024,128]{1,0:T(8,128)(2,1)S(1)}, bf16[1024,128]{1,0:T(8,128)(2,1)S(1)}, u32[]{:S(2)}, u32[]{:S(2)}) collective-permute-start(bf16[1024,128]{1,0:T(8,128)(2,1)S(1)} %collective-permute-done.6.refs_6_), channel_id=1, source_target_pairs={{0,8},{8,0},{1,9},{9,1},{2,10},{10,2},{3,11},{11,3},{4,12},{12,4},... | collective-permute-start | bytes 786440 | tf_op jit(solution)/shard_map/ppermute | solution.py:28
  33.2 8.9 %collective-permute-start.8 = (bf16[1024,128]{1,0:T(8,128)(2,1)S(1)}, bf16[1024,128]{1,0:T(8,128)(2,1)S(1)}, u32[]{:S(2)}, u32[]{:S(2)}) collective-permute-start(bf16[1024,128]{1,0:T(8,128)(2,1)S(1)} %collective-permute-done.7.refs_6_), channel_id=1, source_target_pairs={{0,1},{1,2},{2,3},{3,4},{4,5},{5,6},{6,7},{7,0},{16,23},{17,16},{1... | collective-permute-start | bytes 786440 | tf_op jit(solution)/shard_map/ppermute | solution.py:28
  34.5 12.7 %collective-permute-start.13 = (bf16[1024,128]{1,0:T(8,128)(2,1)S(1)}, bf16[1024,128]{1,0:T(8,128)(2,1)S(1)}, u32[]{:S(2)}, u32[]{:S(2)}) collective-permute-start(bf16[1024,128]{1,0:T(8,128)(2,1)S(1)} %collective-permute-done.4.refs_5_), channel_id=1, source_target_pairs={{0,1},{1,2},{2,3},{3,4},{4,5},{5,6},{6,7},{7,0},{16,23},{17,16},{1... | collective-permute-start | bytes 786440 | tf_op jit(solution)/shard_map/ppermute | solution.py:28
  53.1 14.1 %collective-permute-start.18 = (bf16[1024,256]{1,0:T(8,128)(2,1)S(1)}, bf16[1024,256]{1,0:T(8,128)(2,1)S(1)}, u32[]{:S(2)}, u32[]{:S(2)}) collective-permute-start(bf16[1024,256]{1,0:T(8,128)(2,1)S(1)} %get-tuple-element.55.refs_1_), channel_id=1, source_target_pairs={{0,64},{64,0},{1,65},{65,1},{2,66},{66,2},{3,67},{67,3},{4,68},{68... | collective-permute-start | bytes 1572872 | tf_op jit(solution)/shard_map/ppermute | solution.py:28
  54.4 16.3 %collective-permute-start.19 = (bf16[1024,256]{1,0:T(8,128)(2,1)S(1)}, bf16[1024,256]{1,0:T(8,128)(2,1)S(1)}, u32[]{:S(2)}, u32[]{:S(2)}) collective-permute-start(bf16[1024,256]{1,0:T(8,128)(2,1)S(1)} %get-tuple-element.55.refs_1_), channel_id=1, source_target_pairs={{0,32},{32,0},{1,33},{33,1},{2,34},{34,2},{3,35},{35,3},{4,36},{36... | collective-permute-start | bytes 1572872 | tf_op jit(solution)/shard_map/ppermute | solution.py:28
  58.4 27.8 %collective-permute-start.20 = (bf16[1024,256]{1,0:T(8,128)(2,1)S(1)}, bf16[1024,256]{1,0:T(8,128)(2,1)S(1)}, u32[]{:S(2)}, u32[]{:S(2)}) collective-permute-start(bf16[1024,256]{1,0:T(8,128)(2,1)S(1)} %get-tuple-element.55.refs_1_), channel_id=1, source_target_pairs={{0,96},{32,64},{64,32},{96,0},{1,97},{33,65},{65,33},{97,1},{2,98}... | collective-permute-start | bytes 1572872 | tf_op jit(solution)/shard_map/ppermute | solution.py:28
  70.8 20.9 %all-to-all-start = ((bf16[16,128,128]{2,1,0:T(8,128)(2,1)}), bf16[16,128,128]{2,1,0:T(8,128)(2,1)S(1)}, u32[]{:S(2)}, u32[]{:S(2)}) async-start(bf16[16,128,128]{2,1,0:T(8,128)(2,1)} %column_parts.1), calls=%async_computation | async-start | bytes 1048576 | tf_op jit(solution)/shard_map/all_to_all | solution.py:289
  92.4 9.0 %collective-permute-start.22 = (bf16[1024,128]{1,0:T(8,128)(2,1)S(1)}, bf16[1024,128]{1,0:T(8,128)(2,1)S(1)}, u32[]{:S(2)}, u32[]{:S(2)}) collective-permute-start(bf16[1024,128]{1,0:T(8,128)(2,1)S(1)} %combine.1.refs_1_), channel_id=1, source_target_pairs={{0,8},{8,0},{1,9},{9,1},{2,10},{10,2},{3,11},{11,3},{4,12},{12,4},... | collective-permute-start | bytes 786440 | tf_op jit(solution)/shard_map/ppermute | solution.py:28
  94.4 8.7 %collective-permute-start.27 = (bf16[1024,128]{1,0:T(8,128)(2,1)S(1)}, bf16[1024,128]{1,0:T(8,128)(2,1)S(1)}, u32[]{:S(2)}, u32[]{:S(2)}) collective-permute-start(bf16[1024,128]{1,0:T(8,128)(2,1)S(1)} %combine.1.refs_1_), channel_id=1, source_target_pairs={{0,16},{16,0},{1,17},{17,1},{2,18},{18,2},{3,19},{19,3},{4,20},{20... | collective-permute-start | bytes 786440 | tf_op jit(solution)/shard_map/ppermute | solution.py:28
  94.6 10.0 %collective-permute-start.23 = (bf16[1024,128]{1,0:T(8,128)(2,1)S(1)}, bf16[1024,128]{1,0:T(8,128)(2,1)S(1)}, u32[]{:S(2)}, u32[]{:S(2)}) collective-permute-start(bf16[1024,128]{1,0:T(8,128)(2,1)S(1)} %combine.1.refs_1_), channel_id=1, source_target_pairs={{0,1},{1,2},{2,3},{3,4},{4,5},{5,6},{6,7},{7,0},{16,23},{17,16},{1... | collective-permute-start | bytes 786440 | tf_op jit(solution)/shard_map/ppermute | solution.py:28
  103.1 8.7 %collective-permute-start.28 = (bf16[1024,128]{1,0:T(8,128)(2,1)S(1)}, bf16[1024,128]{1,0:T(8,128)(2,1)S(1)}, u32[]{:S(2)}, u32[]{:S(2)}) collective-permute-start(bf16[1024,128]{1,0:T(8,128)(2,1)S(1)} %collective-permute-done.27), channel_id=1, source_target_pairs={{0,1},{1,2},{2,3},{3,4},{4,5},{5,6},{6,7},{7,0},{16,23},{17,16},{1... | collective-permute-start | bytes 786440 | tf_op jit(solution)/shard_map/ppermute | solution.py:28
  104.6 10.0 %collective-permute-start.25 = (bf16[1024,128]{1,0:T(8,128)(2,1)S(1)}, bf16[1024,128]{1,0:T(8,128)(2,1)S(1)}, u32[]{:S(2)}, u32[]{:S(2)}) collective-permute-start(bf16[1024,128]{1,0:T(8,128)(2,1)S(1)} %collective-permute-done.23.refs_3_), channel_id=1, source_target_pairs={{0,1},{1,2},{2,3},{3,4},{4,5},{5,6},{6,7},{7,0},{16,23},{17,16},{1... | collective-permute-start | bytes 786440 | tf_op jit(solution)/shard_map/ppermute | solution.py:28
  112.3 9.9 %collective-permute-start.29 = (bf16[1024,128]{1,0:T(8,128)(2,1)S(1)}, bf16[1024,128]{1,0:T(8,128)(2,1)S(1)}, u32[]{:S(2)}, u32[]{:S(2)}) collective-permute-start(bf16[1024,128]{1,0:T(8,128)(2,1)S(1)} %collective-permute-done.28.refs_5_), channel_id=1, source_target_pairs={{0,1},{1,2},{2,3},{3,4},{4,5},{5,6},{6,7},{7,0},{16,23},{17,16},{1... | collective-permute-start | bytes 786440 | tf_op jit(solution)/shard_map/ppermute | solution.py:28
  114.6 10.4 %collective-permute-start.26 = (bf16[1024,128]{1,0:T(8,128)(2,1)S(1)}, bf16[1024,128]{1,0:T(8,128)(2,1)S(1)}, u32[]{:S(2)}, u32[]{:S(2)}) collective-permute-start(bf16[1024,128]{1,0:T(8,128)(2,1)S(1)} %collective-permute-done.25.refs_2_), channel_id=1, source_target_pairs={{0,1},{1,2},{2,3},{3,4},{4,5},{5,6},{6,7},{7,0},{16,23},{17,16},{1... | collective-permute-start | bytes 786440 | tf_op jit(solution)/shard_map/ppermute | solution.py:28
  115.4 9.6 %collective-permute-start.33 = (bf16[1024,128]{1,0:T(8,128)(2,1)S(1)}, bf16[1024,128]{1,0:T(8,128)(2,1)S(1)}, u32[]{:S(2)}, u32[]{:S(2)}) collective-permute-start(bf16[1024,128]{1,0:T(8,128)(2,1)S(1)} %collective-permute-done.28.refs_5_), channel_id=1, source_target_pairs={{0,8},{8,0},{1,9},{9,1},{2,10},{10,2},{3,11},{11,3},{4,12},{12,4},... | collective-permute-start | bytes 786440 | tf_op jit(solution)/shard_map/ppermute | solution.py:28
  123.9 8.6 %collective-permute-start.30 = (bf16[1024,128]{1,0:T(8,128)(2,1)S(1)}, bf16[1024,128]{1,0:T(8,128)(2,1)S(1)}, u32[]{:S(2)}, u32[]{:S(2)}) collective-permute-start(bf16[1024,128]{1,0:T(8,128)(2,1)S(1)} %collective-permute-done.29.refs_5_), channel_id=1, source_target_pairs={{0,1},{1,2},{2,3},{3,4},{4,5},{5,6},{6,7},{7,0},{16,23},{17,16},{1... | collective-permute-start | bytes 786440 | tf_op jit(solution)/shard_map/ppermute | solution.py:28
  125.0 10.4 %collective-permute-start.35 = (bf16[1024,128]{1,0:T(8,128)(2,1)S(1)}, bf16[1024,128]{1,0:T(8,128)(2,1)S(1)}, u32[]{:S(2)}, u32[]{:S(2)}) collective-permute-start(bf16[1024,128]{1,0:T(8,128)(2,1)S(1)} %collective-permute-done.26.refs_3_), channel_id=1, source_target_pairs={{0,1},{1,2},{2,3},{3,4},{4,5},{5,6},{6,7},{7,0},{16,23},{17,16},{1... | collective-permute-start | bytes 786440 | tf_op jit(solution)/shard_map/ppermute | solution.py:28
  (27 other events, 135.3 us)

commit v4 on v3

--- a/solution.py
+++ b/solution.py
@@ -217,23 +217,24 @@
 
 
 def gathered_product(block, weights, finish, outs, smem, name):
-    half = lax.axis_size("z") // 2
-    own, other, cross = [block], [swap(block, "core")], [swap(block, "xl")]
-    far = [None]
-    total_own = total_other = None
+    assert lax.axis_size("z") == 8
+    own, other = [block], [swap(block, "core")]
+    cross, far = [swap(after(block, other[0]), "xl")], [None]
     mine = [(0, own[0], cross[0])]
-    for s in range(1, half):
-        own_from, other_from, cross_from = own[-1], other[-1], cross[-1]
-        if s > 1:
-            own_from = after(own_from, cross[s - 2])
-            other_from = after(other_from, own[s - 1])
-            cross_from = after(cross_from, other[s - 1])
-        own.append(z_step(own_from))
-        other.append(z_step(other_from))
-        cross.append(z_step(cross_from))
-        far.append(swap(other[s], "xl"))
-    own.append(z_step(after(own[-1], cross[half - 2], far[1])))
-    cross.append(z_step(after(cross[-1], own[half - 1], far[2])))
+    own.append(z_step(own[0]))
+    other.append(z_step(other[0]))
+    far.append(swap(other[1], "xl"))
+    own.append(z_step(own[1]))
+    cross.append(z_step(after(cross[0], other[1])))
+    other.append(z_step(after(other[1], own[1])))
+    far.append(swap(other[2], "xl"))
+    own.append(z_step(after(own[2], other[1])))
+    cross.append(z_step(after(cross[1], own[2])))
+    other.append(z_step(after(other[2], cross[1])))
+    far.append(swap(other[3], "xl"))
+    own.append(z_step(after(own[3], other[2], far[1])))
+    cross.append(z_step(after(cross[2], own[3])))
+    cross.append(z_step(after(cross[3], far[2])))
 
     total_own, total_other = contract(
         weights,
@@ -254,7 +255,7 @@
     )
     mine = []
     both = swap(total_other, "core")
-    mine += [(s, own[s], cross[s]) for s in (half - 1, half)]
+    mine += [(s, own[s], cross[s]) for s in (3, 4)]
     return contract(
         weights,
         [[total_own, *mine]],
@@ -281,13 +282,13 @@
     unit_other = swap(unit, "core")
     from_y, from_x = swap(joined, "yl"), swap(joined, "xh")
     from_yx = swap(joined, "yl", "xh")
-    w_parts = column_parts(w_out, heads)
+    parts = column_parts(w_out, heads)
+    w_cols = lax.all_to_all(after(parts, joined), HEAD, 0, 0).reshape(heads * HD, HD)
+    unit_other = after(unit_other, w_cols)
 
     own, other = attend(
         doc_lengths, [(unit, None, True), (unit_other, None, False)], [(0, joined)], "attend_own"
     )
-    w_cols = lax.all_to_all(after(w_parts, own, from_y, from_x), HEAD, 0, 0)
-    w_cols = w_cols.reshape(heads * HD, HD)
     own, other = attend(
         doc_lengths,
         [(unit, own, False), (unit_other, other, False)],
@@ -299,7 +300,7 @@
     )
     theirs = swap(other, "core")
     (own,) = attend(doc_lengths, [(unit, own, False)], [(6, from_yx)], "attend_far_own")
-    attended = combine(doc_lengths, after(own, w_cols), theirs, "combine")
+    attended = combine(doc_lengths, own, theirs, "combine")
 
     return gathered_product(
         attended,

time: 144 us -> 149 us (1.035)
  waiting for transfers between devices: 65.2 us -> 83.3 us
  starting transfers between devices: 47.3 us -> 38.9 us
  local copies, waits for them, and re-layouts: 8.43 us -> 3.19 us
    all_to_all x1, waiting for transfers between devices: 0.01 us -> 10.2 us  [per_device(): lax.all_to_all(after(parts, joined), HEAD, 0, 0).reshape(heads * HD, HD)]
    ppermute x39, starting transfers between devices: 40.4 us -> 32 us  [hop(): lax.ppermute(value, axes, [(number[c], number[tuple(target(*c))]) for c i...]
    ppermute x39, waiting for transfers between devices: 65.2 us -> 73.1 us  [hop(): lax.ppermute(value, axes, [(number[c], number[tuple(target(*c))]) for c i...]
    unnamed x22 -> x14, local copies, waits for them, and re-layouts: 8.43 us -> 3.19 us
  transfers between devices with their start and end apart: 40 -> 40, of which waited for: 29 -> 29; matrix products, arithmetic and copies ran while one was open for 0% -> 0% of each run, Pallas kernels for 12% -> 10%
where the time goes in v4:
time: 149 us; the launch traced here: 147 us
  waiting for transfers between devices  83.3 us (56%)
  starting transfers between devices  38.9 us (26%)
  Pallas kernels  21.5 us (14%)
  local copies, waits for them, and re-layouts  3.19 us (2%)
    ppermute x39, waiting for transfers between devices, hop(): lax.ppermute(value, axes, [(number[c], number[tuple(target(*c))]) for c i...  73.1 us
    ppermute x39, starting transfers between devices, hop(): lax.ppermute(value, axes, [(number[c], number[tuple(target(*c))]) for c i...  32 us
    pallas_call x12, Pallas kernels, call(): pl.pallas_call(kernel, out_shape=outs, in_specs=[SMEM] * smem_count + [VM...  21.5 us
    all_to_all x1, waiting for transfers between devices, per_device(): lax.all_to_all(after(parts, joined), HEAD, 0, 0).reshape(heads * HD, HD)  10.2 us
    all_to_all x1, starting transfers between devices, per_device(): lax.all_to_all(after(parts, joined), HEAD, 0, 0).reshape(heads * HD, HD)  6.89 us
    unnamed x14, local copies, waits for them, and re-layouts  3.19 us
  transfers between devices with their start and end apart: 40, of which 29 were waited for; matrix products, arithmetic and copies ran while one was open for 0% of the time, Pallas kernels for 10%

profile of v4, /device:TPU:16, one launch (start us, length us, event | category | flops | bytes accessed | tf_op | source)
XLA Modules:
  0.0 147.1 jit_solution(1289149565950227947)
XLA Ops:
  5.3 5.1 %collective-permute-done.2.refs_4_ = bf16[1024,128]{1,0:T(8,128)(2,1)S(1)} collective-permute-done((bf16[1024,128]{1,0:T(8,128)(2,1)}, bf16[1024,128]{1,0:T(8,128)(2,1)S(1)}, u32[]{:S(2)}, u32[]{:S(2)}) %collective-permute-start.2) | collective-permute-done | bytes 262176 | tf_op jit(solution)/shard_map/ppermute | solution.py:28
  10.4 2.8 %collective-permute-done.3.refs_6_ = bf16[1024,128]{1,0:T(8,128)(2,1)S(1)} collective-permute-done((bf16[1024,128]{1,0:T(8,128)(2,1)S(1)}, bf16[1024,128]{1,0:T(8,128)(2,1)S(1)}, u32[]{:S(2)}, u32[]{:S(2)}) %collective-permute-start.3) | collective-permute-done | bytes 262176 | tf_op jit(solution)/shard_map/ppermute | solution.py:28
  14.0 4.0 %collective-permute-done.5.refs_3_ = bf16[1024,128]{1,0:T(8,128)(2,1)S(1)} collective-permute-done((bf16[1024,128]{1,0:T(8,128)(2,1)S(1)}, bf16[1024,128]{1,0:T(8,128)(2,1)S(1)}, u32[]{:S(2)}, u32[]{:S(2)}) %collective-permute-start.5) | collective-permute-done | bytes 262176 | tf_op jit(solution)/shard_map/ppermute | solution.py:28
  18.0 3.2 %collective-permute-done.4.refs_5_ = bf16[1024,128]{1,0:T(8,128)(2,1)S(1)} collective-permute-done((bf16[1024,128]{1,0:T(8,128)(2,1)S(1)}, bf16[1024,128]{1,0:T(8,128)(2,1)S(1)}, u32[]{:S(2)}, u32[]{:S(2)}) %collective-permute-start.4) | collective-permute-done | bytes 262176 | tf_op jit(solution)/shard_map/ppermute | solution.py:28
  22.7 5.7 %collective-permute-done.7.refs_6_ = bf16[1024,128]{1,0:T(8,128)(2,1)S(1)} collective-permute-done((bf16[1024,128]{1,0:T(8,128)(2,1)S(1)}, bf16[1024,128]{1,0:T(8,128)(2,1)S(1)}, u32[]{:S(2)}, u32[]{:S(2)}) %collective-permute-start.7) | collective-permute-done | bytes 262176 | tf_op jit(solution)/shard_map/ppermute | solution.py:28
  31.2 2.6 %collective-permute-start.13 = (bf16[1024,128]{1,0:T(8,128)(2,1)S(1)}, bf16[1024,128]{1,0:T(8,128)(2,1)S(1)}, u32[]{:S(2)}, u32[]{:S(2)}) collective-permute-start(bf16[1024,128]{1,0:T(8,128)(2,1)S(1)} %collective-permute-done.6.refs_5_), channel_id=1, source_target_pairs={{0,1},{1,2},{2,3},{3,4},{4,5},{5,6},{6,7},{7,0},{16,23},{17,16},{1... | collective-permute-start | bytes 786440 | tf_op jit(solution)/shard_map/ppermute | solution.py:28
  33.8 2.3 %collective-permute-done.12.refs_7_ = bf16[1024,128]{1,0:T(8,128)(2,1)S(1)} collective-permute-done((bf16[1024,128]{1,0:T(8,128)(2,1)S(1)}, bf16[1024,128]{1,0:T(8,128)(2,1)S(1)}, u32[]{:S(2)}, u32[]{:S(2)}) %collective-permute-start.12) | collective-permute-done | bytes 262176 | tf_op jit(solution)/shard_map/ppermute | solution.py:28
  36.0 2.7 %collective-permute-done.10.refs_6_ = bf16[1024,128]{1,0:T(8,128)(2,1)S(1)} collective-permute-done((bf16[1024,128]{1,0:T(8,128)(2,1)S(1)}, bf16[1024,128]{1,0:T(8,128)(2,1)S(1)}, u32[]{:S(2)}, u32[]{:S(2)}) %collective-permute-start.10) | collective-permute-done | bytes 262176 | tf_op jit(solution)/shard_map/ppermute | solution.py:28
  38.8 2.8 %collective-permute-done.8.refs_8_ = bf16[1024,128]{1,0:T(8,128)(2,1)S(1)} collective-permute-done((bf16[1024,128]{1,0:T(8,128)(2,1)S(1)}, bf16[1024,128]{1,0:T(8,128)(2,1)S(1)}, u32[]{:S(2)}, u32[]{:S(2)}) %collective-permute-start.8) | collective-permute-done | bytes 262176 | tf_op jit(solution)/shard_map/ppermute | solution.py:28
  52.6 6.9 %all-to-all-start = ((bf16[16,128,128]{2,1,0:T(8,128)(2,1)}), bf16[16,128,128]{2,1,0:T(8,128)(2,1)S(1)}, u32[]{:S(2)}, u32[]{:S(2)}) async-start(bf16[16,128,128]{2,1,0:T(8,128)(2,1)} %column_parts.1), calls=%async_computation | async-start | bytes 1048576 | tf_op jit(solution)/shard_map/all_to_all | solution.py:286
  60.9 2.7 %collective-permute-start.19 = (bf16[1024,256]{1,0:T(8,128)(2,1)S(1)}, bf16[1024,256]{1,0:T(8,128)(2,1)S(1)}, u32[]{:S(2)}, u32[]{:S(2)}) collective-permute-start(bf16[1024,256]{1,0:T(8,128)(2,1)S(1)} %get-tuple-element.58.refs_1_), channel_id=1, source_target_pairs={{0,32},{32,0},{1,33},{33,1},{2,34},{34,2},{3,35},{35,3},{4,36},{36... | collective-permute-start | bytes 1572872 | tf_op jit(solution)/shard_map/ppermute | solution.py:28
  65.2 10.2 %all-to-all-done = bf16[16,128,128]{2,1,0:T(8,128)(2,1)S(1)} async-done(((bf16[16,128,128]{2,1,0:T(8,128)(2,1)}), bf16[16,128,128]{2,1,0:T(8,128)(2,1)S(1)}, u32[]{:S(2)}, u32[]{:S(2)}) %all-to-all-start) | async-done | bytes 524320 | tf_op jit(solution)/shard_map/all_to_all | solution.py:286
  75.4 4.9 %attend_own.1 = (f32[1024,256]{1,0:T(8,128)S(1)}, f32[1024,256]{1,0:T(8,128)S(1)}) custom-call(s32[2]{0:T(128)S(1)} %copy-done.6, bf16[1024,256]{1,0:T(8,128)(2,1)S(1)} %get-tuple-element.58.refs_1_, bf16[1024,128]{1,0:T(8,128)(2,1)S(1)} %get-tuple-element.60.refs_2_.refs_3_, bf16[1024,128]{1,0:T(8,128)(2,1)S(1)} %collective-permute-done.20.refs_3_.refs_5_.refs_2_), custom_call_target="tpu_custom_call" | custom-call | flops 2147483648 | bytes 3145736 | tf_op jit(solution)/shard_map/attend_own/pallas_call | solution.py:46
  81.7 6.0 %attend_near.1 = (f32[1024,256]{1,0:T(8,128)S(1)}, f32[1024,256]{1,0:T(8,128)S(1)}) custom-call(s32[2]{0:T(128)S(1)} %copy-done.6, bf16[1024,256]{1,0:T(8,128)(2,1)S(1)} %collective-permute-done.18.refs_1_, bf16[1024,256]{1,0:T(8,128)(2,1)S(1)} %collective-permute-done.19.refs_2_, bf16[1024,128]{1,0:T(8,128)(2,1)S(1)} %get-tuple-element.60.refs_2_.refs_3_, ...), custom_call_target="tpu_custom_call" | custom-call | flops 4294967296 | bytes 5767176 | tf_op jit(solution)/shard_map/attend_near/pallas_call | solution.py:46
  87.7 4.7 %collective-permute-done.17.refs_1_ = bf16[1024,256]{1,0:T(8,128)(2,1)S(1)} collective-permute-done((bf16[1024,256]{1,0:T(8,128)(2,1)S(1)}, bf16[1024,256]{1,0:T(8,128)(2,1)S(1)}, u32[]{:S(2)}, u32[]{:S(2)}) %collective-permute-start.17) | collective-permute-done | bytes 524320 | tf_op jit(solution)/shard_map/ppermute | solution.py:28
  102.3 3.5 %collective-permute-done.24.refs_3_ = bf16[1024,128]{1,0:T(8,128)(2,1)S(1)} collective-permute-done((bf16[1024,128]{1,0:T(8,128)(2,1)S(1)}, bf16[1024,128]{1,0:T(8,128)(2,1)S(1)}, u32[]{:S(2)}, u32[]{:S(2)}) %collective-permute-start.24) | collective-permute-done | bytes 262176 | tf_op jit(solution)/shard_map/ppermute | solution.py:28
  106.3 2.8 %collective-permute-done.23.refs_2_ = bf16[1024,128]{1,0:T(8,128)(2,1)S(1)} collective-permute-done((bf16[1024,128]{1,0:T(8,128)(2,1)S(1)}, bf16[1024,128]{1,0:T(8,128)(2,1)S(1)}, u32[]{:S(2)}, u32[]{:S(2)}) %collective-permute-start.23) | collective-permute-done | bytes 262176 | tf_op jit(solution)/shard_map/ppermute | solution.py:28
  109.7 3.7 %collective-permute-done.27.refs_2_ = bf16[1024,128]{1,0:T(8,128)(2,1)S(1)} collective-permute-done((bf16[1024,128]{1,0:T(8,128)(2,1)S(1)}, bf16[1024,128]{1,0:T(8,128)(2,1)S(1)}, u32[]{:S(2)}, u32[]{:S(2)}) %collective-permute-start.27) | collective-permute-done | bytes 262176 | tf_op jit(solution)/shard_map/ppermute | solution.py:28
  113.8 2.9 %collective-permute-done.26.refs_4_ = bf16[1024,128]{1,0:T(8,128)(2,1)S(1)} collective-permute-done((bf16[1024,128]{1,0:T(8,128)(2,1)S(1)}, bf16[1024,128]{1,0:T(8,128)(2,1)S(1)}, u32[]{:S(2)}, u32[]{:S(2)}) %collective-permute-start.26) | collective-permute-done | bytes 262176 | tf_op jit(solution)/shard_map/ppermute | solution.py:28
  117.8 6.0 %collective-permute-done.29.refs_5_ = bf16[1024,128]{1,0:T(8,128)(2,1)S(1)} collective-permute-done((bf16[1024,128]{1,0:T(8,128)(2,1)S(1)}, bf16[1024,128]{1,0:T(8,128)(2,1)S(1)}, u32[]{:S(2)}, u32[]{:S(2)}) %collective-permute-start.29) | collective-permute-done | bytes 262176 | tf_op jit(solution)/shard_map/ppermute | solution.py:28
  126.9 2.8 %collective-permute-start.35 = (bf16[1024,128]{1,0:T(8,128)(2,1)S(1)}, bf16[1024,128]{1,0:T(8,128)(2,1)S(1)}, u32[]{:S(2)}, u32[]{:S(2)}) collective-permute-start(bf16[1024,128]{1,0:T(8,128)(2,1)S(1)} %collective-permute-done.28.refs_3_), channel_id=1, source_target_pairs={{0,1},{1,2},{2,3},{3,4},{4,5},{5,6},{6,7},{7,0},{16,23},{17,16},{1... | collective-permute-start | bytes 786440 | tf_op jit(solution)/shard_map/ppermute | solution.py:28
  130.4 3.7 %collective-permute-done.32.refs_4_ = bf16[1024,128]{1,0:T(8,128)(2,1)S(1)} collective-permute-done((bf16[1024,128]{1,0:T(8,128)(2,1)S(1)}, bf16[1024,128]{1,0:T(8,128)(2,1)S(1)}, u32[]{:S(2)}, u32[]{:S(2)}) %collective-permute-start.32) | collective-permute-done | bytes 262176 | tf_op jit(solution)/shard_map/ppermute | solution.py:28
  134.2 2.8 %collective-permute-done.30.refs_7_ = bf16[1024,128]{1,0:T(8,128)(2,1)S(1)} collective-permute-done((bf16[1024,128]{1,0:T(8,128)(2,1)S(1)}, bf16[1024,128]{1,0:T(8,128)(2,1)S(1)}, u32[]{:S(2)}, u32[]{:S(2)}) %collective-permute-start.30) | collective-permute-done | bytes 262176 | tf_op jit(solution)/shard_map/ppermute | solution.py:28
  139.8 2.8 %collective-permute-done.36.refs_6_ = bf16[1024,128]{1,0:T(8,128)(2,1)S(1)} collective-permute-done((bf16[1024,128]{1,0:T(8,128)(2,1)S(1)}, bf16[1024,128]{1,0:T(8,128)(2,1)S(1)}, u32[]{:S(2)}, u32[]{:S(2)}) %collective-permute-start.36) | collective-permute-done | bytes 262176 | tf_op jit(solution)/shard_map/ppermute | solution.py:28
  (82 shorter events, 49.3 us)
Async XLA Ops:
  0.0 10.4 %collective-permute-start.2 = (bf16[1024,128]{1,0:T(8,128)(2,1)}, bf16[1024,128]{1,0:T(8,128)(2,1)S(1)}, u32[]{:S(2)}, u32[]{:S(2)}) collective-permute-start(bf16[1024,128]{1,0:T(8,128)(2,1)} %refs_2_.2), channel_id=1, source_target_pairs={{0,1},{1,2},{2,3},{3,4},{4,5},{5,6},{6,7},{7,0},{16,23},{17,16},{1... | collective-permute-start | bytes 786440 | tf_op jit(solution)/shard_map/ppermute | solution.py:28
  1.9 11.3 %collective-permute-start.3 = (bf16[1024,128]{1,0:T(8,128)(2,1)S(1)}, bf16[1024,128]{1,0:T(8,128)(2,1)S(1)}, u32[]{:S(2)}, u32[]{:S(2)}) collective-permute-start(bf16[1024,128]{1,0:T(8,128)(2,1)S(1)} %collective-permute-done), channel_id=1, source_target_pairs={{0,1},{1,2},{2,3},{3,4},{4,5},{5,6},{6,7},{7,0},{16,23},{17,16},{1... | collective-permute-start | bytes 786440 | tf_op jit(solution)/shard_map/ppermute | solution.py:28
  3.8 9.4 %collective-permute-start.1 = (bf16[1024,128]{1,0:T(8,128)(2,1)}, bf16[1024,128]{1,0:T(8,128)(2,1)S(1)}, u32[]{:S(2)}, u32[]{:S(2)}) collective-permute-start(bf16[1024,128]{1,0:T(8,128)(2,1)} %refs_2_.2), channel_id=1, source_target_pairs={{0,8},{8,0},{1,9},{9,1},{2,10},{10,2},{3,11},{11,3},{4,12},{12,4},... | collective-permute-start | bytes 786440 | tf_op jit(solution)/shard_map/ppermute | solution.py:28
  13.2 8.0 %collective-permute-start.4 = (bf16[1024,128]{1,0:T(8,128)(2,1)S(1)}, bf16[1024,128]{1,0:T(8,128)(2,1)S(1)}, u32[]{:S(2)}, u32[]{:S(2)}) collective-permute-start(bf16[1024,128]{1,0:T(8,128)(2,1)S(1)} %collective-permute-done.1.refs_3_), channel_id=1, source_target_pairs={{0,1},{1,2},{2,3},{3,4},{4,5},{5,6},{6,7},{7,0},{16,23},{17,16},{1... | collective-permute-start | bytes 786440 | tf_op jit(solution)/shard_map/ppermute | solution.py:28
  18.0 11.9 %collective-permute-start.6 = (bf16[1024,128]{1,0:T(8,128)(2,1)S(1)}, bf16[1024,128]{1,0:T(8,128)(2,1)S(1)}, u32[]{:S(2)}, u32[]{:S(2)}) collective-permute-start(bf16[1024,128]{1,0:T(8,128)(2,1)S(1)} %collective-permute-done.5.refs_3_), channel_id=1, source_target_pairs={{0,1},{1,2},{2,3},{3,4},{4,5},{5,6},{6,7},{7,0},{16,23},{17,16},{1... | collective-permute-start | bytes 786440 | tf_op jit(solution)/shard_map/ppermute | solution.py:28
  18.0 10.4 %collective-permute-start.7 = (bf16[1024,128]{1,0:T(8,128)(2,1)S(1)}, bf16[1024,128]{1,0:T(8,128)(2,1)S(1)}, u32[]{:S(2)}, u32[]{:S(2)}) collective-permute-start(bf16[1024,128]{1,0:T(8,128)(2,1)S(1)} %collective-permute-done.3.refs_6_), channel_id=1, source_target_pairs={{0,1},{1,2},{2,3},{3,4},{4,5},{5,6},{6,7},{7,0},{16,23},{17,16},{1... | collective-permute-start | bytes 786440 | tf_op jit(solution)/shard_map/ppermute | solution.py:28
  21.2 10.0 %collective-permute-start.9 = (bf16[1024,128]{1,0:T(8,128)(2,1)S(1)}, bf16[1024,128]{1,0:T(8,128)(2,1)S(1)}, u32[]{:S(2)}, u32[]{:S(2)}) collective-permute-start(bf16[1024,128]{1,0:T(8,128)(2,1)S(1)} %collective-permute-done.4.refs_5_), channel_id=1, source_target_pairs={{0,1},{1,2},{2,3},{3,4},{4,5},{5,6},{6,7},{7,0},{16,23},{17,16},{1... | collective-permute-start | bytes 786440 | tf_op jit(solution)/shard_map/ppermute | solution.py:28
  21.2 10.0 %collective-permute-start.11 = (bf16[1024,128]{1,0:T(8,128)(2,1)S(1)}, bf16[1024,128]{1,0:T(8,128)(2,1)S(1)}, u32[]{:S(2)}, u32[]{:S(2)}) collective-permute-start(bf16[1024,128]{1,0:T(8,128)(2,1)S(1)} %collective-permute-done.3.refs_6_), channel_id=1, source_target_pairs={{0,8},{8,0},{1,9},{9,1},{2,10},{10,2},{3,11},{11,3},{4,12},{12,4},... | collective-permute-start | bytes 786440 | tf_op jit(solution)/shard_map/ppermute | solution.py:28
  31.2 10.4 %collective-permute-start.8 = (bf16[1024,128]{1,0:T(8,128)(2,1)S(1)}, bf16[1024,128]{1,0:T(8,128)(2,1)S(1)}, u32[]{:S(2)}, u32[]{:S(2)}) collective-permute-start(bf16[1024,128]{1,0:T(8,128)(2,1)S(1)} %collective-permute-done.7.refs_6_), channel_id=1, source_target_pairs={{0,1},{1,2},{2,3},{3,4},{4,5},{5,6},{6,7},{7,0},{16,23},{17,16},{1... | collective-permute-start | bytes 786440 | tf_op jit(solution)/shard_map/ppermute | solution.py:28
  31.2 15.5 %collective-permute-start.13 = (bf16[1024,128]{1,0:T(8,128)(2,1)S(1)}, bf16[1024,128]{1,0:T(8,128)(2,1)S(1)}, u32[]{:S(2)}, u32[]{:S(2)}) collective-permute-start(bf16[1024,128]{1,0:T(8,128)(2,1)S(1)} %collective-permute-done.6.refs_5_), channel_id=1, source_target_pairs={{0,1},{1,2},{2,3},{3,4},{4,5},{5,6},{6,7},{7,0},{16,23},{17,16},{1... | collective-permute-start | bytes 786440 | tf_op jit(solution)/shard_map/ppermute | solution.py:28
  38.8 8.4 %collective-permute-start.14 = (bf16[1024,128]{1,0:T(8,128)(2,1)S(1)}, bf16[1024,128]{1,0:T(8,128)(2,1)S(1)}, u32[]{:S(2)}, u32[]{:S(2)}) collective-permute-start(bf16[1024,128]{1,0:T(8,128)(2,1)S(1)} %collective-permute-done.10.refs_6_), channel_id=1, source_target_pairs={{0,1},{1,2},{2,3},{3,4},{4,5},{5,6},{6,7},{7,0},{16,23},{17,16},{1... | collective-permute-start | bytes 786440 | tf_op jit(solution)/shard_map/ppermute | solution.py:28
  52.6 22.7 %all-to-all-start = ((bf16[16,128,128]{2,1,0:T(8,128)(2,1)}), bf16[16,128,128]{2,1,0:T(8,128)(2,1)S(1)}, u32[]{:S(2)}, u32[]{:S(2)}) async-start(bf16[16,128,128]{2,1,0:T(8,128)(2,1)} %column_parts.1), calls=%async_computation | async-start | bytes 1048576 | tf_op jit(solution)/shard_map/all_to_all | solution.py:286
  59.5 20.8 %collective-permute-start.18 = (bf16[1024,256]{1,0:T(8,128)(2,1)S(1)}, bf16[1024,256]{1,0:T(8,128)(2,1)S(1)}, u32[]{:S(2)}, u32[]{:S(2)}) collective-permute-start(bf16[1024,256]{1,0:T(8,128)(2,1)S(1)} %get-tuple-element.58.refs_1_), channel_id=1, source_target_pairs={{0,64},{64,0},{1,65},{65,1},{2,66},{66,2},{3,67},{67,3},{4,68},{68... | collective-permute-start | bytes 1572872 | tf_op jit(solution)/shard_map/ppermute | solution.py:28
  60.9 20.8 %collective-permute-start.19 = (bf16[1024,256]{1,0:T(8,128)(2,1)S(1)}, bf16[1024,256]{1,0:T(8,128)(2,1)S(1)}, u32[]{:S(2)}, u32[]{:S(2)}) collective-permute-start(bf16[1024,256]{1,0:T(8,128)(2,1)S(1)} %get-tuple-element.58.refs_1_), channel_id=1, source_target_pairs={{0,32},{32,0},{1,33},{33,1},{2,34},{34,2},{3,35},{35,3},{4,36},{36... | collective-permute-start | bytes 1572872 | tf_op jit(solution)/shard_map/ppermute | solution.py:28
  63.6 28.7 %collective-permute-start.17 = (bf16[1024,256]{1,0:T(8,128)(2,1)S(1)}, bf16[1024,256]{1,0:T(8,128)(2,1)S(1)}, u32[]{:S(2)}, u32[]{:S(2)}) collective-permute-start(bf16[1024,256]{1,0:T(8,128)(2,1)S(1)} %get-tuple-element.58.refs_1_), channel_id=1, source_target_pairs={{0,96},{32,64},{64,32},{96,0},{1,97},{33,65},{65,33},{97,1},{2,98}... | collective-permute-start | bytes 1572872 | tf_op jit(solution)/shard_map/ppermute | solution.py:28
  99.9 9.1 %collective-permute-start.23 = (bf16[1024,128]{1,0:T(8,128)(2,1)S(1)}, bf16[1024,128]{1,0:T(8,128)(2,1)S(1)}, u32[]{:S(2)}, u32[]{:S(2)}) collective-permute-start(bf16[1024,128]{1,0:T(8,128)(2,1)S(1)} %combine.1.refs_1_), channel_id=1, source_target_pairs={{0,8},{8,0},{1,9},{9,1},{2,10},{10,2},{3,11},{11,3},{4,12},{12,4},... | collective-permute-start | bytes 786440 | tf_op jit(solution)/shard_map/ppermute | solution.py:28
  101.1 7.9 %collective-permute-start.25 = (bf16[1024,128]{1,0:T(8,128)(2,1)S(1)}, bf16[1024,128]{1,0:T(8,128)(2,1)S(1)}, u32[]{:S(2)}, u32[]{:S(2)}) collective-permute-start(bf16[1024,128]{1,0:T(8,128)(2,1)S(1)} %collective-permute-done.22), channel_id=1, source_target_pairs={{0,1},{1,2},{2,3},{3,4},{4,5},{5,6},{6,7},{7,0},{16,23},{17,16},{1... | collective-permute-start | bytes 786440 | tf_op jit(solution)/shard_map/ppermute | solution.py:28
  113.4 11.8 %collective-permute-start.28 = (bf16[1024,128]{1,0:T(8,128)(2,1)S(1)}, bf16[1024,128]{1,0:T(8,128)(2,1)S(1)}, u32[]{:S(2)}, u32[]{:S(2)}) collective-permute-start(bf16[1024,128]{1,0:T(8,128)(2,1)S(1)} %collective-permute-done.27.refs_2_), channel_id=1, source_target_pairs={{0,1},{1,2},{2,3},{3,4},{4,5},{5,6},{6,7},{7,0},{16,23},{17,16},{1... | collective-permute-start | bytes 786440 | tf_op jit(solution)/shard_map/ppermute | solution.py:28
  113.4 10.4 %collective-permute-start.29 = (bf16[1024,128]{1,0:T(8,128)(2,1)S(1)}, bf16[1024,128]{1,0:T(8,128)(2,1)S(1)}, u32[]{:S(2)}, u32[]{:S(2)}) collective-permute-start(bf16[1024,128]{1,0:T(8,128)(2,1)S(1)} %collective-permute-done.25.refs_5_), channel_id=1, source_target_pairs={{0,1},{1,2},{2,3},{3,4},{4,5},{5,6},{6,7},{7,0},{16,23},{17,16},{1... | collective-permute-start | bytes 786440 | tf_op jit(solution)/shard_map/ppermute | solution.py:28
  116.6 10.0 %collective-permute-start.31 = (bf16[1024,128]{1,0:T(8,128)(2,1)S(1)}, bf16[1024,128]{1,0:T(8,128)(2,1)S(1)}, u32[]{:S(2)}, u32[]{:S(2)}) collective-permute-start(bf16[1024,128]{1,0:T(8,128)(2,1)S(1)} %collective-permute-done.26.refs_4_), channel_id=1, source_target_pairs={{0,1},{1,2},{2,3},{3,4},{4,5},{5,6},{6,7},{7,0},{16,23},{17,16},{1... | collective-permute-start | bytes 786440 | tf_op jit(solution)/shard_map/ppermute | solution.py:28
  116.6 10.3 %collective-permute-start.33 = (bf16[1024,128]{1,0:T(8,128)(2,1)S(1)}, bf16[1024,128]{1,0:T(8,128)(2,1)S(1)}, u32[]{:S(2)}, u32[]{:S(2)}) collective-permute-start(bf16[1024,128]{1,0:T(8,128)(2,1)S(1)} %collective-permute-done.25.refs_5_), channel_id=1, source_target_pairs={{0,8},{8,0},{1,9},{9,1},{2,10},{10,2},{3,11},{11,3},{4,12},{12,4},... | collective-permute-start | bytes 786440 | tf_op jit(solution)/shard_map/ppermute | solution.py:28
  126.6 10.4 %collective-permute-start.30 = (bf16[1024,128]{1,0:T(8,128)(2,1)S(1)}, bf16[1024,128]{1,0:T(8,128)(2,1)S(1)}, u32[]{:S(2)}, u32[]{:S(2)}) collective-permute-start(bf16[1024,128]{1,0:T(8,128)(2,1)S(1)} %collective-permute-done.29.refs_5_), channel_id=1, source_target_pairs={{0,1},{1,2},{2,3},{3,4},{4,5},{5,6},{6,7},{7,0},{16,23},{17,16},{1... | collective-permute-start | bytes 786440 | tf_op jit(solution)/shard_map/ppermute | solution.py:28
  126.9 12.8 %collective-permute-start.35 = (bf16[1024,128]{1,0:T(8,128)(2,1)S(1)}, bf16[1024,128]{1,0:T(8,128)(2,1)S(1)}, u32[]{:S(2)}, u32[]{:S(2)}) collective-permute-start(bf16[1024,128]{1,0:T(8,128)(2,1)S(1)} %collective-permute-done.28.refs_3_), channel_id=1, source_target_pairs={{0,1},{1,2},{2,3},{3,4},{4,5},{5,6},{6,7},{7,0},{16,23},{17,16},{1... | collective-permute-start | bytes 786440 | tf_op jit(solution)/shard_map/ppermute | solution.py:28
  134.2 8.4 %collective-permute-start.36 = (bf16[1024,128]{1,0:T(8,128)(2,1)S(1)}, bf16[1024,128]{1,0:T(8,128)(2,1)S(1)}, u32[]{:S(2)}, u32[]{:S(2)}) collective-permute-start(bf16[1024,128]{1,0:T(8,128)(2,1)S(1)} %collective-permute-done.32.refs_4_), channel_id=1, source_target_pairs={{0,1},{1,2},{2,3},{3,4},{4,5},{5,6},{6,7},{7,0},{16,23},{17,16},{1... | collective-permute-start | bytes 786440 | tf_op jit(solution)/shard_map/ppermute | solution.py:28
  (23 other events, 97.1 us)

commit v5 on v2

--- a/solution.py
+++ b/solution.py
@@ -32,9 +32,9 @@
     return hop(value, axes, lambda *c: tuple(1 - i for i in c))
 
 
-def z_step(value):
+def z_step(value, way):
     depth = lax.axis_size("z")
-    return hop(value, ("core", "z"), lambda c, z: (c, (z + 1 - 2 * c) % depth))
+    return hop(value, ("z",), lambda z: ((z - way) % depth,))
 
 
 def params(mib):
@@ -63,7 +63,7 @@
     return doc_ref[lax.axis_index("yh")] - (in_doc ^ mask) * ROWS
 
 
-def contract(weights, jobs, name, finish=None, extras=(), outs=None, smem=()):
+def contract(weights, jobs, name, finish=None, outs=None, smem=()):
     width = sum(w.shape[1] for w in weights)
     flat, plan = [], []
     for total, *terms in jobs:
@@ -73,20 +73,19 @@
     tile = 256
     if outs is None:
         outs = [jax.ShapeDtypeStruct((rows, width), F32)] * len(jobs)
-    n_s, n_w, n_e, n_f = len(smem), len(weights), len(extras), len(flat)
+    n_s, n_w, n_f = len(smem), len(weights), len(flat)
     depth = lax.axis_size("z")
 
     def kernel(*refs):
         w_refs = refs[n_s : n_s + n_w]
-        e_refs = refs[n_s + n_w : n_s + n_w + n_e]
-        b_refs = list(refs[n_s + n_w + n_e : n_s + n_w + n_e + n_f])
-        o_refs = refs[n_s + n_w + n_e + n_f :]
-        xl, z, core = lax.axis_index("xl"), lax.axis_index("z"), lax.axis_index("core")
+        b_refs = list(refs[n_s + n_w : n_s + n_w + n_f])
+        o_refs = refs[n_s + n_w + n_f :]
+        xl, z = lax.axis_index("xl"), lax.axis_index("z")
         taken = {}
 
         def weight(step):
             if step not in taken:
-                z_at = (z + depth + (2 * core - 1) * step) % depth
+                z_at = (z + depth + step) % depth
                 halves = []
                 for side in (xl, 1 - xl):
                     first = pl.multiple_of((side * depth + z_at) * HD, HD)
@@ -109,22 +108,21 @@
                 if finish is None:
                     o_refs[index][here, :] = total.astype(o_refs[index].dtype)
                 else:
-                    finish(refs[:n_s], e_refs, o_refs, total, first, tile)
+                    finish(refs[:n_s], o_refs, total, first, tile)
 
     terms = sum(len(steps) for _, steps in plan)
     return call(
         kernel,
         outs,
         n_s,
-        [*smem, *weights, *extras, *flat],
+        [*smem, *weights, *flat],
         name,
         2 * rows * 256 * width * terms,
     )
 
 
-def finish_units(smem, extras, outs, total, first, tile):
+def finish_units(smem, outs, total, first, tile):
     here = slice(first, first + tile)
-    total = total + extras[0][here, :]
     proj = total[:, :HD]
     unit = proj * lax.rsqrt(jnp.sum(proj * proj, axis=-1, keepdims=True) + 1e-06)
     row = lax.broadcasted_iota(jnp.int32, (tile, HD), 0) + first
@@ -135,9 +133,9 @@
     outs[1][here, :] = unit
 
 
-def finish_out(smem, extras, outs, total, first, tile):
+def finish_out(smem, outs, total, first, tile):
     here = slice(first, first + tile)
-    outs[0][here, :] = (total + extras[0][here, :]).astype(BF16)
+    outs[0][here, :] = total.astype(BF16)
 
 
 def attend(doc_lengths, groups, blocks, name, out_type=F32, tile_q=512, tile_k=512):
@@ -217,43 +215,25 @@
 
 
 def gathered_product(block, weights, finish, outs, smem, name):
-    half = lax.axis_size("z") // 2
-    own, other, cross = [block], [swap(block, "core")], [swap(block, "xl")]
-    far = [None]
-    total_own = total_other = None
-    mine = [(0, own[0], cross[0])]
-    for s in range(1, half):
-        own_from, other_from, cross_from = own[-1], other[-1], cross[-1]
-        if s > 1:
-            own_from = after(own_from, cross[s - 2])
-            other_from = after(other_from, own[s - 1])
-            cross_from = after(cross_from, other[s - 1], *far[s - 2 : s - 1][: s - 2])
-        own.append(z_step(own_from))
-        other.append(z_step(other_from))
-        cross.append(z_step(cross_from))
-        far.append(swap(other[s], "xl"))
-    own.append(z_step(after(own[-1], cross[half - 2])))
-    cross.append(z_step(after(cross[-1], own[half - 1], far[half - 2])))
-
-    for s in range(1, half - 1):
-        mine.append((s, own[s], cross[s]))
-        mine[0] = (mine[0][0], after(mine[0][1], own[s + 1], other[s + 1], cross[s + 1]), mine[0][2])
-        total_own, total_other = contract(
-            weights, [[total_own, *mine], [total_other, (s, other[s], far[s])]], f"{name}_{s}"
-        )
-        mine = []
-    last_other = after(other[half - 1], own[half])
-    (total_other,) = contract(
-        weights, [[total_other, (half - 1, last_other, far[half - 1])]], f"{name}_{half - 1}"
-    )
-    both = swap(total_other, "core")
-    mine += [(s, own[s], cross[s]) for s in (half - 1, half)]
+    assert lax.axis_size("z") == 8
+    own, cross = {0: block}, {0: swap(block, "xl")}
+    for s in (1, 2, 3):
+        for way in (-1, 1):
+            own[way * s] = z_step(own[way * (s - 1)], way)
+            held = cross[way * (s - 1)]
+            cross[way * s] = z_step(after(held, own[way]) if s == 1 else held, way)
+    own[4], cross[4] = z_step(own[-3], -1), z_step(cross[3], 1)
+
+    def terms(*places):
+        return [(d, own[d], cross[d]) for d in places]
+
+    own[0] = after(own[0], own[3], own[-3], cross[3], cross[-3])
+    (total,) = contract(weights, [[None, *terms(0, 1, -1, 2, -2)]], f"{name}_near")
     return contract(
         weights,
-        [[total_own, *mine]],
-        f"{name}_last",
+        [[total, *terms(3, -3, 4)]],
+        f"{name}_far",
         finish=finish,
-        extras=[both],
         outs=outs,
         smem=smem,
     )
@@ -274,13 +254,12 @@
     unit_other = swap(unit, "core")
     from_y, from_x = swap(joined, "yl"), swap(joined, "xh")
     from_yx = swap(joined, "yl", "xh")
-    w_parts = column_parts(w_out, heads)
+    parts = column_parts(w_out, heads)
 
     own, other = attend(
         doc_lengths, [(unit, None, True), (unit_other, None, False)], [(0, joined)], "attend_own"
     )
-    w_cols = lax.all_to_all(after(w_parts, own, from_y, from_x), HEAD, 0, 0)
-    w_cols = w_cols.reshape(heads * HD, HD)
+    w_cols = lax.all_to_all(after(parts, own, from_y), HEAD, 0, 0).reshape(heads * HD, HD)
     own, other = attend(
         doc_lengths,
         [(unit, own, False), (unit_other, other, False)],

time: 144 us -> 138 us (0.958)
  waiting for transfers between devices: 71.2 us -> 55.1 us
  starting transfers between devices: 41.9 us -> 52.4 us
    ppermute x39 -> x35, waiting for transfers between devices: 71.2 us -> 53.3 us  [hop(): lax.ppermute(value, axes, [(number[c], number[tuple(target(*c))]) for c i...]
    ppermute x39 -> x35, starting transfers between devices: 36.9 us -> 48.6 us  [hop(): lax.ppermute(value, axes, [(number[c], number[tuple(target(*c))]) for c i...]
    all_to_all x1, waiting for transfers between devices: 0.01 us -> 1.8 us  [per_device(): lax.all_to_all(after(parts, own, from_y), HEAD, 0, 0)]
    pallas_call x14 -> x10, Pallas kernels: 21.9 us -> 21.2 us  [call(): pl.pallas_call(kernel, out_shape=outs, in_specs=[SMEM] * smem_count + [VM...]
  transfers between devices with their start and end apart: 40 -> 36, of which waited for: 27 -> 21; matrix products, arithmetic and copies ran while one was open for 0% -> 0% of each run, Pallas kernels for 13% -> 13%
where the time goes in v5:
time: 138 us; the launch traced here: 137 us
  waiting for transfers between devices  55.1 us (40%)
  starting transfers between devices  52.4 us (38%)
  Pallas kernels  21.2 us (15%)
  local copies, waits for them, and re-layouts  8.42 us (6%)
    ppermute x35, waiting for transfers between devices, hop(): lax.ppermute(value, axes, [(number[c], number[tuple(target(*c))]) for c i...  53.3 us
    ppermute x35, starting transfers between devices, hop(): lax.ppermute(value, axes, [(number[c], number[tuple(target(*c))]) for c i...  48.6 us
    pallas_call x10, Pallas kernels, call(): pl.pallas_call(kernel, out_shape=outs, in_specs=[SMEM] * smem_count + [VM...  21.2 us
    unnamed x22, local copies, waits for them, and re-layouts  8.42 us
    all_to_all x1, starting transfers between devices, per_device(): lax.all_to_all(after(parts, own, from_y), HEAD, 0, 0)  3.85 us
  transfers between devices with their start and end apart: 36, of which 21 were waited for; matrix products, arithmetic and copies ran while one was open for 0% of the time, Pallas kernels for 13%

profile of v5, /device:TPU:16, one launch (start us, length us, event | category | flops | bytes accessed | tf_op | source)
XLA Modules:
  0.0 137.3 jit_solution(7258028684834290072)
XLA Ops:
  0.0 5.9 %collective-permute-start = (bf16[1024,128]{1,0:T(8,128)(2,1)}, bf16[1024,128]{1,0:T(8,128)(2,1)S(1)}, u32[]{:S(2)}, u32[]{:S(2)}) collective-permute-start(bf16[1024,128]{1,0:T(8,128)(2,1)} %refs_2_.1), channel_id=1, source_target_pairs={{0,7},{1,0},{2,1},{3,2},{4,3},{5,4},{6,5},{7,6},{8,15},{9,8},{10,9... | collective-permute-start | bytes 786440 | tf_op jit(solution)/shard_map/ppermute | solution.py:28
  7.4 4.4 %collective-permute-done.refs_4_ = bf16[1024,128]{1,0:T(8,128)(2,1)S(1)} collective-permute-done((bf16[1024,128]{1,0:T(8,128)(2,1)}, bf16[1024,128]{1,0:T(8,128)(2,1)S(1)}, u32[]{:S(2)}, u32[]{:S(2)}) %collective-permute-start) | collective-permute-done | bytes 262176 | tf_op jit(solution)/shard_map/ppermute | solution.py:28
  16.3 4.4 %collective-permute-done.7.refs_5_ = bf16[1024,128]{1,0:T(8,128)(2,1)S(1)} collective-permute-done((bf16[1024,128]{1,0:T(8,128)(2,1)S(1)}, bf16[1024,128]{1,0:T(8,128)(2,1)S(1)}, u32[]{:S(2)}, u32[]{:S(2)}) %collective-permute-start.7) | collective-permute-done | bytes 262176 | tf_op jit(solution)/shard_map/ppermute | solution.py:28
  20.7 3.0 %collective-permute-start.8 = (bf16[1024,128]{1,0:T(8,128)(2,1)S(1)}, bf16[1024,128]{1,0:T(8,128)(2,1)S(1)}, u32[]{:S(2)}, u32[]{:S(2)}) collective-permute-start(bf16[1024,128]{1,0:T(8,128)(2,1)S(1)} %collective-permute-done.7.refs_5_), channel_id=1, source_target_pairs={{0,7},{1,0},{2,1},{3,2},{4,3},{5,4},{6,5},{7,6},{8,15},{9,8},{10,9... | collective-permute-start | bytes 786440 | tf_op jit(solution)/shard_map/ppermute | solution.py:28
  23.7 3.0 %collective-permute-done.10.refs_7_ = bf16[1024,128]{1,0:T(8,128)(2,1)S(1)} collective-permute-done((bf16[1024,128]{1,0:T(8,128)(2,1)S(1)}, bf16[1024,128]{1,0:T(8,128)(2,1)S(1)}, u32[]{:S(2)}, u32[]{:S(2)}) %collective-permute-start.10) | collective-permute-done | bytes 262176 | tf_op jit(solution)/shard_map/ppermute | solution.py:28
  26.7 5.6 %collective-permute-done.4.refs_10_ = bf16[1024,128]{1,0:T(8,128)(2,1)S(1)} collective-permute-done((bf16[1024,128]{1,0:T(8,128)(2,1)S(1)}, bf16[1024,128]{1,0:T(8,128)(2,1)S(1)}, u32[]{:S(2)}, u32[]{:S(2)}) %collective-permute-start.4) | collective-permute-done | bytes 262176 | tf_op jit(solution)/shard_map/ppermute | solution.py:28
  32.3 3.2 %collective-permute-start.9 = (bf16[1024,128]{1,0:T(8,128)(2,1)S(1)}, bf16[1024,128]{1,0:T(8,128)(2,1)S(1)}, u32[]{:S(2)}, u32[]{:S(2)}) collective-permute-start(bf16[1024,128]{1,0:T(8,128)(2,1)S(1)} %collective-permute-done.8.refs_9_), channel_id=1, source_target_pairs={{0,7},{1,0},{2,1},{3,2},{4,3},{5,4},{6,5},{7,6},{8,15},{9,8},{10,9... | collective-permute-start | bytes 786440 | tf_op jit(solution)/shard_map/ppermute | solution.py:28
  36.0 3.7 %collective-permute-start.2 = (bf16[1024,128]{1,0:T(8,128)(2,1)S(1)}, bf16[1024,128]{1,0:T(8,128)(2,1)S(1)}, u32[]{:S(2)}, u32[]{:S(2)}) collective-permute-start(bf16[1024,128]{1,0:T(8,128)(2,1)S(1)} %collective-permute-done.1.refs_8_), channel_id=1, source_target_pairs={{0,7},{1,0},{2,1},{3,2},{4,3},{5,4},{6,5},{7,6},{8,15},{9,8},{10,9... | collective-permute-start | bytes 786440 | tf_op jit(solution)/shard_map/ppermute | solution.py:28
  39.7 3.9 %collective-permute-done.5.refs_6_ = bf16[1024,128]{1,0:T(8,128)(2,1)S(1)} collective-permute-done((bf16[1024,128]{1,0:T(8,128)(2,1)S(1)}, bf16[1024,128]{1,0:T(8,128)(2,1)S(1)}, u32[]{:S(2)}, u32[]{:S(2)}) %collective-permute-start.5) | collective-permute-done | bytes 262176 | tf_op jit(solution)/shard_map/ppermute | solution.py:28
  43.6 3.2 %collective-permute-start.14 = (bf16[1024,128]{1,0:T(8,128)(2,1)S(1)}, bf16[1024,128]{1,0:T(8,128)(2,1)S(1)}, u32[]{:S(2)}, u32[]{:S(2)}) collective-permute-start(bf16[1024,128]{1,0:T(8,128)(2,1)S(1)} %collective-permute-done.9.refs_5_), channel_id=1, source_target_pairs={{0,7},{1,0},{2,1},{3,2},{4,3},{5,4},{6,5},{7,6},{8,15},{9,8},{10,9... | collective-permute-start | bytes 786440 | tf_op jit(solution)/shard_map/ppermute | solution.py:28
  55.8 2.7 %collective-permute-start.18 = (bf16[1024,256]{1,0:T(8,128)(2,1)S(1)}, bf16[1024,256]{1,0:T(8,128)(2,1)S(1)}, u32[]{:S(2)}, u32[]{:S(2)}) collective-permute-start(bf16[1024,256]{1,0:T(8,128)(2,1)S(1)} %get-tuple-element.22.refs_1_), channel_id=1, source_target_pairs={{0,32},{32,0},{1,33},{33,1},{2,34},{34,2},{3,35},{35,3},{4,36},{36... | collective-permute-start | bytes 1572872 | tf_op jit(solution)/shard_map/ppermute | solution.py:28
  60.4 4.9 %attend_own.1 = (f32[1024,256]{1,0:T(8,128)S(1)}, f32[1024,256]{1,0:T(8,128)S(1)}) custom-call(s32[2]{0:T(128)S(1)} %copy-done.4, bf16[1024,256]{1,0:T(8,128)(2,1)S(1)} %get-tuple-element.22.refs_1_, bf16[1024,128]{1,0:T(8,128)(2,1)S(1)} %get-tuple-element.23.refs_2_.refs_3_, bf16[1024,128]{1,0:T(8,128)(2,1)S(1)} %collective-permute-done.15.refs_3_.refs_5_.refs_2_), custom_call_target="tpu_custom_call" | custom-call | flops 2147483648 | bytes 3145736 | tf_op jit(solution)/shard_map/attend_own/pallas_call | solution.py:46
  67.4 3.8 %all-to-all-start = ((bf16[16,128,128]{2,1,0:T(8,128)(2,1)}), bf16[16,128,128]{2,1,0:T(8,128)(2,1)S(1)}, u32[]{:S(2)}, u32[]{:S(2)}) async-start(bf16[16,128,128]{2,1,0:T(8,128)(2,1)} %column_parts.1), calls=%async_computation | async-start | bytes 1048576 | tf_op jit(solution)/shard_map/all_to_all | solution.py:262
  73.7 6.0 %attend_near.1 = (f32[1024,256]{1,0:T(8,128)S(1)}, f32[1024,256]{1,0:T(8,128)S(1)}) custom-call(s32[2]{0:T(128)S(1)} %copy-done.4, bf16[1024,256]{1,0:T(8,128)(2,1)S(1)} %collective-permute-done.16.refs_1_, bf16[1024,256]{1,0:T(8,128)(2,1)S(1)} %collective-permute-done.18.refs_2_, bf16[1024,128]{1,0:T(8,128)(2,1)S(1)} %get-tuple-element.23.refs_2_.refs_3_, ...), custom_call_target="tpu_custom_call" | custom-call | flops 4294967296 | bytes 5767176 | tf_op jit(solution)/shard_map/attend_near/pallas_call | solution.py:46
  88.9 2.6 %collective-permute-start.20 = (bf16[1024,128]{1,0:T(8,128)(2,1)S(1)}, bf16[1024,128]{1,0:T(8,128)(2,1)S(1)}, u32[]{:S(2)}, u32[]{:S(2)}) collective-permute-start(bf16[1024,128]{1,0:T(8,128)(2,1)S(1)} %combine.1.refs_1_), channel_id=1, source_target_pairs={{0,7},{1,0},{2,1},{3,2},{4,3},{5,4},{6,5},{7,6},{8,15},{9,8},{10,9... | collective-permute-start | bytes 786440 | tf_op jit(solution)/shard_map/ppermute | solution.py:28
  91.5 3.5 %collective-permute-done.26.refs_2_ = bf16[1024,128]{1,0:T(8,128)(2,1)S(1)} collective-permute-done((bf16[1024,128]{1,0:T(8,128)(2,1)S(1)}, bf16[1024,128]{1,0:T(8,128)(2,1)S(1)}, u32[]{:S(2)}, u32[]{:S(2)}) %collective-permute-start.26) | collective-permute-done | bytes 262176 | tf_op jit(solution)/shard_map/ppermute | solution.py:28
  96.6 3.7 %collective-permute-start.27 = (bf16[1024,128]{1,0:T(8,128)(2,1)S(1)}, bf16[1024,128]{1,0:T(8,128)(2,1)S(1)}, u32[]{:S(2)}, u32[]{:S(2)}) collective-permute-start(bf16[1024,128]{1,0:T(8,128)(2,1)S(1)} %collective-permute-done.26.refs_2_), channel_id=1, source_target_pairs={{0,7},{1,0},{2,1},{3,2},{4,3},{5,4},{6,5},{7,6},{8,15},{9,8},{10,9... | collective-permute-start | bytes 786440 | tf_op jit(solution)/shard_map/ppermute | solution.py:28
  100.3 4.2 %collective-permute-done.27.refs_4_ = bf16[1024,128]{1,0:T(8,128)(2,1)S(1)} collective-permute-done((bf16[1024,128]{1,0:T(8,128)(2,1)S(1)}, bf16[1024,128]{1,0:T(8,128)(2,1)S(1)}, u32[]{:S(2)}, u32[]{:S(2)}) %collective-permute-start.27) | collective-permute-done | bytes 262176 | tf_op jit(solution)/shard_map/ppermute | solution.py:28
  104.5 3.7 %collective-permute-start.28 = (bf16[1024,128]{1,0:T(8,128)(2,1)S(1)}, bf16[1024,128]{1,0:T(8,128)(2,1)S(1)}, u32[]{:S(2)}, u32[]{:S(2)}) collective-permute-start(bf16[1024,128]{1,0:T(8,128)(2,1)S(1)} %collective-permute-done.27.refs_4_), channel_id=1, source_target_pairs={{0,7},{1,0},{2,1},{3,2},{4,3},{5,4},{6,5},{7,6},{8,15},{9,8},{10,9... | collective-permute-start | bytes 786440 | tf_op jit(solution)/shard_map/ppermute | solution.py:28
  110.8 5.6 %collective-permute-done.24.refs_9_ = bf16[1024,128]{1,0:T(8,128)(2,1)S(1)} collective-permute-done((bf16[1024,128]{1,0:T(8,128)(2,1)S(1)}, bf16[1024,128]{1,0:T(8,128)(2,1)S(1)}, u32[]{:S(2)}, u32[]{:S(2)}) %collective-permute-start.24) | collective-permute-done | bytes 262176 | tf_op jit(solution)/shard_map/ppermute | solution.py:28
  116.4 3.2 %collective-permute-start.29 = (bf16[1024,128]{1,0:T(8,128)(2,1)S(1)}, bf16[1024,128]{1,0:T(8,128)(2,1)S(1)}, u32[]{:S(2)}, u32[]{:S(2)}) collective-permute-start(bf16[1024,128]{1,0:T(8,128)(2,1)S(1)} %collective-permute-done.28.refs_8_), channel_id=1, source_target_pairs={{0,7},{1,0},{2,1},{3,2},{4,3},{5,4},{6,5},{7,6},{8,15},{9,8},{10,9... | collective-permute-start | bytes 786440 | tf_op jit(solution)/shard_map/ppermute | solution.py:28
  120.2 3.7 %collective-permute-start.22 = (bf16[1024,128]{1,0:T(8,128)(2,1)S(1)}, bf16[1024,128]{1,0:T(8,128)(2,1)S(1)}, u32[]{:S(2)}, u32[]{:S(2)}) collective-permute-start(bf16[1024,128]{1,0:T(8,128)(2,1)S(1)} %collective-permute-done.21.refs_7_), channel_id=1, source_target_pairs={{0,7},{1,0},{2,1},{3,2},{4,3},{5,4},{6,5},{7,6},{8,15},{9,8},{10,9... | collective-permute-start | bytes 786440 | tf_op jit(solution)/shard_map/ppermute | solution.py:28
  123.9 3.7 %collective-permute-done.25.refs_4_ = bf16[1024,128]{1,0:T(8,128)(2,1)S(1)} collective-permute-done((bf16[1024,128]{1,0:T(8,128)(2,1)S(1)}, bf16[1024,128]{1,0:T(8,128)(2,1)S(1)}, u32[]{:S(2)}, u32[]{:S(2)}) %collective-permute-start.25) | collective-permute-done | bytes 262176 | tf_op jit(solution)/shard_map/ppermute | solution.py:28
  127.6 3.2 %collective-permute-start.34 = (bf16[1024,128]{1,0:T(8,128)(2,1)S(1)}, bf16[1024,128]{1,0:T(8,128)(2,1)S(1)}, u32[]{:S(2)}, u32[]{:S(2)}) collective-permute-start(bf16[1024,128]{1,0:T(8,128)(2,1)S(1)} %collective-permute-done.29.refs_3_), channel_id=1, source_target_pairs={{0,7},{1,0},{2,1},{3,2},{4,3},{5,4},{6,5},{7,6},{8,15},{9,8},{10,9... | collective-permute-start | bytes 786440 | tf_op jit(solution)/shard_map/ppermute | solution.py:28
  (80 shorter events, 42.2 us)
Async XLA Ops:
  0.0 11.7 %collective-permute-start = (bf16[1024,128]{1,0:T(8,128)(2,1)}, bf16[1024,128]{1,0:T(8,128)(2,1)S(1)}, u32[]{:S(2)}, u32[]{:S(2)}) collective-permute-start(bf16[1024,128]{1,0:T(8,128)(2,1)} %refs_2_.1), channel_id=1, source_target_pairs={{0,7},{1,0},{2,1},{3,2},{4,3},{5,4},{6,5},{7,6},{8,15},{9,8},{10,9... | collective-permute-start | bytes 786440 | tf_op jit(solution)/shard_map/ppermute | solution.py:28
  16.3 10.5 %collective-permute-start.10 = (bf16[1024,128]{1,0:T(8,128)(2,1)S(1)}, bf16[1024,128]{1,0:T(8,128)(2,1)S(1)}, u32[]{:S(2)}, u32[]{:S(2)}) collective-permute-start(bf16[1024,128]{1,0:T(8,128)(2,1)S(1)} %collective-permute-done.6.refs_3_), channel_id=1, source_target_pairs={{0,1},{1,2},{2,3},{3,4},{4,5},{5,6},{6,7},{7,0},{8,9},{9,10},{10,1... | collective-permute-start | bytes 786440 | tf_op jit(solution)/shard_map/ppermute | solution.py:28
  16.3 16.1 %collective-permute-start.4 = (bf16[1024,128]{1,0:T(8,128)(2,1)S(1)}, bf16[1024,128]{1,0:T(8,128)(2,1)S(1)}, u32[]{:S(2)}, u32[]{:S(2)}) collective-permute-start(bf16[1024,128]{1,0:T(8,128)(2,1)S(1)} %collective-permute-done.3.refs_6_), channel_id=1, source_target_pairs={{0,1},{1,2},{2,3},{3,4},{4,5},{5,6},{6,7},{7,0},{8,9},{9,10},{10,1... | collective-permute-start | bytes 786440 | tf_op jit(solution)/shard_map/ppermute | solution.py:28
  20.7 11.6 %collective-permute-start.8 = (bf16[1024,128]{1,0:T(8,128)(2,1)S(1)}, bf16[1024,128]{1,0:T(8,128)(2,1)S(1)}, u32[]{:S(2)}, u32[]{:S(2)}) collective-permute-start(bf16[1024,128]{1,0:T(8,128)(2,1)S(1)} %collective-permute-done.7.refs_5_), channel_id=1, source_target_pairs={{0,7},{1,0},{2,1},{3,2},{4,3},{5,4},{6,5},{7,6},{8,15},{9,8},{10,9... | collective-permute-start | bytes 786440 | tf_op jit(solution)/shard_map/ppermute | solution.py:28
  23.7 12.3 %collective-permute-start.1 = (bf16[1024,128]{1,0:T(8,128)(2,1)S(1)}, bf16[1024,128]{1,0:T(8,128)(2,1)S(1)}, u32[]{:S(2)}, u32[]{:S(2)}) collective-permute-start(bf16[1024,128]{1,0:T(8,128)(2,1)S(1)} %collective-permute-done.refs_4_), channel_id=1, source_target_pairs={{0,7},{1,0},{2,1},{3,2},{4,3},{5,4},{6,5},{7,6},{8,15},{9,8},{10,9... | collective-permute-start | bytes 786440 | tf_op jit(solution)/shard_map/ppermute | solution.py:28
  26.7 13.0 %collective-permute-start.11 = (bf16[1024,128]{1,0:T(8,128)(2,1)S(1)}, bf16[1024,128]{1,0:T(8,128)(2,1)S(1)}, u32[]{:S(2)}, u32[]{:S(2)}) collective-permute-start(bf16[1024,128]{1,0:T(8,128)(2,1)S(1)} %collective-permute-done.10.refs_7_), channel_id=1, source_target_pairs={{0,1},{1,2},{2,3},{3,4},{4,5},{5,6},{6,7},{7,0},{8,9},{9,10},{10,1... | collective-permute-start | bytes 786440 | tf_op jit(solution)/shard_map/ppermute | solution.py:28
  32.3 11.2 %collective-permute-start.5 = (bf16[1024,128]{1,0:T(8,128)(2,1)S(1)}, bf16[1024,128]{1,0:T(8,128)(2,1)S(1)}, u32[]{:S(2)}, u32[]{:S(2)}) collective-permute-start(bf16[1024,128]{1,0:T(8,128)(2,1)S(1)} %collective-permute-done.4.refs_10_), channel_id=1, source_target_pairs={{0,1},{1,2},{2,3},{3,4},{4,5},{5,6},{6,7},{7,0},{8,9},{9,10},{10,1... | collective-permute-start | bytes 786440 | tf_op jit(solution)/shard_map/ppermute | solution.py:28
  32.3 11.2 %collective-permute-start.9 = (bf16[1024,128]{1,0:T(8,128)(2,1)S(1)}, bf16[1024,128]{1,0:T(8,128)(2,1)S(1)}, u32[]{:S(2)}, u32[]{:S(2)}) collective-permute-start(bf16[1024,128]{1,0:T(8,128)(2,1)S(1)} %collective-permute-done.8.refs_9_), channel_id=1, source_target_pairs={{0,7},{1,0},{2,1},{3,2},{4,3},{5,4},{6,5},{7,6},{8,15},{9,8},{10,9... | collective-permute-start | bytes 786440 | tf_op jit(solution)/shard_map/ppermute | solution.py:28
  36.0 11.2 %collective-permute-start.2 = (bf16[1024,128]{1,0:T(8,128)(2,1)S(1)}, bf16[1024,128]{1,0:T(8,128)(2,1)S(1)}, u32[]{:S(2)}, u32[]{:S(2)}) collective-permute-start(bf16[1024,128]{1,0:T(8,128)(2,1)S(1)} %collective-permute-done.1.refs_8_), channel_id=1, source_target_pairs={{0,7},{1,0},{2,1},{3,2},{4,3},{5,4},{6,5},{7,6},{8,15},{9,8},{10,9... | collective-permute-start | bytes 786440 | tf_op jit(solution)/shard_map/ppermute | solution.py:28
  39.7 9.6 %collective-permute-start.12 = (bf16[1024,128]{1,0:T(8,128)(2,1)S(1)}, bf16[1024,128]{1,0:T(8,128)(2,1)S(1)}, u32[]{:S(2)}, u32[]{:S(2)}) collective-permute-start(bf16[1024,128]{1,0:T(8,128)(2,1)S(1)} %collective-permute-done.11.refs_11_), channel_id=1, source_target_pairs={{0,1},{1,2},{2,3},{3,4},{4,5},{5,6},{6,7},{7,0},{8,9},{9,10},{10,1... | collective-permute-start | bytes 786440 | tf_op jit(solution)/shard_map/ppermute | solution.py:28
  43.6 9.6 %collective-permute-start.13 = (bf16[1024,128]{1,0:T(8,128)(2,1)S(1)}, bf16[1024,128]{1,0:T(8,128)(2,1)S(1)}, u32[]{:S(2)}, u32[]{:S(2)}) collective-permute-start(bf16[1024,128]{1,0:T(8,128)(2,1)S(1)} %collective-permute-done.5.refs_6_), channel_id=1, source_target_pairs={{0,1},{1,2},{2,3},{3,4},{4,5},{5,6},{6,7},{7,0},{8,9},{9,10},{10,1... | collective-permute-start | bytes 786440 | tf_op jit(solution)/shard_map/ppermute | solution.py:28
  43.6 9.6 %collective-permute-start.14 = (bf16[1024,128]{1,0:T(8,128)(2,1)S(1)}, bf16[1024,128]{1,0:T(8,128)(2,1)S(1)}, u32[]{:S(2)}, u32[]{:S(2)}) collective-permute-start(bf16[1024,128]{1,0:T(8,128)(2,1)S(1)} %collective-permute-done.9.refs_5_), channel_id=1, source_target_pairs={{0,7},{1,0},{2,1},{3,2},{4,3},{5,4},{6,5},{7,6},{8,15},{9,8},{10,9... | collective-permute-start | bytes 786440 | tf_op jit(solution)/shard_map/ppermute | solution.py:28
  54.5 12.9 %collective-permute-start.16 = (bf16[1024,256]{1,0:T(8,128)(2,1)S(1)}, bf16[1024,256]{1,0:T(8,128)(2,1)S(1)}, u32[]{:S(2)}, u32[]{:S(2)}) collective-permute-start(bf16[1024,256]{1,0:T(8,128)(2,1)S(1)} %get-tuple-element.22.refs_1_), channel_id=1, source_target_pairs={{0,64},{64,0},{1,65},{65,1},{2,66},{66,2},{3,67},{67,3},{4,68},{68... | collective-permute-start | bytes 1572872 | tf_op jit(solution)/shard_map/ppermute | solution.py:28
  55.8 15.4 %collective-permute-start.18 = (bf16[1024,256]{1,0:T(8,128)(2,1)S(1)}, bf16[1024,256]{1,0:T(8,128)(2,1)S(1)}, u32[]{:S(2)}, u32[]{:S(2)}) collective-permute-start(bf16[1024,256]{1,0:T(8,128)(2,1)S(1)} %get-tuple-element.22.refs_1_), channel_id=1, source_target_pairs={{0,32},{32,0},{1,33},{33,1},{2,34},{34,2},{3,35},{35,3},{4,36},{36... | collective-permute-start | bytes 1572872 | tf_op jit(solution)/shard_map/ppermute | solution.py:28
  59.5 20.3 %collective-permute-start.17 = (bf16[1024,256]{1,0:T(8,128)(2,1)S(1)}, bf16[1024,256]{1,0:T(8,128)(2,1)S(1)}, u32[]{:S(2)}, u32[]{:S(2)}) collective-permute-start(bf16[1024,256]{1,0:T(8,128)(2,1)S(1)} %get-tuple-element.22.refs_1_), channel_id=1, source_target_pairs={{0,96},{32,64},{64,32},{96,0},{1,97},{33,65},{65,33},{97,1},{2,98}... | collective-permute-start | bytes 1572872 | tf_op jit(solution)/shard_map/ppermute | solution.py:28
  67.4 19.7 %all-to-all-start = ((bf16[16,128,128]{2,1,0:T(8,128)(2,1)}), bf16[16,128,128]{2,1,0:T(8,128)(2,1)S(1)}, u32[]{:S(2)}, u32[]{:S(2)}) async-start(bf16[16,128,128]{2,1,0:T(8,128)(2,1)} %column_parts.1), calls=%async_computation | async-start | bytes 1048576 | tf_op jit(solution)/shard_map/all_to_all | solution.py:262
  100.3 10.5 %collective-permute-start.30 = (bf16[1024,128]{1,0:T(8,128)(2,1)S(1)}, bf16[1024,128]{1,0:T(8,128)(2,1)S(1)}, u32[]{:S(2)}, u32[]{:S(2)}) collective-permute-start(bf16[1024,128]{1,0:T(8,128)(2,1)S(1)} %collective-permute-done.26.refs_2_), channel_id=1, source_target_pairs={{0,1},{1,2},{2,3},{3,4},{4,5},{5,6},{6,7},{7,0},{8,9},{9,10},{10,1... | collective-permute-start | bytes 786440 | tf_op jit(solution)/shard_map/ppermute | solution.py:28
  100.3 16.1 %collective-permute-start.24 = (bf16[1024,128]{1,0:T(8,128)(2,1)S(1)}, bf16[1024,128]{1,0:T(8,128)(2,1)S(1)}, u32[]{:S(2)}, u32[]{:S(2)}) collective-permute-start(bf16[1024,128]{1,0:T(8,128)(2,1)S(1)} %collective-permute-done.23.refs_5_), channel_id=1, source_target_pairs={{0,1},{1,2},{2,3},{3,4},{4,5},{5,6},{6,7},{7,0},{8,9},{9,10},{10,1... | collective-permute-start | bytes 786440 | tf_op jit(solution)/shard_map/ppermute | solution.py:28
  104.5 11.9 %collective-permute-start.28 = (bf16[1024,128]{1,0:T(8,128)(2,1)S(1)}, bf16[1024,128]{1,0:T(8,128)(2,1)S(1)}, u32[]{:S(2)}, u32[]{:S(2)}) collective-permute-start(bf16[1024,128]{1,0:T(8,128)(2,1)S(1)} %collective-permute-done.27.refs_4_), channel_id=1, source_target_pairs={{0,7},{1,0},{2,1},{3,2},{4,3},{5,4},{6,5},{7,6},{8,15},{9,8},{10,9... | collective-permute-start | bytes 786440 | tf_op jit(solution)/shard_map/ppermute | solution.py:28
  108.2 12.0 %collective-permute-start.21 = (bf16[1024,128]{1,0:T(8,128)(2,1)S(1)}, bf16[1024,128]{1,0:T(8,128)(2,1)S(1)}, u32[]{:S(2)}, u32[]{:S(2)}) collective-permute-start(bf16[1024,128]{1,0:T(8,128)(2,1)S(1)} %collective-permute-done.20.refs_3_), channel_id=1, source_target_pairs={{0,7},{1,0},{2,1},{3,2},{4,3},{5,4},{6,5},{7,6},{8,15},{9,8},{10,9... | collective-permute-start | bytes 786440 | tf_op jit(solution)/shard_map/ppermute | solution.py:28
  110.8 13.1 %collective-permute-start.31 = (bf16[1024,128]{1,0:T(8,128)(2,1)S(1)}, bf16[1024,128]{1,0:T(8,128)(2,1)S(1)}, u32[]{:S(2)}, u32[]{:S(2)}) collective-permute-start(bf16[1024,128]{1,0:T(8,128)(2,1)S(1)} %collective-permute-done.30.refs_6_), channel_id=1, source_target_pairs={{0,1},{1,2},{2,3},{3,4},{4,5},{5,6},{6,7},{7,0},{8,9},{9,10},{10,1... | collective-permute-start | bytes 786440 | tf_op jit(solution)/shard_map/ppermute | solution.py:28
  116.4 11.2 %collective-permute-start.25 = (bf16[1024,128]{1,0:T(8,128)(2,1)S(1)}, bf16[1024,128]{1,0:T(8,128)(2,1)S(1)}, u32[]{:S(2)}, u32[]{:S(2)}) collective-permute-start(bf16[1024,128]{1,0:T(8,128)(2,1)S(1)} %collective-permute-done.24.refs_9_), channel_id=1, source_target_pairs={{0,1},{1,2},{2,3},{3,4},{4,5},{5,6},{6,7},{7,0},{8,9},{9,10},{10,1... | collective-permute-start | bytes 786440 | tf_op jit(solution)/shard_map/ppermute | solution.py:28
  116.4 11.2 %collective-permute-start.29 = (bf16[1024,128]{1,0:T(8,128)(2,1)S(1)}, bf16[1024,128]{1,0:T(8,128)(2,1)S(1)}, u32[]{:S(2)}, u32[]{:S(2)}) collective-permute-start(bf16[1024,128]{1,0:T(8,128)(2,1)S(1)} %collective-permute-done.28.refs_8_), channel_id=1, source_target_pairs={{0,7},{1,0},{2,1},{3,2},{4,3},{5,4},{6,5},{7,6},{8,15},{9,8},{10,9... | collective-permute-start | bytes 786440 | tf_op jit(solution)/shard_map/ppermute | solution.py:28
  120.2 10.9 %collective-permute-start.22 = (bf16[1024,128]{1,0:T(8,128)(2,1)S(1)}, bf16[1024,128]{1,0:T(8,128)(2,1)S(1)}, u32[]{:S(2)}, u32[]{:S(2)}) collective-permute-start(bf16[1024,128]{1,0:T(8,128)(2,1)S(1)} %collective-permute-done.21.refs_7_), channel_id=1, source_target_pairs={{0,7},{1,0},{2,1},{3,2},{4,3},{5,4},{6,5},{7,6},{8,15},{9,8},{10,9... | collective-permute-start | bytes 786440 | tf_op jit(solution)/shard_map/ppermute | solution.py:28
  (23 other events, 112.9 us)
